TPU v7x, 256 devices: a whole 4x4x8 slice. The times are simulated.
256 devices in a mesh: dp: 32 (over z_hi, x, y), frame: 8 (over z_lo, core).
Axes of the slice: x: 4, y: 4, z: 8 (z_hi: 2, z_lo: 4; z = z_hi * 4 + z_lo), core: 2. Of those that a mesh axis runs over, the one named last changes fastest.
Arguments:
- clip_tokens: bfloat16 [32, 32, 64, 1024], P('dp', 'frame'), may hold values from -8 to 8
- out_grad: bfloat16 [32, 32, 64, 1024], P('dp', 'frame'), may hold values from -6 to 6
- ln_gain: float32 [1024], replicated, may hold values from 0.4 to 1.6
- w_project: bfloat16 [1024, 3072], replicated, may hold values from -2 to 2
- w_expand: bfloat16 [1024, 8192], P(None, 'frame'), may hold values from -0.1875 to 0.1875
Outputs:
- token_grad: bfloat16 [32, 32, 64, 1024], P('dp', 'frame')
- project_grad: float32 [1024, 3072], P('dp', 'frame')
- expand_grad: float32 [1024, 8192], P('dp', 'frame')
- gain_grad: float32 [1024], replicated
All inputs are finite; a program needn't handle non-finite values.
Results may differ from a plain program's by a relative error of at most 0.015.
The roundings to bfloat16 on the way count: a program that leaves them out, or rounds other values in their place, can miss the bound.
Values may be sent and summed in bfloat16 or wider, within the bound.
No kernel may reach another device: no remote copies, remote signals or barrier semaphores. Data moves between devices by JAX's collectives and lax.ppermute only.
A program may use at most 128 MiB of HBM per device.

v0:
```python
import jax
import jax.numpy as jnp
from jax import lax
from jax.sharding import PartitionSpec as P

HEADS = 16


EPSILON = 1e-05


def standardize(inputs):
    center = inputs - jnp.mean(inputs, axis=-1, keepdims=True)
    spread = lax.rsqrt(jnp.mean(center * center, axis=-1, keepdims=True) + EPSILON)
    return (center * spread, spread)


def attend(patch_proj, head_count, score_scale):
    frames_all, patch_local, three_width = patch_proj.shape
    model_width = three_width // 3
    head_size = model_width // head_count
    split_proj = patch_proj.reshape(frames_all, patch_local, 3, head_count, head_size)
    queries = split_proj[:, :, 0]
    key_rows = split_proj[:, :, 1]
    value_rows = split_proj[:, :, 2]
    scores = (
        jnp.einsum("fphd,gphd->phfg", queries, key_rows, preferred_element_type=jnp.float32)
        * score_scale
    )
    attention = jax.nn.softmax(scores, axis=-1)
    rounded = attention.astype(jnp.bfloat16)
    attended = jnp.einsum(
        "phfg,gphd->fphd", rounded, value_rows, preferred_element_type=jnp.float32
    ).astype(jnp.bfloat16)
    return (
        queries,
        key_rows,
        value_rows,
        attention,
        rounded,
        attended.reshape(frames_all, patch_local, model_width),
    )


def attend_back(queries, key_rows, value_rows, attention, rounded, attended_grad, score_scale):
    frames_all, patch_local, head_count, head_size = queries.shape
    prob_grad = jnp.einsum(
        "fphd,gphd->phfg", attended_grad, value_rows, preferred_element_type=jnp.float32
    )
    centered_prob = prob_grad - jnp.sum(attention * prob_grad, axis=-1, keepdims=True)
    score_grad = (attention * centered_prob * score_scale).astype(jnp.bfloat16)
    query_grad = jnp.einsum(
        "phfg,gphd->fphd", score_grad, key_rows, preferred_element_type=jnp.float32
    )
    key_grad = jnp.einsum(
        "phfg,fphd->gphd", score_grad, queries, preferred_element_type=jnp.float32
    )
    value_grad = jnp.einsum(
        "phfg,fphd->gphd", rounded, attended_grad, preferred_element_type=jnp.float32
    )
    stacked = jnp.stack([query_grad, key_grad, value_grad], axis=2).astype(jnp.bfloat16)
    return stacked.reshape(frames_all, patch_local, 3 * head_count * head_size)


def per_device(clip_tokens, out_grad, ln_gain, w_project, w_expand):
    frame_count = lax.axis_size("frame")
    clip_count = lax.axis_size("dp")
    frames_dev = clip_tokens.shape[1]
    patches = clip_tokens.shape[2]
    model_width = clip_tokens.shape[3]
    head_size = model_width // HEADS
    score_scale = head_size ** (-0.5)
    tokens_clip = frames_dev * frame_count * patches
    inputs = clip_tokens[0].astype(jnp.float32)
    standard, spread = standardize(inputs)
    normed = (standard * ln_gain).astype(jnp.bfloat16)
    incoming = out_grad[0]
    projected = jnp.dot(
        normed.reshape(-1, model_width), w_project, preferred_element_type=jnp.float32
    ).astype(jnp.bfloat16)
    projected = projected.reshape(frames_dev, patches, 3 * model_width)
    patch_proj, incoming_moved = (
        lax.all_to_all(projected, "frame", split_axis=1, concat_axis=0, tiled=True),
        lax.all_to_all(incoming, "frame", split_axis=1, concat_axis=0, tiled=True),
    )
    queries, key_rows, value_rows, attention, rounded, attended = attend(
        patch_proj, HEADS, score_scale
    )
    partial_value = jnp.sum(inputs, axis=(0, 1)) + jnp.sum(
        attended.astype(jnp.float32), axis=(0, 1)
    )
    pooled = lax.psum(partial_value, "frame") / tokens_clip
    pooled_b = pooled.astype(jnp.bfloat16)
    embedding = jnp.dot(pooled_b[None, :], w_expand, preferred_element_type=jnp.float32)
    columns = w_expand.shape[1]
    clip_denom = clip_count - 1
    coefficient = 100.0 * tokens_clip / (columns * frame_count * clip_denom)
    own_index = lax.axis_index("dp")
    gathered = lax.all_gather(embedding, "dp", axis=0, tiled=True)
    own_cols = gathered - jnp.mean(gathered, axis=0, keepdims=True)
    gram_matrix = lax.psum(jnp.dot(own_cols, own_cols.T, precision=lax.Precision.HIGHEST), "frame")
    variances = jnp.sum(own_cols * own_cols, axis=0) / clip_denom
    gram_row = lax.dynamic_slice_in_dim(gram_matrix, own_index, 1, 0)
    own_row = lax.dynamic_slice_in_dim(own_cols, own_index, 1, 0)
    embed_grad = coefficient * (
        jnp.dot(gram_row, own_cols, precision=lax.Precision.HIGHEST) / clip_denom
        - own_row * variances
    )
    embed_grad_b = embed_grad.astype(jnp.bfloat16)
    block_rows = model_width // clip_count
    pooled_all, grad_all = (
        lax.all_gather(pooled_b[None, :], "dp", axis=0, tiled=True),
        lax.all_gather(embed_grad_b, "dp", axis=0, tiled=True),
    )
    row_part = lax.dynamic_slice_in_dim(pooled_all, own_index * block_rows, block_rows, 1)
    expand_grad = jnp.dot(row_part.T, grad_all, preferred_element_type=jnp.float32)
    pool_part = jnp.einsum("ne,de->nd", embed_grad_b, w_expand, preferred_element_type=jnp.float32)[
        0
    ]
    pool_grad = lax.psum(pool_part, "frame")
    share_grad = pool_grad / tokens_clip
    attended_grad = (incoming_moved.astype(jnp.float32) + share_grad).astype(jnp.bfloat16)
    attended_grad = attended_grad.reshape(queries.shape)
    projected_grad = attend_back(
        queries, key_rows, value_rows, attention, rounded, attended_grad, score_scale
    )
    returned = lax.all_to_all(projected_grad, "frame", split_axis=0, concat_axis=1, tiled=True)
    flat_grad = returned.reshape(-1, 3 * model_width)
    flat_normed = normed.reshape(-1, model_width)
    normed_grad = jnp.einsum("te,de->td", flat_grad, w_project, preferred_element_type=jnp.float32)
    normed_grad = normed_grad.reshape(frames_dev, patches, model_width)
    rows_sum = lax.psum_scatter(
        jnp.einsum("td,te->de", flat_normed, flat_grad, preferred_element_type=jnp.float32).astype(
            jnp.bfloat16
        ),
        "dp",
        scatter_dimension=0,
        tiled=True,
    )
    project_grad = lax.psum_scatter(rows_sum, "frame", scatter_dimension=1, tiled=True).astype(
        jnp.float32
    )
    gain_grad = lax.psum(jnp.sum(normed_grad * standard, axis=(0, 1)), ("dp", "frame"))
    total_grad = incoming.astype(jnp.float32) + share_grad
    scaled = normed_grad * ln_gain
    centered_grad = (
        scaled
        - jnp.mean(scaled, axis=-1, keepdims=True)
        - standard * jnp.mean(scaled * standard, axis=-1, keepdims=True)
    )
    token_grad = (total_grad + spread * centered_grad).astype(jnp.bfloat16)[None]
    return (token_grad, project_grad, expand_grad, gain_grad)


def solution(mesh):
    return jax.shard_map(
        per_device,
        mesh=mesh,
        in_specs=(
            P("dp", "frame", None, None),
            P("dp", "frame", None, None),
            P(),
            P(),
            P(None, "frame"),
        ),
        out_specs=(P("dp", "frame", None, None), P("dp", "frame"), P("dp", "frame"), P()),
        check_vma=False,
    )
```

profile of v0, /device:TPU:8, one launch (start us, length us, event | category | flops | bytes accessed | tf_op | source)
XLA Modules:
  0.0 688.0 jit_solution(12936115907367004296)
XLA Ops:
  9.6 5.9 all-to-all-start.1
  16.5 4.6 convolution_convert_fusion.1
  23.4 7.4 %all-to-all-done.1 = bf16[4,64,1024]{2,0,1:T(4,128)(2,1)S(1)} async-done(((bf16[4,64,1024]{2,0,1:T(4,128)(2,1)}), bf16[4,64,1024]{2,0,1:T(4,128)(2,1)S(1)}, u32[]{:S(2)}, u32[]{:S(2)}) %all-to-all-start.1) | async-done | bytes 524320 | tf_op jit(solution)/shard_map/all_to_all | solution.py:84
  30.9 4.3 all-to-all-start
  39.2 33.7 %all-to-all-done = bf16[4,64,3072]{2,0,1:T(4,128)(2,1)} async-done(((bf16[4,64,3072]{2,0,1:T(4,128)(2,1)}), bf16[4,64,3072]{2,0,1:T(4,128)(2,1)}, u32[]{:S(2)}, u32[]{:S(2)}) %all-to-all-start) | async-done | bytes 1572896 | tf_op jit(solution)/shard_map/all_to_all | solution.py:83
  76.2 4.9 reshape.124
  81.1 4.2 fusion.59
  85.3 4.7 fusion.60
  90.0 2.9 convert_reduce_fusion
  93.0 14.5 %psum.28 = f32[1024]{0:T(1024)S(1)} all-reduce(f32[1024]{0:T(1024)S(1)} %add.59), channel_id=1, replica_groups=mesh['dp'=32,'frame'=8] {'frame'}, use_global_device_ids=true, to_apply=%region_6.0 | all-reduce | flops 1024 | bytes 8192 | tf_op jit(solution)/shard_map/psum | solution.py:92
  107.9 107.6 %all-gather = f32[32768]{0:T(1024)S(1)} all-gather(f32[1024]{0:T(1024)S(1)} %bitcast.140), channel_id=2, replica_groups=mesh['dp'=32,'frame'=8] {'dp'}, dimensions={0}, use_global_device_ids=true | all-gather | bytes 135168 | tf_op jit(solution)/shard_map/all_gather | solution.py:99
  215.9 25.9 %psum.29 = f32[32,32]{1,0:T(8,128)S(1)} all-reduce(f32[32,32]{1,0:T(8,128)S(1)} %fusion.62), channel_id=1, replica_groups=mesh['dp'=32,'frame'=8] {'frame'}, use_global_device_ids=true, to_apply=%region_8.0 | all-reduce | flops 1024 | bytes 8192 | tf_op jit(solution)/shard_map/psum | solution.py:101
  242.7 13.8 %psum.30 = f32[1024]{0:T(1024)S(1)} all-reduce(f32[1024]{0:T(1024)S(1)} %bitcast.141), channel_id=1, replica_groups=mesh['dp'=32,'frame'=8] {'frame'}, use_global_device_ids=true, to_apply=%region_10.0 | all-reduce | flops 1024 | bytes 8192 | tf_op jit(solution)/shard_map/psum | solution.py:120
  263.0 6.1 fusion.25
  269.1 6.1 fusion.22
  280.7 4.9 convert_element_type.98
  285.6 4.3 all-to-all-start.2
  290.3 37.5 %all-to-all-done.2 = bf16[32,8,3072]{2,1,0:T(8,128)(2,1)} async-done(((bf16[32,8,3072]{2,1,0:T(8,128)(2,1)}), bf16[32,8,3072]{2,1,0:T(8,128)(2,1)}, u32[]{:S(2)}, u32[]{:S(2)}) %all-to-all-start.2) | async-done | bytes 1572896 | tf_op jit(solution)/shard_map/all_to_all | solution.py:127
  329.3 4.5 convolution_convert_fusion
  333.9 116.5 %all-gather.1 = bf16[32768]{0:T(1024)(128)(2,1)S(1)} all-gather(bf16[1024]{0:T(1024)(128)(2,1)S(1)} %multiply_convert_fusion.2), channel_id=3, replica_groups=mesh['dp'=32,'frame'=8] {'dp'}, dimensions={0}, use_global_device_ids=true | all-gather | bytes 67584 | tf_op jit(solution)/shard_map/all_gather | solution.py:112
  450.4 107.8 %all-gather.2 = bf16[32,1,1024]{2,1,0:T(2,128)(2,1)S(1)} all-gather(bf16[1,1,1024]{2,1,0:T(2,128)(2,1)S(1)} %bitcast.139), channel_id=1, replica_groups=mesh['dp'=32,'frame'=8] {'dp'}, dimensions={0}, use_global_device_ids=true | all-gather | bytes 67584 | tf_op jit(solution)/shard_map/all_gather | solution.py:113
  559.1 6.4 multiply_reduce_fusion.2
  565.6 36.9 %reduce-scatter.5.cloned.1.call-done = bf16[32,3072]{1,0:T(8,128)(2,1)} async-done(((bf16[1024,3072]{1,0:T(8,128)(2,1)}), bf16[32,3072]{1,0:T(8,128)(2,1)}) %reduce-scatter.5.cloned.1.call-update) | async-done | bytes 196624 | tf_op jit(solution)/shard_map/reduce_scatter | solution.py:132
  604.6 72.4 %psum.31 = f32[1024]{0:T(1024)} all-reduce(f32[1024]{0:T(1024)S(1)} %get-tuple-element.4), channel_id=1, replica_groups=mesh['dp'=32,'frame'=8] {'dp','frame'}, use_global_device_ids=true, to_apply=%region_17.0 | all-reduce | flops 1024 | bytes 8192 | tf_op jit(solution)/shard_map/psum | solution.py:143
  (61 shorter events, 35.8 us)
Async XLA Ops:
  7.2 100.3 %copy-start = (bf16[1024,1024]{1,0:T(8,128)(2,1)S(1)}, bf16[1024,1024]{1,0:T(8,128)(2,1)}, u32[]{:S(2)}) copy-start(bf16[1024,1024]{1,0:T(8,128)(2,1)} %param.9) | copy-start | bytes 6291460
  7.2 8.3 %copy-start.1 = (bf16[1,4,64,1024]{3,2,1,0:T(8,128)(2,1)S(1)}, bf16[1,4,64,1024]{3,2,1,0:T(8,128)(2,1)}, u32[]{:S(2)}) copy-start(bf16[1,4,64,1024]{3,2,1,0:T(8,128)(2,1)} %param.5) | copy-start | bytes 1572868
  7.2 9.0 %copy-start.4 = (f32[1024]{0:T(1024)S(1)}, f32[1024]{0:T(1024)}, u32[]{:S(2)}) copy-start(f32[1024]{0:T(1024)} %param.7) | copy-start | bytes 12292
  9.6 21.3 %all-to-all-start.1 = ((bf16[4,64,1024]{2,0,1:T(4,128)(2,1)}), bf16[4,64,1024]{2,0,1:T(4,128)(2,1)S(1)}, u32[]{:S(2)}, u32[]{:S(2)}) async-start(bf16[4,64,1024]{2,0,1:T(4,128)(2,1)} %copy.55), calls=%async_computation.1 | async-start | bytes 1048576 | tf_op jit(solution)/shard_map/all_to_all | solution.py:84
  30.9 42.1 %all-to-all-start = ((bf16[4,64,3072]{2,0,1:T(4,128)(2,1)}), bf16[4,64,3072]{2,0,1:T(4,128)(2,1)}, u32[]{:S(2)}, u32[]{:S(2)}) async-start(bf16[4,64,3072]{2,0,1:T(4,128)(2,1)} %copy.48), calls=%async_computation | async-start | bytes 3145728 | tf_op jit(solution)/shard_map/all_to_all | solution.py:83
  256.5 2.0 copy-start.2
  258.5 2.7 copy-start.5
  285.6 42.1 %all-to-all-start.2 = ((bf16[32,8,3072]{2,1,0:T(8,128)(2,1)}), bf16[32,8,3072]{2,1,0:T(8,128)(2,1)}, u32[]{:S(2)}, u32[]{:S(2)}) async-start(bf16[32,8,3072]{2,1,0:T(8,128)(2,1)} %convert_element_type.98), calls=%async_computation.2 | async-start | bytes 3145728 | tf_op jit(solution)/shard_map/all_to_all | solution.py:127
  289.9 312.6 %reduce-scatter.5.cloned.1.call-start = ((), (), s32[]{:S(2)}) async-start(), calls=%async_computation.5 | async-start | bytes 6488064 | tf_op jit(solution)/shard_map/reduce_scatter | solution.py:132
  333.8 345.7 %reduce-scatter.7.cloned.1.call-start = ((), (), s32[]{:S(2)}) async-start(), calls=%async_computation.6 | async-start | bytes 884736
  565.6 111.5 %copy-start.3 = (bf16[1,4,64,1024]{3,2,1,0:T(8,128)(2,1)S(1)}, bf16[1,4,64,1024]{3,2,1,0:T(8,128)(2,1)}, u32[]{:S(2)}) copy-start(bf16[1,4,64,1024]{3,2,1,0:T(8,128)(2,1)} %param.6) | copy-start | bytes 1572868
Sparse Core Ops, SparseCore 0:
  334.0 268.4 reduce-scatter.4
  605.0 32.5 reduce-scatter.6
where the time goes:
time: 690 us; the launch traced here: 688 us
  blocking collectives  459 us (67%)
  waiting for transfers between devices  116 us (17%)
  matrix products  42.2 us (6%)
  local copies, waits for them, and re-layouts  33.9 us (5%)
  starting transfers between devices  14.6 us (2%)
  between operations  14.3 us (2%)
  other arithmetic  8.88 us (1%)
    all_gather x1, blocking collectives, per_device(): lax.all_gather(pooled_b[None, :], 'dp', axis=0, tiled=True)  116 us
    all_gather x1, blocking collectives, per_device(): lax.all_gather(embed_grad_b, 'dp', axis=0, tiled=True)  108 us
    all_gather x1, blocking collectives, per_device(): gathered = lax.all_gather(embedding, 'dp', axis=0, tiled=True)  108 us
    psum x1, blocking collectives, per_device(): lax.psum(jnp.sum(normed_grad * standard, axis=(0, 1)), ('dp', 'frame'))  72.4 us
    all_to_all x1, waiting for transfers between devices, per_device(): lax.all_to_all(projected_grad, 'frame', split_axis=0, concat_axis=1, tile...  37.5 us
    reduce_scatter x1, waiting for transfers between devices, per_device(): lax.psum_scatter(jnp.einsum('td,te->de', flat_normed, flat_grad, preferre...  36.9 us
    all_to_all x1, waiting for transfers between devices, per_device(): lax.all_to_all(projected, 'frame', split_axis=1, concat_axis=0, tiled=True)  33.7 us
    psum x1, blocking collectives, per_device(): lax.psum(jnp.dot(own_cols, own_cols.T, precision=lax.Precision.HIGHEST),...  25.9 us
  transfers between devices with their start and end apart: 5, of which 4 were waited for; matrix products, arithmetic and copies ran while one was open for 3% of the time, Pallas kernels for 0%

commit v1 on v0

v1 whole, which is shorter than its diff:
```python
import jax
import jax.numpy as jnp
from jax import lax
from jax.experimental import pallas as pl
from jax.experimental.pallas import tpu as pltpu
from jax.sharding import PartitionSpec as P

HEADS = 16
EPSILON = 1e-05
F32 = jnp.float32
BF16 = jnp.bfloat16
MIB = 1 << 20
NT = (((1,), (1,)), ((), ()))
TN = (((0,), (0,)), ((), ()))


def dot(a, b, dims=(((1,), (0,)), ((), ())), precision=None):
    return lax.dot_general(a, b, dims, precision=precision, preferred_element_type=F32)


def standardize(inputs):
    center = inputs - jnp.mean(inputs, axis=-1, keepdims=True)
    spread = lax.rsqrt(jnp.mean(center * center, axis=-1, keepdims=True) + EPSILON)
    return center * spread, spread


def params(mib):
    return pltpu.CompilerParams(vmem_limit_bytes=mib * MIB)


def cost(flops, moved, exps=0):
    return pl.CostEstimate(flops=flops, bytes_accessed=moved, transcendentals=exps)


def pack_kernel(source, packed):
    size = packed.shape[2]
    for group in range(packed.shape[0]):
        packed[group] = source[:, group * size : (group + 1) * size, :]


def unpack_kernel(packed, target):
    size = packed.shape[2]
    for group in range(packed.shape[0]):
        target[:, group * size : (group + 1) * size, :] = packed[group]


def pack(array, groups):
    frames, patches, width = array.shape
    shape = (groups, frames, patches // groups, width)
    return pl.pallas_call(
        pack_kernel,
        out_shape=jax.ShapeDtypeStruct(shape, array.dtype),
        compiler_params=params(8),
        cost_estimate=cost(0, 4 * array.size),
    )(array)


def unpack(array):
    groups, frames, size, width = array.shape
    return pl.pallas_call(
        unpack_kernel,
        out_shape=jax.ShapeDtypeStruct((frames, groups * size, width), array.dtype),
        compiler_params=params(8),
        cost_estimate=cost(0, 4 * array.size),
    )(array)


def lane_halves(slab):
    lane = lax.broadcasted_iota(jnp.int32, slab.shape, 1)
    low = lane < slab.shape[1] // 2
    zero = jnp.zeros_like(slab)
    return jnp.where(low, slab, zero), jnp.where(low, zero, slab)


def same_patch(rows, patches):
    first = lax.broadcasted_iota(jnp.int32, (rows, rows), 0)
    second = lax.broadcasted_iota(jnp.int32, (rows, rows), 1)
    return lax.rem(first, patches) == lax.rem(second, patches)


def softmax(query, keys, scale, mask):
    scores = jnp.where(mask, dot(query, keys, NT) * scale, -jnp.inf)
    weights = jnp.exp(scores - jnp.max(scores, axis=-1, keepdims=True))
    return weights / jnp.sum(weights, axis=-1, keepdims=True)


def forward_kernel(patches, x_ref, gain_ref, w_ref, normed_ref, proj_ref, pool_ref):
    rows, width = x_ref.shape
    inputs = x_ref[...].astype(F32)
    standard, _ = standardize(inputs)
    normed = (standard * gain_ref[...]).astype(BF16)
    normed_ref[...] = normed
    pool_ref[...] = jnp.sum(inputs, axis=0, keepdims=True)
    for part in range(6):
        cols = pl.ds(part * width // 2, width // 2)
        proj_ref[:, cols] = dot(normed, w_ref[:, cols]).astype(BF16)
    mask = same_patch(rows, patches)
    slab = 2 * width // HEADS
    scale = (width // HEADS) ** -0.5
    for pair in range(HEADS // 2):
        at = pair * slab
        query = proj_ref[:, at : at + slab]
        keys = proj_ref[:, width + at : width + at + slab]
        values = proj_ref[:, 2 * width + at : 2 * width + at + slab]
        probs = [softmax(part, keys, scale, mask).astype(BF16) for part in lane_halves(query)]
        attended = dot(jnp.concatenate(probs, 1), jnp.concatenate(lane_halves(values), 0))
        attended = attended.astype(BF16).astype(F32)
        pool_ref[:, at : at + slab] += jnp.sum(attended, axis=0, keepdims=True)


def forward(tokens, gain, w_project, patches):
    rows, width = tokens.shape
    return pl.pallas_call(
        lambda *refs: forward_kernel(patches, *refs),
        out_shape=(
            jax.ShapeDtypeStruct((rows, width), BF16),
            jax.ShapeDtypeStruct((rows, 3 * width), BF16),
            jax.ShapeDtypeStruct((1, width), F32),
        ),
        compiler_params=params(40),
        cost_estimate=cost(10 * rows * width * width, 10 * MIB, HEADS * rows * rows),
    )(tokens, gain, w_project)


def backward_kernel(patches, block, core_ref, proj_ref, grad_ref, share_ref, out_ref, send_ref):
    rows, width = grad_ref.shape
    mask = same_patch(rows, patches)
    slab = 2 * width // HEADS
    scale = (width // HEADS) ** -0.5
    for pair in range(HEADS // 2):
        at = pair * slab
        query = proj_ref[:, at : at + slab]
        keys = proj_ref[:, width + at : width + at + slab]
        values = proj_ref[:, 2 * width + at : 2 * width + at + slab]
        grads = grad_ref[:, at : at + slab].astype(F32) + share_ref[:, at : at + slab]
        grads = grads.astype(BF16)
        query_halves = lane_halves(query)
        grad_halves = lane_halves(grads)
        rounded, score_grads = [], []
        for part, grad in zip(query_halves, grad_halves):
            probs = softmax(part, keys, scale, mask)
            prob_grad = dot(grad, values, NT)
            centered = prob_grad - jnp.sum(probs * prob_grad, axis=-1, keepdims=True)
            score_grads.append((probs * centered * scale).astype(BF16))
            rounded.append(probs.astype(BF16))
        key_halves = lane_halves(keys)
        query_grad = dot(jnp.concatenate(score_grads, 1), jnp.concatenate(key_halves, 0))
        key_grad = dot(jnp.concatenate(score_grads, 0), jnp.concatenate(query_halves, 0), TN)
        value_grad = dot(jnp.concatenate(rounded, 0), jnp.concatenate(grad_halves, 0), TN)
        for first, part in zip((0, width, 2 * width), (query_grad, key_grad, value_grad)):
            start = first + at
            part = part.astype(BF16)
            out_ref[:, start : start + slab] = part
            number, inside = divmod(start, block)
            owner, place = number % 2, number // 2 * block + inside

            @pl.when(core_ref[0] != owner)
            def _():
                send_ref[:, place : place + slab] = part


def backward(core, projected, grads, share, patches, block):
    rows, width = grads.shape
    return pl.pallas_call(
        lambda *refs: backward_kernel(patches, block, *refs),
        in_specs=[pl.BlockSpec(memory_space=pltpu.SMEM)]
        + [pl.BlockSpec(memory_space=pltpu.VMEM)] * 3,
        out_shape=(
            jax.ShapeDtypeStruct(projected.shape, BF16),
            jax.ShapeDtypeStruct((rows, projected.shape[1] // 2), BF16),
        ),
        compiler_params=params(40),
        cost_estimate=cost(16 * rows * rows * width, 8 * MIB, HEADS * rows * rows),
    )(core.reshape(1), projected, grads, share)


def weight_kernel(_, own_ref, other_ref, grad_ref, other_grad_ref, out_ref, flipped):
    rows = own_ref.shape[0]

    @pl.when(pl.program_id(0) == 0)
    def _():
        flipped[:, :rows] = own_ref[...].T
        flipped[:, rows:] = other_ref[...].T

    both = jnp.concatenate([grad_ref[...], other_grad_ref[...]], axis=0)
    terms = dot(flipped[...], both).astype(BF16)
    groups, halves, block = out_ref.shape[:3]
    for half in range(halves):
        for group in range(groups):
            at = (half * groups + group) * block
            out_ref[group, half] = terms[at : at + block]


def weight_terms(core, normed, other_normed, grads, other_grads, groups, halves, steps, cores):
    rows, width = normed.shape
    cols = other_grads.shape[1]
    step = cols // steps
    block = width // (groups * halves)
    return pl.pallas_call(
        weight_kernel,
        grid_spec=pltpu.PrefetchScalarGridSpec(
            num_scalar_prefetch=1,
            grid=(steps,),
            in_specs=[
                pl.BlockSpec((rows, width), lambda i, core: (0, 0)),
                pl.BlockSpec((rows, width), lambda i, core: (0, 0)),
                pl.BlockSpec((rows, step), lambda i, core: (0, cores * i + core[0])),
                pl.BlockSpec((rows, step), lambda i, core: (0, i)),
            ],
            out_specs=pl.BlockSpec(
                (groups, halves, block, step), lambda i, core: (0, 0, 0, i)
            ),
            scratch_shapes=[pltpu.VMEM((width, 2 * rows), BF16)],
        ),
        out_shape=jax.ShapeDtypeStruct((groups, halves, block, cols), BF16),
        compiler_params=params(40),
        cost_estimate=cost(4 * rows * width * cols, 6 * MIB),
    )(core.reshape(1), normed, other_normed, grads, other_grads)


def token_kernel(x_ref, grad_ref, share_ref, gain_ref, proj_ref, w_ref, out_ref, gain_out, total):
    step = pl.program_id(0)
    term = dot(proj_ref[...], w_ref[...], NT)

    @pl.when(step == 0)
    def _():
        total[...] = term

    @pl.when(step > 0)
    def _():
        total[...] += term

    @pl.when(step == pl.num_programs(0) - 1)
    def _():
        normed_grad = total[...]
        standard, spread = standardize(x_ref[...].astype(F32))
        gain_out[...] = jnp.sum(normed_grad * standard, axis=0, keepdims=True)
        scaled = normed_grad * gain_ref[...]
        centered = (
            scaled
            - jnp.mean(scaled, axis=-1, keepdims=True)
            - standard * jnp.mean(scaled * standard, axis=-1, keepdims=True)
        )
        total_grad = grad_ref[...].astype(F32) + share_ref[...]
        out_ref[...] = (total_grad + spread * centered).astype(BF16)


def token_grads(tokens, grads, share, gain, proj_grad, w_project, blocks=3):
    rows, width = tokens.shape
    cols = w_project.shape[1] // blocks
    whole = lambda a: pl.BlockSpec(a.shape, lambda i: (0, 0))
    return pl.pallas_call(
        token_kernel,
        grid=(blocks,),
        in_specs=[
            whole(tokens),
            whole(grads),
            whole(share),
            whole(gain),
            pl.BlockSpec((rows, cols), lambda i: (0, i)),
            pl.BlockSpec((width, cols), lambda i: (0, i)),
        ],
        out_specs=(
            pl.BlockSpec((rows, width), lambda i: (0, 0)),
            pl.BlockSpec((1, width), lambda i: (0, 0)),
        ),
        out_shape=(
            jax.ShapeDtypeStruct((rows, width), BF16),
            jax.ShapeDtypeStruct((1, width), F32),
        ),
        scratch_shapes=[pltpu.VMEM((rows, width), F32)],
        compiler_params=params(40),
        cost_estimate=cost(6 * rows * width * width, 9 * MIB),
    )(tokens, grads, share, gain, proj_grad, w_project)


def embed_kernel(pooled_ref, w_ref, centered_ref, gram_ref):
    embedding = dot(pooled_ref[...], w_ref[...])
    centered = embedding - jnp.mean(embedding, axis=0, keepdims=True)
    centered_ref[...] = centered
    gram_ref[...] = dot(centered, centered, NT, lax.Precision.HIGHEST)


def embed(pooled_all, w_expand):
    clips = pooled_all.shape[0]
    return pl.pallas_call(
        embed_kernel,
        out_shape=(
            jax.ShapeDtypeStruct((clips, w_expand.shape[1]), F32),
            jax.ShapeDtypeStruct((clips, clips), F32),
        ),
        compiler_params=params(16),
        cost_estimate=cost(2 * clips * w_expand.size, 2 * MIB),
    )(pooled_all, w_expand)


def embed_grad_kernel(coefficient, gram_ref, centered_ref, own_ref, w_ref, grad_ref, pool_ref):
    clips = gram_ref.shape[0]
    centered = centered_ref[...]
    variances = jnp.sum(centered * centered, axis=0, keepdims=True) / (clips - 1)
    mixed = dot(gram_ref[...], centered, precision=lax.Precision.HIGHEST)
    grads = coefficient * (mixed / (clips - 1) - centered * variances)
    grads_b = grads.astype(BF16)
    grad_ref[...] = grads_b
    row = lax.broadcasted_iota(jnp.int32, grads.shape, 0)
    own = jnp.where(row == own_ref[0], grads, 0.0)
    own = jnp.sum(own, axis=0, keepdims=True)
    own = jnp.broadcast_to(own, (16, own.shape[1])).astype(BF16)
    pool_ref[...] = dot(own, w_ref[...], NT)[0:1]


def embed_grads(gram, centered, own_index, w_expand, coefficient):
    return pl.pallas_call(
        lambda *refs: embed_grad_kernel(coefficient, *refs),
        in_specs=[
            pl.BlockSpec(memory_space=pltpu.VMEM),
            pl.BlockSpec(memory_space=pltpu.VMEM),
            pl.BlockSpec(memory_space=pltpu.SMEM),
            pl.BlockSpec(memory_space=pltpu.VMEM),
        ],
        out_shape=(
            jax.ShapeDtypeStruct(centered.shape, BF16),
            jax.ShapeDtypeStruct((1, w_expand.shape[0]), F32),
        ),
        compiler_params=params(16),
        cost_estimate=cost(2 * 16 * w_expand.size, 2 * MIB),
    )(gram, centered, own_index.reshape(1), w_expand)


DP = ("zh", "x", "y")
FRAME = ("zl", "core")
SIZES = {"zh": 2, "x": 4, "y": 4, "zl": 4, "core": 2}
SWAP = [(0, 1), (1, 0)]


def exchange(array, axis):
    count = lax.axis_size(axis)
    copies = jnp.broadcast_to(array[None], (count,) + array.shape)
    return lax.all_to_all(copies, axis, split_axis=0, concat_axis=0, tiled=True)


def per_device(clip_tokens, out_grad, ln_gain, w_project, w_expand):
    frame_count = lax.axis_size(FRAME)
    clip_count = lax.axis_size(DP)
    core = lax.axis_index("core")
    frames_dev, patches, width = clip_tokens.shape[1:]
    patches_dev = patches // frame_count
    rows = frames_dev * patches
    tokens_clip = frames_dev * frame_count * patches
    column_block = 3 * width // frame_count
    gain = ln_gain[None, :]

    def to_patches(array):
        moved = lax.all_to_all(
            pack(array, frame_count), FRAME, split_axis=0, concat_axis=0, tiled=True
        )
        return moved.reshape(rows, width)

    tokens = to_patches(clip_tokens[0])
    grads = to_patches(out_grad[0])
    normed, projected, pool_part = forward(tokens, gain, w_project, patches_dev)
    other_normed = lax.ppermute(normed, "core", SWAP)

    pooled = jnp.sum(exchange(pool_part[0], FRAME), axis=0) / tokens_clip
    pooled_all = exchange(pooled.astype(BF16), DP)
    centered, gram_part = embed(pooled_all, w_expand)
    gram = jnp.sum(exchange(gram_part, FRAME), axis=0)
    own_index = lax.axis_index(DP)
    coefficient = 100.0 * tokens_clip / (w_expand.shape[1] * frame_count * (clip_count - 1))
    embed_grad, pool_grad_part = embed_grads(gram, centered, own_index, w_expand, coefficient)
    block_rows = width // clip_count
    row_part = lax.dynamic_slice_in_dim(pooled_all, own_index * block_rows, block_rows, 1)
    expand_grad = dot(row_part, embed_grad, TN)
    share = jnp.sum(exchange(pool_grad_part, FRAME), axis=0) / tokens_clip

    projected_grad, outgoing = backward(core, projected, grads, share, patches_dev, column_block)
    other_grad = lax.ppermute(outgoing, "core", SWAP)
    terms = weight_terms(
        core,
        normed,
        other_normed,
        projected_grad,
        other_grad,
        lax.axis_size(("x", "y")),
        lax.axis_size("zh"),
        lax.axis_size("zl"),
        lax.axis_size("core"),
    )
    terms = lax.all_to_all(terms, ("x", "y"), split_axis=0, concat_axis=0, tiled=True)
    terms = jnp.sum(terms.astype(F32), axis=0).astype(BF16)
    terms = terms.reshape(terms.shape[0], block_rows, lax.axis_size("zl"), column_block)
    terms = terms.swapaxes(1, 2).reshape(-1, block_rows, column_block)
    terms = lax.all_to_all(terms, ("zh", "zl"), split_axis=0, concat_axis=0, tiled=True)
    project_grad = jnp.sum(terms.astype(F32), axis=0)

    token_part, gain_part = token_grads(tokens, grads, share, gain, projected_grad, w_project)
    returned = lax.all_to_all(
        token_part.reshape(frame_count, frames_dev, patches_dev, width),
        FRAME,
        split_axis=0,
        concat_axis=0,
        tiled=True,
    )
    token_grad = unpack(returned)[None]
    gain_clip = jnp.sum(exchange(gain_part, FRAME), axis=0)
    gain_grad = jnp.sum(exchange(gain_clip, DP), axis=0)[0]
    return (token_grad, project_grad, expand_grad, gain_grad)


def solution(mesh):
    split = jax.sharding.Mesh(
        mesh.devices.reshape(tuple(SIZES.values())), tuple(SIZES)
    )
    return jax.shard_map(
        per_device,
        mesh=split,
        in_specs=(
            P(DP, FRAME, None, None),
            P(DP, FRAME, None, None),
            P(),
            P(),
            P(None, FRAME),
        ),
        out_specs=(P(DP, FRAME, None, None), P(DP, FRAME), P(DP, FRAME), P()),
        check_vma=False,
    )
```

time: 690 us -> 234 us (0.34)
  blocking collectives: 459 us -> 103 us
  waiting for transfers between devices: 116 us -> 47 us
  matrix products: 42.2 us -> 0.85 us
  Pallas kernels: 0 us -> 24.1 us
  between operations: 14.3 us -> 0.9 us
  starting transfers between devices: 14.6 us -> 25.9 us
  local copies, waits for them, and re-layouts: 33.9 us -> 23.6 us
    all_gather x3 -> x0, blocking collectives: 332 us -> none  [the longest x1 116 us: per_device(): lax.all_gather(pooled_b[None, :], 'dp', axis=0, tiled=True)]
    psum x4 -> x0, blocking collectives: 127 us -> none  [the longest x1 72.4 us: per_device(): lax.psum(jnp.sum(normed_grad * standard, axis=(0, 1)), ('dp', 'frame'))]
    all_to_all x0 -> x5, blocking collectives: none -> 103 us  [the longest x1 43.8 us: per_device(): lax.all_to_all(terms, ('x', 'y'), split_axis=0, concat_axis=0, tiled=True)]
    reduce_scatter x1 -> x0, waiting for transfers between devices: 36.9 us -> none  [per_device(): lax.psum_scatter(jnp.einsum('td,te->de', flat_normed, flat_grad, preferre...]
    dot_general x13 -> x1, matrix products: 37.5 us -> 0.85 us  [dot(): lax.dot_general(a, b, dims, precision=precision, preferred_element_type=F32)]
    all_to_all x3 -> x6, waiting for transfers between devices: 78.6 us -> 47 us  [the longest x1 15.2 us: to_patches(): lax.all_to_all(pack(array, frame_count), FRAME, split_axis=0, concat_axis...]
    pallas_call x0 -> x9, Pallas kernels: none -> 24.1 us  [the longest x1 8.27 us: backward(): pl.pallas_call(lambda *refs: backward_kernel(patches, block, *refs), in_s...]
    unnamed x14 -> x43, local copies, waits for them, and re-layouts: 3.08 us -> 20.3 us
  transfers between devices with their start and end apart: 5 -> 8, of which waited for: 4 -> 6; matrix products, arithmetic and copies ran while one was open for 3% -> 2% of each run, Pallas kernels for 0% -> 4%
where the time goes in v1:
time: 234 us; the launch traced here: 233 us
  blocking collectives  103 us (44%)
  waiting for transfers between devices  47 us (20%)
  starting transfers between devices  25.9 us (11%)
  Pallas kernels  24.1 us (10%)
  local copies, waits for them, and re-layouts  23.6 us (10%)
  other arithmetic  7.13 us (3%)
    all_to_all x1, blocking collectives, per_device(): lax.all_to_all(terms, ('x', 'y'), split_axis=0, concat_axis=0, tiled=True)  43.8 us
    all_to_all x3, blocking collectives, exchange(): return lax.all_to_all(copies, axis, split_axis=0, concat_axis=0, tiled=True)  38.5 us
    all_to_all x1, blocking collectives, to_patches(): lax.all_to_all(pack(array, frame_count), FRAME, split_axis=0, concat_axis...  21.1 us
    unnamed x43, local copies, waits for them, and re-layouts  20.3 us
    all_to_all x1, waiting for transfers between devices, to_patches(): lax.all_to_all(pack(array, frame_count), FRAME, split_axis=0, concat_axis...  15.2 us
    all_to_all x1, waiting for transfers between devices, per_device(): lax.all_to_all(token_part.reshape(frame_count, frames_dev, patches_dev, w...  12.2 us
    all_to_all x3, waiting for transfers between devices, exchange(): return lax.all_to_all(copies, axis, split_axis=0, concat_axis=0, tiled=True)  11.7 us
    all_to_all x3, starting transfers between devices, exchange(): return lax.all_to_all(copies, axis, split_axis=0, concat_axis=0, tiled=True)  11.6 us
  transfers between devices with their start and end apart: 8, of which 6 were waited for; matrix products, arithmetic and copies ran while one was open for 2% of the time, Pallas kernels for 4%

profile of v1, /device:TPU:8, one launch (start us, length us, event | category | flops | bytes accessed | tf_op | source)
XLA Modules:
  0.0 232.8 jit_solution(8817069881504917033)
XLA Ops:
  1.7 21.1 %all_to_all.59 = bf16[8,4,8,1024]{3,2,1,0:T(8,128)(2,1)S(1)} all-to-all(bf16[8,4,8,1024]{3,2,1,0:T(8,128)(2,1)S(1)} %shard_map.84), channel_id=1, replica_groups=mesh['zh'=2,'x'=4,'y'=4,'zl'=4,'core'=2] {'zl','core'}, dimensions={0} | all-to-all | bytes 1048576 | tf_op jit(solution)/shard_map/all_to_all | solution.py:354
  22.8 2.8 %copy-done.1 = bf16[1024,3072]{1,0:T(8,128)(2,1)S(1)} copy-done((bf16[1024,3072]{1,0:T(8,128)(2,1)S(1)}, bf16[1024,3072]{1,0:T(8,128)(2,1)}, u32[]{:S(2)}) %copy-start.1) | copy-done | bytes 6291480
  26.2 5.2 %shard_map.86 = (bf16[256,1024]{1,0:T(8,128)(2,1)S(1)}, bf16[256,3072]{1,0:T(8,128)(2,1)S(1)}, f32[1,1024]{1,0:T(1,128)S(1)}) custom-call(bf16[256,1024]{1,0:T(8,128)(2,1)S(1)} %bitcast.21, f32[1,1024]{1,0:T(1,128)S(1)} %bitcast.31, bf16[1024,3072]{1,0:T(8,128)(2,1)S(1)} %copy-done.1), custom_call_target="tpu_custom_call" | custom-call | flops 2684354560 | bytes 10485760 | tf_op jit(solution)/shard_map/pallas_call | solution.py:113
  33.4 8.1 %all_to_all.60 = f32[8,1,1024]{2,1,0:T(1,128)S(1)} all-to-all(f32[8,1,1024]{2,1,0:T(1,128)S(1)} %broadcast_in_dim.21), channel_id=1, replica_groups=mesh['zh'=2,'x'=4,'y'=4,'zl'=4,'core'=2] {'zl','core'}, dimensions={0} | all-to-all | bytes 65536 | tf_op jit(solution)/shard_map/all_to_all | solution.py:339
  43.2 22.3 %all_to_all.61 = bf16[32,2,512]{2,1,0:T(2,128)(2,1)S(1)} all-to-all(bf16[32,2,512]{2,1,0:T(2,128)(2,1)S(1)} %reshape.76), channel_id=1, replica_groups=mesh['zh'=2,'x'=4,'y'=4,'zl'=4,'core'=2] {'zh','x','y'}, dimensions={0} | all-to-all | bytes 131072 | tf_op jit(solution)/shard_map/all_to_all | solution.py:339
  67.0 1.6 reshape.78
  68.6 3.3 %all-to-all-start.4 = ((f32[8,1,1024]{2,1,0:T(1,128)}), f32[8,1,1024]{2,1,0:T(1,128)S(1)}, u32[]{:S(2)}, u32[]{:S(2)}) async-start(f32[8,1,1024]{2,1,0:T(1,128)} %reshape.78), calls=%async_computation.4 | async-start | bytes 65536 | tf_op jit(solution)/shard_map/all_to_all | solution.py:339
  72.0 5.7 %all-to-all-done.4 = f32[8,1,1024]{2,1,0:T(1,128)S(1)} async-done(((f32[8,1,1024]{2,1,0:T(1,128)}), f32[8,1,1024]{2,1,0:T(1,128)S(1)}, u32[]{:S(2)}, u32[]{:S(2)}) %all-to-all-start.4) | async-done | bytes 32800 | tf_op jit(solution)/shard_map/all_to_all | solution.py:339
  82.0 3.3 %all-to-all-start.5 = ((f32[8,1,1024]{2,1,0:T(1,128)}), f32[8,1,1024]{2,1,0:T(1,128)S(1)}, u32[]{:S(2)}, u32[]{:S(2)}) async-start(f32[8,1,1024]{2,1,0:T(1,128)} %broadcast_in_dim.50), calls=%async_computation.5 | async-start | bytes 65536 | tf_op jit(solution)/shard_map/all_to_all | solution.py:339
  86.2 4.8 %all-to-all-done.5 = f32[8,1,1024]{2,1,0:T(1,128)S(1)} async-done(((f32[8,1,1024]{2,1,0:T(1,128)}), f32[8,1,1024]{2,1,0:T(1,128)S(1)}, u32[]{:S(2)}, u32[]{:S(2)}) %all-to-all-start.5) | async-done | bytes 32800 | tf_op jit(solution)/shard_map/all_to_all | solution.py:339
  91.0 3.5 %all-to-all-start.1 = ((bf16[8,4,8,1024]{3,2,1,0:T(8,128)(2,1)}), bf16[8,4,8,1024]{3,2,1,0:T(8,128)(2,1)S(1)}, u32[]{:S(2)}, u32[]{:S(2)}) async-start(bf16[8,4,8,1024]{3,2,1,0:T(8,128)(2,1)} %shard_map.85), calls=%async_computation.1 | async-start | bytes 1048576 | tf_op jit(solution)/shard_map/all_to_all | solution.py:354
  94.6 15.2 %all-to-all-done.1 = bf16[8,4,8,1024]{3,2,1,0:T(8,128)(2,1)S(1)} async-done(((bf16[8,4,8,1024]{3,2,1,0:T(8,128)(2,1)}), bf16[8,4,8,1024]{3,2,1,0:T(8,128)(2,1)S(1)}, u32[]{:S(2)}, u32[]{:S(2)}) %all-to-all-start.1) | async-done | bytes 524320 | tf_op jit(solution)/shard_map/all_to_all | solution.py:354
  111.2 8.3 %shard_map.89 = (bf16[256,3072]{1,0:T(8,128)(2,1)S(1)}, bf16[256,1536]{1,0:T(8,128)(2,1)}) custom-call(s32[1]{0:T(128)} %bitcast.9.refs_0_._, bf16[256,3072]{1,0:T(8,128)(2,1)S(1)} %copy-done.18, bf16[256,1024]{1,0:T(8,128)(2,1)S(1)} %bitcast.23, f32[1,1024]{1,0:T(1,128)S(1)} %bitcast.29), custom_call_target="tpu_custom_call" | custom-call | flops 1073741824 | bytes 8388608 | tf_op jit(solution)/shard_map/pallas_call | solution.py:164
  120.0 2.8 %copy-done.2 = bf16[1024,3072]{1,0:T(8,128)(2,1)S(1)} copy-done((bf16[1024,3072]{1,0:T(8,128)(2,1)S(1)}, bf16[1024,3072]{1,0:T(8,128)(2,1)}, u32[]{:S(2)}) %copy-start.2) | copy-done | bytes 6291480
  122.8 3.8 %shard_map.90 = (bf16[256,1024]{1,0:T(8,128)(2,1)S(1)}, f32[1,1024]{1,0:T(1,128)S(1)}) custom-call(bf16[256,1024]{1,0:T(8,128)(2,1)S(1)} %bitcast.22, bf16[256,1024]{1,0:T(8,128)(2,1)S(1)} %bitcast.24, f32[1,1024]{1,0:T(1,128)S(1)} %bitcast.30, f32[1,1024]{1,0:T(1,128)S(1)} %bitcast.32, bf16[256,3072]{1,0:T(8,128)(2,1)S(1)} %get-tuple-element.20.proj_ref.grad_ref, ...), custom_call_target="tpu_custom_call" | custom-call | flops 1610612736 | bytes 9437184 | tf_op jit(solution)/shard_map/pallas_call | solution.py:252
  127.5 8.1 %all_to_all.62 = f32[8,1,1024]{2,1,0:T(1,128)S(1)} all-to-all(f32[8,1,1024]{2,1,0:T(1,128)S(1)} %broadcast_in_dim.53), channel_id=1, replica_groups=mesh['zh'=2,'x'=4,'y'=4,'zl'=4,'core'=2] {'zl','core'}, dimensions={0} | all-to-all | bytes 65536 | tf_op jit(solution)/shard_map/all_to_all | solution.py:339
  136.4 5.0 %all-to-all-start.10 = ((f32[32,1,1024]{2,1,0:T(1,128)}), f32[32,1,1024]{2,1,0:T(1,128)S(1)}, u32[]{:S(2)}, u32[]{:S(2)}) async-start(f32[32,1,1024]{2,1,0:T(1,128)} %broadcast_in_dim.54), calls=%async_computation.10 | async-start | bytes 262144 | tf_op jit(solution)/shard_map/all_to_all | solution.py:339
  147.7 3.7 %shard_map.92 = bf16[16,2,32,1536]{3,2,1,0:T(8,128)(2,1)S(1)} custom-call(s32[1]{0:T(128)} %bitcast.9.refs_0_._, bf16[256,1024]{1,0:T(8,128)(2,1)S(1)} %copy-done.12, bf16[256,1024]{1,0:T(8,128)(2,1)S(1)} %copy-done.14, bf16[256,3072]{1,0:T(8,128)(2,1)S(1)} %copy-done.4, bf16[256,1536]{1,0:T(8,128)(2,1)S(1)} %copy-done.6), custom_call_target="tpu_custom_call" | custom-call | flops 1610612736 | bytes 6291456 | tf_op jit(solution)/shard_map/pallas_call | solution.py:199
  152.6 43.8 %all_to_all.63 = bf16[16,2,32,1536]{3,2,1,0:T(8,128)(2,1)} all-to-all(bf16[16,2,32,1536]{3,2,1,0:T(8,128)(2,1)S(1)} %shard_map.92), channel_id=1, replica_groups=mesh['zh'=2,'x'=4,'y'=4,'zl'=4,'core'=2] {'x','y'}, dimensions={0} | all-to-all | bytes 6291456 | tf_op jit(solution)/shard_map/all_to_all | solution.py:389
  196.4 3.5 %all-to-all-start.6 = ((bf16[8,4,8,1024]{3,2,1,0:T(8,128)(2,1)}), bf16[8,4,8,1024]{3,2,1,0:T(8,128)(2,1)S(1)}, u32[]{:S(2)}, u32[]{:S(2)}) async-start(bf16[8,4,8,1024]{3,2,1,0:T(8,128)(2,1)} %bitcast.27), calls=%async_computation.6 | async-start | bytes 1048576 | tf_op jit(solution)/shard_map/all_to_all | solution.py:397
  199.9 2.4 %reduce_sum.69 = bf16[2,32,1536]{2,1,0:T(8,128)(2,1)S(1)} reduce(bf16[16,2,32,1536]{3,2,1,0:T(8,128)(2,1)} %all_to_all.63, bf16[]{:T(256)} %constant.33.clone.1), dimensions={0}, to_apply=%region_3.0 | reduce | flops 1474560 | bytes 3342338 | tf_op jit(solution)/shard_map/reduce_sum | solution.py:390
  203.0 12.2 %all-to-all-done.6.packed = bf16[8,4,8,1024]{3,2,1,0:T(8,128)(2,1)S(1)} async-done(((bf16[8,4,8,1024]{3,2,1,0:T(8,128)(2,1)}), bf16[8,4,8,1024]{3,2,1,0:T(8,128)(2,1)S(1)}, u32[]{:S(2)}, u32[]{:S(2)}) %all-to-all-start.6) | async-done | bytes 524320 | tf_op jit(solution)/shard_map/all_to_all | solution.py:397
  215.2 6.7 %all-to-all-start.8 = ((bf16[8,32,384]{2,1,0:T(8,128)(2,1)}), bf16[8,32,384]{2,1,0:T(8,128)(2,1)S(1)}, u32[]{:S(2)}, u32[]{:S(2)}) async-start(bf16[8,32,384]{2,1,0:T(8,128)(2,1)} %bitcast.12), calls=%async_computation.8 | async-start | bytes 393216 | tf_op jit(solution)/shard_map/all_to_all | solution.py:393
  224.4 7.8 %all-to-all-done.8 = bf16[8,32,384]{2,1,0:T(8,128)(2,1)S(1)} async-done(((bf16[8,32,384]{2,1,0:T(8,128)(2,1)}), bf16[8,32,384]{2,1,0:T(8,128)(2,1)S(1)}, u32[]{:S(2)}, u32[]{:S(2)}) %all-to-all-start.8) | async-done | bytes 196640 | tf_op jit(solution)/shard_map/all_to_all | solution.py:393
  (72 shorter events, 26.9 us)
Async XLA Ops:
  0.6 1.0 copy-start.7
  22.8 2.8 %copy-start.1 = (bf16[1024,3072]{1,0:T(8,128)(2,1)S(1)}, bf16[1024,3072]{1,0:T(8,128)(2,1)}, u32[]{:S(2)}) copy-start(bf16[1024,3072]{1,0:T(8,128)(2,1)} %w_ref.3) | copy-start | bytes 18874372
  26.2 39.4 %copy-start = (bf16[1024,1024]{1,0:T(8,128)(2,1)S(1)}, bf16[1024,1024]{1,0:T(8,128)(2,1)}, u32[]{:S(2)}) copy-start(bf16[1024,1024]{1,0:T(8,128)(2,1)} %refs_3_.1) | copy-start | bytes 6291460
  31.4 0.8 copy-start.10
  32.2 1.2 copy-start.17
  41.6 43.8 %copy-start.8 = (bf16[1,4,64,1024]{3,2,1,0:T(8,128)(2,1)S(1)}, bf16[1,4,64,1024]{3,2,1,0:T(8,128)(2,1)}, u32[]{:S(2)}) copy-start(bf16[1,4,64,1024]{3,2,1,0:T(8,128)(2,1)} %param.6) | copy-start | bytes 1572868
  68.6 9.0 %all-to-all-start.4 = ((f32[8,1,1024]{2,1,0:T(1,128)}), f32[8,1,1024]{2,1,0:T(1,128)S(1)}, u32[]{:S(2)}, u32[]{:S(2)}) async-start(f32[8,1,1024]{2,1,0:T(1,128)} %reshape.78), calls=%async_computation.4 | async-start | bytes 65536 | tf_op jit(solution)/shard_map/all_to_all | solution.py:339
  81.4 38.1 %copy-start.11 = (bf16[256,1024]{1,0:T(8,128)(2,1)S(1)}, bf16[256,1024]{1,0:T(8,128)(2,1)}, u32[]{:S(2)}) copy-start(bf16[256,1024]{1,0:T(8,128)(2,1)} %copy-done.10) | copy-start | bytes 1572868
  81.4 38.7 %copy-start.16 = (f32[1024]{0:T(1024)S(1)}, f32[1024]{0:T(1024)}, u32[]{:S(2)}) copy-start(f32[1024]{0:T(1024)} %param.7) | copy-start | bytes 12292
  82.0 9.0 %all-to-all-start.5 = ((f32[8,1,1024]{2,1,0:T(1,128)}), f32[8,1,1024]{2,1,0:T(1,128)S(1)}, u32[]{:S(2)}, u32[]{:S(2)}) async-start(f32[8,1,1024]{2,1,0:T(1,128)} %broadcast_in_dim.50), calls=%async_computation.5 | async-start | bytes 65536 | tf_op jit(solution)/shard_map/all_to_all | solution.py:339
  91.0 18.8 %all-to-all-start.1 = ((bf16[8,4,8,1024]{3,2,1,0:T(8,128)(2,1)}), bf16[8,4,8,1024]{3,2,1,0:T(8,128)(2,1)S(1)}, u32[]{:S(2)}, u32[]{:S(2)}) async-start(bf16[8,4,8,1024]{3,2,1,0:T(8,128)(2,1)} %shard_map.85), calls=%async_computation.1 | async-start | bytes 1048576 | tf_op jit(solution)/shard_map/all_to_all | solution.py:354
  109.8 1.4 copy-start.18
  119.5 7.2 %copy-start.3 = (bf16[256,3072]{1,0:T(8,128)(2,1)}, bf16[256,3072]{1,0:T(8,128)(2,1)S(1)}, u32[]{:S(2)}) copy-start(bf16[256,3072]{1,0:T(8,128)(2,1)S(1)} %get-tuple-element.20.proj_ref.grad_ref) | copy-start | bytes 4718596
  119.5 22.7 %collective-permute-start.1 = (bf16[256,1536]{1,0:T(8,128)(2,1)}, bf16[256,1536]{1,0:T(8,128)(2,1)S(1)}, u32[]{:S(2)}, u32[]{:S(2)}) collective-permute-start(bf16[256,1536]{1,0:T(8,128)(2,1)} %get-tuple-element.23), channel_id=1, source_target_pairs={{0,1},{1,0},{2,3},{3,2},{4,5},{5,4},{6,7},{7,6},{8,9},{9,8},{10,11... | collective-permute-start | bytes 2359304 | tf_op jit(solution)/shard_map/ppermute | solution.py:377
  119.5 21.8 %collective-permute-start = (bf16[256,1024]{1,0:T(8,128)(2,1)S(1)}, bf16[256,1024]{1,0:T(8,128)(2,1)S(1)}, u32[]{:S(2)}, u32[]{:S(2)}) collective-permute-start(bf16[256,1024]{1,0:T(8,128)(2,1)S(1)} %copy-done.11), channel_id=1, source_target_pairs={{0,1},{1,0},{2,3},{3,2},{4,5},{5,4},{6,7},{7,6},{8,9},{9,8},{10,11... | collective-permute-start | bytes 1572872 | tf_op jit(solution)/shard_map/ppermute | solution.py:362
  120.0 2.8 %copy-start.2 = (bf16[1024,3072]{1,0:T(8,128)(2,1)S(1)}, bf16[1024,3072]{1,0:T(8,128)(2,1)}, u32[]{:S(2)}) copy-start(bf16[1024,3072]{1,0:T(8,128)(2,1)} %w_ref.3) | copy-start | bytes 18874372
  136.4 16.2 %all-to-all-start.10 = ((f32[32,1,1024]{2,1,0:T(1,128)}), f32[32,1,1024]{2,1,0:T(1,128)S(1)}, u32[]{:S(2)}, u32[]{:S(2)}) async-start(f32[32,1,1024]{2,1,0:T(1,128)} %broadcast_in_dim.54), calls=%async_computation.10 | async-start | bytes 262144 | tf_op jit(solution)/shard_map/all_to_all | solution.py:339
  142.2 0.9 copy-start.5
  143.0 1.4 copy-start.4
  144.4 1.1 copy-start.6
  145.6 1.0 copy-start.12
  146.6 1.0 copy-start.14
  196.4 18.8 %all-to-all-start.6 = ((bf16[8,4,8,1024]{3,2,1,0:T(8,128)(2,1)}), bf16[8,4,8,1024]{3,2,1,0:T(8,128)(2,1)S(1)}, u32[]{:S(2)}, u32[]{:S(2)}) async-start(bf16[8,4,8,1024]{3,2,1,0:T(8,128)(2,1)} %bitcast.27), calls=%async_computation.6 | async-start | bytes 1048576 | tf_op jit(solution)/shard_map/all_to_all | solution.py:397
  215.2 17.0 %all-to-all-start.8 = ((bf16[8,32,384]{2,1,0:T(8,128)(2,1)}), bf16[8,32,384]{2,1,0:T(8,128)(2,1)S(1)}, u32[]{:S(2)}, u32[]{:S(2)}) async-start(bf16[8,32,384]{2,1,0:T(8,128)(2,1)} %bitcast.12), calls=%async_computation.8 | async-start | bytes 393216 | tf_op jit(solution)/shard_map/all_to_all | solution.py:393
  (3 other events, 2.3 us)

commit v2 on v1

v2 whole, which is shorter than its diff:
```python
import jax
import jax.numpy as jnp
from jax import lax
from jax.experimental import pallas as pl
from jax.experimental.pallas import tpu as pltpu
from jax.sharding import PartitionSpec as P

HEADS = 16
EPSILON = 1e-05
F32 = jnp.float32
BF16 = jnp.bfloat16
MIB = 1 << 20
NT = (((1,), (1,)), ((), ()))
TN = (((0,), (0,)), ((), ()))


def dot(a, b, dims=(((1,), (0,)), ((), ())), precision=None):
    return lax.dot_general(a, b, dims, precision=precision, preferred_element_type=F32)


def standardize(inputs):
    center = inputs - jnp.mean(inputs, axis=-1, keepdims=True)
    spread = lax.rsqrt(jnp.mean(center * center, axis=-1, keepdims=True) + EPSILON)
    return center * spread, spread


def far(array):
    return pltpu.with_memory_space_constraint(array, pltpu.HBM)


VMEM = pl.BlockSpec(memory_space=pltpu.VMEM)
SMEM = pl.BlockSpec(memory_space=pltpu.SMEM)
HBM = pl.BlockSpec(memory_space=pltpu.HBM)


def params(mib):
    return pltpu.CompilerParams(vmem_limit_bytes=mib * MIB)


def cost(flops, moved, exps=0):
    return pl.CostEstimate(flops=flops, bytes_accessed=moved, transcendentals=exps)


def pack_kernel(source, packed):
    size = packed.shape[2]
    for group in range(packed.shape[0]):
        packed[group] = source[:, group * size : (group + 1) * size, :]


def select_kernel(index_ref, source, own, other, arrived):
    copies = [
        pltpu.make_async_copy(source.at[:, index_ref[0]], own, arrived.at[0]),
        pltpu.make_async_copy(source.at[:, index_ref[0] ^ 1], other, arrived.at[1]),
    ]
    for copy in copies:
        copy.start()
    for copy in copies:
        copy.wait()


def pack(array, groups):
    frames, patches, width = array.shape
    shape = (groups, frames, patches // groups, width)
    return pl.pallas_call(
        pack_kernel,
        out_shape=jax.ShapeDtypeStruct(shape, array.dtype),
        compiler_params=params(8),
        cost_estimate=cost(0, 4 * array.size),
    )(array)


def select(index, array):
    shape = jax.ShapeDtypeStruct(array.shape[:1] + array.shape[2:], array.dtype)
    return pl.pallas_call(
        select_kernel,
        in_specs=[SMEM, HBM],
        out_specs=[VMEM, VMEM],
        out_shape=(shape, shape),
        scratch_shapes=[pltpu.SemaphoreType.DMA((2,))],
        compiler_params=params(8),
        cost_estimate=cost(0, 4 * shape.size),
    )(index, far(array))


def merge_kernel(core_ref, own, other, out):
    out[:, core_ref[0]] = own[...]
    out[:, 1 - core_ref[0]] = other[...]


def merge(core, own, other):
    shape = jax.ShapeDtypeStruct(own.shape[:1] + (2,) + own.shape[1:], own.dtype)
    return pl.pallas_call(
        merge_kernel,
        in_specs=[SMEM, VMEM, VMEM],
        out_shape=shape,
        compiler_params=params(8),
        cost_estimate=cost(0, 4 * shape.size),
    )(core, own, other)


def place_kernel(core_ref, own, other, target):
    for group in range(own.shape[0]):
        target[:, group, core_ref[0]] = own[group]
        target[:, group, 1 - core_ref[0]] = other[group]


def place(core, own, other):
    chips, frames, size, width = own.shape
    placed = pl.pallas_call(
        place_kernel,
        in_specs=[SMEM, VMEM, VMEM],
        out_shape=jax.ShapeDtypeStruct((frames, chips, 2, size, width), own.dtype),
        compiler_params=params(8),
        cost_estimate=cost(0, 8 * own.size),
    )(core, own, other)
    return placed.reshape(frames, chips * 2 * size, width)


def row_tiles(row):
    tile = row.shape[1] // 8
    return jnp.concatenate([row[:, i * tile : (i + 1) * tile] for i in range(8)], axis=0)


def tiles_row(tiles):
    return jnp.concatenate([tiles[i : i + 1] for i in range(tiles.shape[0])], axis=1)


def lane_halves(slab):
    lane = lax.broadcasted_iota(jnp.int32, slab.shape, 1)
    low = lane < slab.shape[1] // 2
    zero = jnp.zeros_like(slab)
    return jnp.where(low, slab, zero), jnp.where(low, zero, slab)


def same_patch(rows, patches):
    first = lax.broadcasted_iota(jnp.int32, (rows, rows), 0)
    second = lax.broadcasted_iota(jnp.int32, (rows, rows), 1)
    return lax.rem(first, patches) == lax.rem(second, patches)


def softmax(query, keys, scale, mask):
    scores = jnp.where(mask, dot(query, keys, NT) * scale, -jnp.inf)
    weights = jnp.exp(scores - jnp.max(scores, axis=-1, keepdims=True))
    return weights / jnp.sum(weights, axis=-1, keepdims=True)


def forward_kernel(
    patches,
    x_ref,
    gain_ref,
    w_hbm,
    normed_hbm,
    proj_hbm,
    pool_ref,
    w_ref,
    normed_ref,
    proj_ref,
    total,
    arrived,
    sent,
):
    rows, width = x_ref.shape
    parts = arrived.shape[0]
    chunk = w_ref.shape[1] // parts
    chunks = [pl.ds(part * chunk, chunk) for part in range(parts)]
    loads = [
        pltpu.make_async_copy(w_hbm.at[:, cols], w_ref.at[:, cols], arrived.at[part])
        for part, cols in enumerate(chunks)
    ]
    for load in loads:
        load.start()
    inputs = x_ref[...].astype(F32)
    standard, _ = standardize(inputs)
    normed = (standard * gain_ref[...]).astype(BF16)
    normed_ref[...] = normed
    stores = [pltpu.make_async_copy(normed_ref, normed_hbm, sent.at[parts])]
    stores[-1].start()
    total[...] = jnp.sum(inputs, axis=0, keepdims=True)
    for part, cols in enumerate(chunks):
        loads[part].wait()
        proj_ref[:, cols] = dot(normed, w_ref[:, cols]).astype(BF16)
        stores.append(
            pltpu.make_async_copy(proj_ref.at[:, cols], proj_hbm.at[:, cols], sent.at[part])
        )
        stores[-1].start()
    mask = same_patch(rows, patches)
    slab = 2 * width // HEADS
    scale = (width // HEADS) ** -0.5
    for pair in range(HEADS // 2):
        at = pair * slab
        query = proj_ref[:, at : at + slab]
        keys = proj_ref[:, width + at : width + at + slab]
        values = proj_ref[:, 2 * width + at : 2 * width + at + slab]
        probs = [softmax(part, keys, scale, mask).astype(BF16) for part in lane_halves(query)]
        attended = dot(jnp.concatenate(probs, 1), jnp.concatenate(lane_halves(values), 0))
        attended = attended.astype(BF16).astype(F32)
        total[:, at : at + slab] += jnp.sum(attended, axis=0, keepdims=True)
    tiles = row_tiles(total[...])
    for copy in range(pool_ref.shape[0]):
        pool_ref[copy] = tiles
    for store in stores:
        store.wait()


def forward(tokens, gain, w_project, patches, copies):
    rows, width = tokens.shape
    parts = 6
    return pl.pallas_call(
        lambda *refs: forward_kernel(patches, *refs),
        in_specs=[VMEM, VMEM, HBM],
        out_specs=[HBM, HBM, VMEM],
        out_shape=(
            jax.ShapeDtypeStruct((rows, width), BF16),
            jax.ShapeDtypeStruct((rows, 3 * width), BF16),
            jax.ShapeDtypeStruct((copies, 8, width // 8), F32),
        ),
        scratch_shapes=[
            pltpu.VMEM(w_project.shape, BF16),
            pltpu.VMEM((rows, width), BF16),
            pltpu.VMEM((rows, 3 * width), BF16),
            pltpu.VMEM((1, width), F32),
            pltpu.SemaphoreType.DMA((parts,)),
            pltpu.SemaphoreType.DMA((parts + 1,)),
        ],
        compiler_params=params(56),
        cost_estimate=cost(10 * rows * width * width, 10 * MIB, HEADS * rows * rows),
    )(tokens, gain, far(w_project))


def flip_kernel(normed_ref, other_ref, w_ref, flipped, w_flipped):
    rows, width = normed_ref.shape
    flipped[:, :rows] = normed_ref[...].T
    flipped[:, rows:] = other_ref[...].T
    for part in range(w_ref.shape[1] // rows):
        w_flipped[part * rows : (part + 1) * rows] = w_ref[:, part * rows : (part + 1) * rows].T


def flip(normed, other_normed, w_project):
    rows, width = normed.shape
    return pl.pallas_call(
        flip_kernel,
        in_specs=[VMEM] * 3,
        out_shape=(
            jax.ShapeDtypeStruct((width, 2 * rows), BF16),
            jax.ShapeDtypeStruct((3 * width, width), BF16),
        ),
        compiler_params=params(56),
        cost_estimate=cost(0, 14 * MIB),
    )(normed, other_normed, w_project)


def attend_kernel(patches, proj_ref, rounded, norm):
    rows = proj_ref.shape[0]
    width = proj_ref.shape[1] // 3
    mask = same_patch(rows, patches)
    slab = 2 * width // HEADS
    scale = (width // HEADS) ** -0.5
    for pair in range(HEADS // 2):
        at = pair * slab
        query = proj_ref[:, at : at + slab]
        keys = proj_ref[:, width + at : width + at + slab]
        for half, part in enumerate(lane_halves(keys)):
            head = 2 * pair + half
            scores = jnp.where(mask, dot(part, query, NT) * scale, -jnp.inf)
            weights = jnp.exp(scores - jnp.max(scores, axis=0, keepdims=True))
            probs = (weights / jnp.sum(weights, axis=0, keepdims=True)).astype(BF16)
            rounded[head] = probs
            norm[head : head + 1] = 1.0 / jnp.sum(probs.astype(F32), axis=0, keepdims=True)


def attend(projected, patches):
    rows = projected.shape[0]
    return pl.pallas_call(
        lambda *refs: attend_kernel(patches, *refs),
        in_specs=[VMEM],
        out_shape=(
            jax.ShapeDtypeStruct((HEADS, rows, rows), BF16),
            jax.ShapeDtypeStruct((HEADS, rows), F32),
        ),
        compiler_params=params(56),
        cost_estimate=cost(rows * rows * projected.shape[1], 6 * MIB, HEADS * rows * rows),
    )(projected)


def total_share(parts_ref, count):
    return tiles_row(jnp.sum(parts_ref[...], axis=0)) / count


def value_kernel(
    block, count, core_ref, grad_ref, parts_ref, rounded_hbm, out_ref, keep_ref, send_ref, rounded, arrived
):
    rows, width = grad_ref.shape
    loads = []
    for pair in range(HEADS // 2):
        part = pl.ds(2 * pair, 2)
        loads.append(
            pltpu.make_async_copy(rounded_hbm.at[part], rounded.at[part], arrived.at[pair])
        )
        loads[-1].start()
    share = total_share(parts_ref, count)
    slab = 2 * width // HEADS
    first = width - 2 * block
    for pair in range(HEADS // 2):
        at = pair * slab
        grads = (grad_ref[:, at : at + slab].astype(F32) + share[:, at : at + slab]).astype(BF16)
        loads[pair].wait()
        probs = jnp.concatenate([rounded[2 * pair], rounded[2 * pair + 1]], 1)
        value_grad = dot(probs, jnp.concatenate(lane_halves(grads), 0)).astype(BF16)
        out_ref[:, at : at + slab] = value_grad
        if at >= first:
            owner, place = divmod(at - first, block)

            @pl.when(core_ref[0] == owner)
            def _():
                keep_ref[:, place : place + slab] = value_grad

            @pl.when(core_ref[0] != owner)
            def _():
                send_ref[:, place : place + slab] = value_grad


def value_grads(core, grads, share_parts, rounded, block, count):
    rows, width = grads.shape
    part = jax.ShapeDtypeStruct((rows, block), BF16)
    return pl.pallas_call(
        lambda *refs: value_kernel(block, count, *refs),
        in_specs=[SMEM, VMEM, VMEM, HBM],
        out_shape=(jax.ShapeDtypeStruct((rows, width), BF16), part, part),
        scratch_shapes=[
            pltpu.VMEM(rounded.shape, BF16),
            pltpu.SemaphoreType.DMA((HEADS // 2,)),
        ],
        compiler_params=params(56),
        cost_estimate=cost(4 * rows * rows * width, 4 * MIB),
    )(core, grads, share_parts, far(rounded))


def backward_kernel(
    block,
    count,
    core_ref,
    x_ref,
    proj_ref,
    grad_ref,
    parts_ref,
    rounded_hbm,
    norm_ref,
    value_ref,
    gain_ref,
    w_hbm,
    keep_ref,
    send_ref,
    token_ref,
    gain_out,
    proj_grad,
    rounded,
    w_ref,
    arrived,
):
    rows, width = grad_ref.shape
    loads = []
    for pair in range(HEADS // 2):
        part = pl.ds(2 * pair, 2)
        loads.append(
            pltpu.make_async_copy(rounded_hbm.at[part], rounded.at[part], arrived.at[pair])
        )
        loads[-1].start()
    w_load = pltpu.make_async_copy(w_hbm, w_ref, arrived.at[HEADS // 2])
    w_load.start()
    share = total_share(parts_ref, count)
    slab = 2 * width // HEADS
    scale = (width // HEADS) ** -0.5

    def hand_on(start, part):
        number, inside = divmod(start, block)
        owner, place = number % 2, number // 2 * block + inside

        @pl.when(core_ref[0] == owner)
        def _():
            keep_ref[:, place : place + slab] = part

        @pl.when(core_ref[0] != owner)
        def _():
            send_ref[:, place : place + slab] = part

    for pair in range(HEADS // 2):
        at = pair * slab
        query = proj_ref[:, at : at + slab]
        keys = proj_ref[:, width + at : width + at + slab]
        values = proj_ref[:, 2 * width + at : 2 * width + at + slab]
        grads = (grad_ref[:, at : at + slab].astype(F32) + share[:, at : at + slab]).astype(BF16)
        score_grads = []
        loads[pair].wait()
        for half, part in enumerate(lane_halves(values)):
            head = 2 * pair + half
            probs = rounded[head].astype(F32)
            prob_grad = dot(part, grads, NT)
            mean = jnp.sum(probs * prob_grad, axis=0, keepdims=True) * norm_ref[head : head + 1]
            score_grads.append((probs * (prob_grad - mean) * scale).astype(BF16))
        both = jnp.concatenate(lane_halves(query), 0)
        key_grad = dot(jnp.concatenate(score_grads, 1), both).astype(BF16)
        both = jnp.concatenate(lane_halves(keys), 0)
        query_grad = dot(jnp.concatenate(score_grads, 0), both, TN).astype(BF16)
        proj_grad[:, at : at + slab] = query_grad
        proj_grad[:, width + at : width + at + slab] = key_grad
        hand_on(at, query_grad)
        hand_on(width + at, key_grad)
        if at < width - 2 * block:
            hand_on(2 * width + at, value_ref[:, at : at + slab])

    w_load.wait()
    normed_grad = dot(proj_grad[...], w_ref[: 2 * width]) + dot(value_ref[...], w_ref[2 * width :])
    standard, spread = standardize(x_ref[...].astype(F32))
    gain_out[...] = row_tiles(jnp.sum(normed_grad * standard, axis=0, keepdims=True))
    scaled = normed_grad * gain_ref[...]
    centered = (
        scaled
        - jnp.mean(scaled, axis=-1, keepdims=True)
        - standard * jnp.mean(scaled * standard, axis=-1, keepdims=True)
    )
    total_grad = grad_ref[...].astype(F32) + share
    token_ref[...] = (total_grad + spread * centered).astype(BF16)


def backward(
    core, tokens, projected, grads, share_parts, rounded, norm, value_grad, gain, w_flipped, block, count
):
    rows, width = grads.shape
    half = jax.ShapeDtypeStruct((rows, (3 * width - 2 * block) // 2), BF16)
    return pl.pallas_call(
        lambda *refs: backward_kernel(block, count, *refs),
        in_specs=[SMEM] + [VMEM] * 4 + [HBM] + [VMEM] * 3 + [HBM],
        out_shape=(
            half,
            half,
            jax.ShapeDtypeStruct((rows, width), BF16),
            jax.ShapeDtypeStruct((8, width // 8), F32),
        ),
        scratch_shapes=[
            pltpu.VMEM((rows, 2 * width), BF16),
            pltpu.VMEM(rounded.shape, BF16),
            pltpu.VMEM(w_flipped.shape, BF16),
            pltpu.SemaphoreType.DMA((HEADS // 2 + 1,)),
        ],
        compiler_params=params(56),
        cost_estimate=cost(14 * rows * rows * width, 12 * MIB),
    )(
        core,
        tokens,
        projected,
        grads,
        share_parts,
        far(rounded),
        norm,
        value_grad,
        gain,
        far(w_flipped),
    )


def split_sum(tiles):
    high = tiles.astype(BF16).astype(F32)
    return jnp.concatenate([high, tiles - high], axis=0).astype(BF16)


def weight_kernel(halves, flipped, grad_ref, other_grad_ref, *refs):
    *gain_refs, out_hbm, staged, sent = refs
    groups, _, lanes = out_hbm.shape
    steps = sent.shape[0] - 1
    cols = grad_ref.shape[1] // steps
    tiles = cols // lanes
    block = flipped.shape[0] // (groups * halves)
    span = tiles * halves * block
    copies = []
    for step in range(steps):
        at = pl.ds(step * cols, cols)
        both = jnp.concatenate([grad_ref[:, at], other_grad_ref[:, at]], axis=0)
        terms = dot(flipped[...], both).astype(BF16)
        for tile in range(tiles):
            for half in range(halves):
                for group in range(groups):
                    start = (half * groups + group) * block
                    place = step * span + (tile * halves + half) * block
                    staged[group, place : place + block] = terms[
                        start : start + block, tile * lanes : (tile + 1) * lanes
                    ]
        part = pl.ds(step * span, span)
        copies.append(
            pltpu.make_async_copy(staged.at[:, part], out_hbm.at[:, part], sent.at[step])
        )
        copies[-1].start()
    if gain_refs:
        gains = split_sum(gain_refs[0][...] + gain_refs[1][...])
        for group in range(groups):
            staged[group, steps * span :] = gains
        part = pl.ds(steps * span, 16)
        copies.append(
            pltpu.make_async_copy(staged.at[:, part], out_hbm.at[:, part], sent.at[steps])
        )
        copies[-1].start()
    for copy in copies:
        copy.wait()


def weight_terms(flipped, grads, other_grads, gains, groups, halves, steps):
    width, rows = flipped.shape
    lanes = 128
    extra = 16 if gains else 0
    shape = (groups, width // groups * grads.shape[1] // lanes + extra, lanes)
    return pl.pallas_call(
        lambda *refs: weight_kernel(halves, *refs),
        in_specs=[VMEM] * (3 + len(gains)),
        out_specs=HBM,
        out_shape=jax.ShapeDtypeStruct(shape, BF16),
        scratch_shapes=[pltpu.VMEM(shape, BF16), pltpu.SemaphoreType.DMA((steps + 1,))],
        compiler_params=params(24),
        cost_estimate=cost(2 * rows * width * grads.shape[1], 6 * MIB),
    )(flipped, grads, other_grads, *gains)


def regroup_kernel(block, terms_ref, last_ref, out_ref):
    halves, steps, rows, _ = out_ref.shape
    tiles = (rows - 16) // block
    total = jnp.sum(terms_ref[...].astype(F32), axis=0)
    last = jnp.sum(last_ref[...].astype(F32), axis=0).astype(BF16)
    terms = total.astype(BF16)
    end = total.shape[0] - 16
    gains = split_sum(total[end : end + 8] + total[end + 8 :])
    for half in range(halves):
        for step in range(steps):
            source, first = (terms, step * tiles) if step < steps - 1 else (last, 0)
            for tile in range(tiles):
                start = ((first + tile) * halves + half) * block
                out_ref[half, step, tile * block : (tile + 1) * block] = source[
                    start : start + block
                ]
            out_ref[half, step, tiles * block :] = gains


def regroup(terms, last, halves, steps, block):
    lanes = terms.shape[2]
    shape = (halves, steps, last.shape[1] // halves + 16, lanes)
    return pl.pallas_call(
        lambda *refs: regroup_kernel(block, *refs),
        in_specs=[VMEM, VMEM],
        out_shape=jax.ShapeDtypeStruct(shape, BF16),
        compiler_params=params(32),
        cost_estimate=cost(terms.size, 4 * MIB),
    )(terms, last)


def finish_kernel(terms_ref, out_ref, gain_ref):
    total = jnp.sum(terms_ref[...].astype(F32), axis=0)
    block = out_ref.shape[0]
    lanes = total.shape[1]
    for tile in range(out_ref.shape[1] // lanes):
        out_ref[:, tile * lanes : (tile + 1) * lanes] = total[tile * block : (tile + 1) * block]
    end = total.shape[0] - 16
    gain_ref[...] = tiles_row(total[end : end + 8] + total[end + 8 :])


def finish(terms, block):
    count, rows, lanes = terms.shape
    return pl.pallas_call(
        finish_kernel,
        in_specs=[VMEM],
        out_shape=(
            jax.ShapeDtypeStruct((block, (rows - 16) // block * lanes), F32),
            jax.ShapeDtypeStruct((1, 8 * lanes), F32),
        ),
        compiler_params=params(16),
        cost_estimate=cost(terms.size, MIB),
    )(terms)


def pool_kernel(halves, tokens, parts_ref, out_ref):
    per_clip = parts_ref.shape[0] // halves
    for half in range(halves):
        pooled = jnp.sum(parts_ref[half * per_clip : (half + 1) * per_clip], axis=0) / tokens
        pooled = pooled.astype(BF16).astype(F32)
        for copy in range(out_ref.shape[0]):
            out_ref[copy, half] = pooled


def pool(parts, halves, tokens, copies):
    return pl.pallas_call(
        lambda *refs: pool_kernel(halves, tokens, *refs),
        in_specs=[VMEM],
        out_shape=jax.ShapeDtypeStruct((copies, halves) + parts.shape[1:], F32),
        compiler_params=params(8),
        cost_estimate=cost(parts.size, MIB),
    )(parts)


def embed_kernel(pooled_ref, w_ref, pooled_out, centered_ref, gram_ref, rows_ref):
    groups, halves, tiles, lanes = pooled_ref.shape
    for half in range(halves):
        for tile in range(tiles):
            rows_ref[half * groups : (half + 1) * groups, tile * lanes : (tile + 1) * lanes] = (
                pooled_ref[:, half, tile, :]
            )
    pooled = rows_ref[...].astype(BF16)
    pooled_out[...] = pooled
    embedding = dot(pooled, w_ref[...])
    centered = embedding - jnp.mean(embedding, axis=0, keepdims=True)
    centered_ref[...] = centered
    gram = dot(centered, centered, NT, lax.Precision.HIGHEST)
    size = gram_ref.shape[1]
    gram = [gram[i : i + size] for i in range(0, gram.shape[0], size)]
    gram = jnp.concatenate(gram, axis=1)
    for copy in range(gram_ref.shape[0]):
        gram_ref[copy] = gram


def embed(pooled, w_expand, copies):
    clips = pooled.shape[0] * pooled.shape[1]
    width, columns = w_expand.shape
    return pl.pallas_call(
        embed_kernel,
        in_specs=[VMEM, VMEM],
        out_shape=(
            jax.ShapeDtypeStruct((clips, width), BF16),
            jax.ShapeDtypeStruct((clips, columns), F32),
            jax.ShapeDtypeStruct((copies, min(clips, 8), clips * clips // min(clips, 8)), F32),
        ),
        scratch_shapes=[pltpu.VMEM((clips, width), F32)],
        compiler_params=params(16),
        cost_estimate=cost(2 * clips * w_expand.size, 2 * MIB),
    )(pooled, w_expand)


def embed_grad_kernel(coefficient, own_ref, gram_ref, centered_ref, w_ref, grad_ref, pool_ref):
    clips = centered_ref.shape[0]
    centered = centered_ref[...]
    gram = jnp.sum(gram_ref[...], axis=0)
    gram = [gram[:, i : i + clips] for i in range(0, gram.shape[1], clips)]
    gram = jnp.concatenate(gram, axis=0)
    variances = jnp.sum(centered * centered, axis=0, keepdims=True) / (clips - 1)
    mixed = dot(gram, centered, precision=lax.Precision.HIGHEST)
    grads = coefficient * (mixed / (clips - 1) - centered * variances)
    grad_ref[...] = grads.astype(BF16)
    row = lax.broadcasted_iota(jnp.int32, grads.shape, 0)
    own = jnp.sum(jnp.where(row == own_ref[0], grads, 0.0), axis=0, keepdims=True)
    own = jnp.broadcast_to(own, (16, own.shape[1])).astype(BF16)
    part = row_tiles(dot(own, w_ref[...], NT)[0:1])
    for copy in range(pool_ref.shape[0]):
        pool_ref[copy] = part


def embed_grads(own_index, gram_parts, centered, w_expand, coefficient):
    width = w_expand.shape[0]
    return pl.pallas_call(
        lambda *refs: embed_grad_kernel(coefficient, *refs),
        in_specs=[SMEM, VMEM, VMEM, VMEM],
        out_shape=(
            jax.ShapeDtypeStruct(centered.shape, BF16),
            jax.ShapeDtypeStruct((gram_parts.shape[0], 8, width // 8), F32),
        ),
        compiler_params=params(16),
        cost_estimate=cost(2 * 16 * w_expand.size, 2 * MIB),
    )(own_index, gram_parts, centered, w_expand)


DP = ("zh", "x", "y")
FRAME = ("zl", "core")
SIZES = {"zh": 2, "x": 4, "y": 4, "zl": 4, "core": 2}
SWAP = [(0, 1), (1, 0)]


def to_each(array, axis):
    return lax.all_to_all(array, axis, split_axis=0, concat_axis=0, tiled=True)


def per_device(clip_tokens, out_grad, ln_gain, w_project, w_expand):
    frame_count = lax.axis_size(FRAME)
    clip_count = lax.axis_size(DP)
    halves, steps = lax.axis_size("zh"), lax.axis_size("zl")
    plane = lax.axis_size(("x", "y"))
    core = lax.axis_index("core").reshape(1)
    own_frame = lax.axis_index(FRAME).reshape(1)
    own_clip = lax.axis_index(DP)
    frames_dev, patches, width = clip_tokens.shape[1:]
    patches_dev = patches // frame_count
    rows = frames_dev * patches
    tokens_clip = frames_dev * frame_count * patches
    column_block = 3 * width // frame_count
    block_rows = width // clip_count
    gain = ln_gain[None, :]

    tokens = to_each(pack(clip_tokens[0], frame_count), FRAME).reshape(rows, width)
    out_grad, tokens = lax.optimization_barrier((out_grad, tokens))
    gathered = lax.all_gather(out_grad[0], "zl", axis=0, tiled=True)
    normed, projected, pool_parts = forward(
        tokens, gain, w_project, patches_dev, halves * frame_count
    )
    other_normed = lax.ppermute(normed, "core", SWAP)

    pool_parts = to_each(pool_parts, ("zh",) + FRAME)
    pooled = to_each(pool(pool_parts, halves, tokens_clip, plane), ("x", "y"))
    flipped, w_flipped = flip(normed, other_normed, w_project)
    pooled, flipped, w_flipped = lax.optimization_barrier((pooled, flipped, w_flipped))
    pooled_all, centered, gram_parts = embed(pooled, w_expand, frame_count)
    gram_parts = to_each(gram_parts, FRAME)
    rounded, norm = attend(projected, patches_dev)
    gram_parts, rounded, norm = lax.optimization_barrier((gram_parts, rounded, norm))
    coefficient = 100.0 * tokens_clip / (w_expand.shape[1] * frame_count * (clip_count - 1))
    embed_grad, share_parts = embed_grads(
        own_clip.reshape(1), gram_parts, centered, w_expand, coefficient
    )
    gathered, share_parts = lax.optimization_barrier((gathered, share_parts))
    share_parts = to_each(share_parts, FRAME)
    row_part = lax.dynamic_slice_in_dim(pooled_all, own_clip * block_rows, block_rows, 1)
    expand_grad = dot(row_part, embed_grad, TN)

    own_part, other_part = select(
        own_frame, gathered.reshape(-1, frame_count, patches_dev, width)
    )
    other_part = lax.ppermute(other_part, "core", SWAP)
    grads = merge(
        core,
        own_part.reshape(-1, rows // frame_count, width),
        other_part.reshape(-1, rows // frame_count, width),
    ).reshape(rows, width)

    value_grad, kept, outgoing = value_grads(
        core, grads, share_parts, rounded, column_block, tokens_clip
    )
    incoming = lax.ppermute(outgoing, "core", SWAP)
    last = weight_terms(flipped, kept, incoming, (), plane, halves, 1)
    last = to_each(last, ("x", "y"))
    kept, outgoing, token_part, gain_part = backward(
        core,
        tokens,
        projected,
        grads,
        share_parts,
        rounded,
        norm,
        value_grad,
        gain,
        w_flipped,
        column_block,
        tokens_clip,
    )
    token_parts = lax.all_gather(
        token_part.reshape(frame_count, frames_dev, patches_dev, width), "zl"
    )
    incoming, other_gain = lax.ppermute((outgoing, gain_part), "core", SWAP)
    terms = weight_terms(
        flipped, kept, incoming, (gain_part, other_gain), plane, halves, steps - 1
    )
    last, terms = lax.optimization_barrier((last, terms))
    terms = to_each(terms, ("x", "y"))
    terms = regroup(terms, last, halves, steps, block_rows)
    terms = to_each(terms.reshape((-1,) + terms.shape[2:]), ("zh", "zl"))
    project_grad, gain_grad = finish(terms, block_rows)
    own_part, other_part = select(own_frame, token_parts)
    other_part = lax.ppermute(other_part, "core", SWAP)
    token_grad = place(core, own_part, other_part)[None]
    return (token_grad, project_grad, expand_grad, gain_grad[0])


def solution(mesh):
    split = jax.sharding.Mesh(
        mesh.devices.reshape(tuple(SIZES.values())), tuple(SIZES)
    )
    return jax.shard_map(
        per_device,
        mesh=split,
        in_specs=(
            P(DP, FRAME, None, None),
            P(DP, FRAME, None, None),
            P(),
            P(),
            P(None, FRAME),
        ),
        out_specs=(P(DP, FRAME, None, None), P(DP, FRAME), P(DP, FRAME), P()),
        check_vma=False,
    )
```

time: 234 us -> 192 us (0.82)
  waiting for transfers between devices: 47 us -> 16.1 us
  blocking collectives: 103 us -> 73.4 us
  Pallas kernels: 24.1 us -> 51.5 us
  local copies, waits for them, and re-layouts: 23.6 us -> 6.53 us
  between operations: 0.9 us -> 14.2 us
  other arithmetic: 7.13 us -> 0 us
    all_to_all x6 -> x5, waiting for transfers between devices: 47 us -> 12.7 us  [to_each(): return lax.all_to_all(array, axis, split_axis=0, concat_axis=0, tiled=True)]
    all_to_all x5 -> x3, blocking collectives: 103 us -> 73.4 us  [to_each(): return lax.all_to_all(array, axis, split_axis=0, concat_axis=0, tiled=True)]
    pallas_call x6 -> x15, Pallas kernels: 22.5 us -> 49.9 us  [the longest x1 11.4 us: backward(): pl.pallas_call(lambda *refs: backward_kernel(block, count, *refs), in_spe...]
    unnamed x43 -> x20, local copies, waits for them, and re-layouts: 20.3 us -> 6.53 us
    reduce_sum x7 -> x0, other arithmetic: 4.7 us -> none  [the longest x1 2.35 us: per_device(): terms = jnp.sum(terms.astype(F32), axis=0).astype(BF16)]
    ppermute x1 -> x5, waiting for transfers between devices: 0.01 us -> 3.36 us  [the longest x2 1.71 us: per_device(): incoming, other_gain = lax.ppermute((outgoing, gain_part), 'core', SWAP)]
    broadcast_in_dim x7 -> x0, local copies, waits for them, and re-layouts: 2.67 us -> none  [exchange(): copies = jnp.broadcast_to(array[None], (count,) + array.shape)]
    all_to_all x6 -> x5, starting transfers between devices: 25.4 us -> 26.8 us  [to_each(): return lax.all_to_all(array, axis, split_axis=0, concat_axis=0, tiled=True)]
  transfers between devices with their start and end apart: 8 -> 13, of which waited for: 6 -> 5; matrix products, arithmetic and copies ran while one was open for 2% -> 1% of each run, Pallas kernels for 4% -> 23%
where the time goes in v2:
time: 192 us; the launch traced here: 191 us
  blocking collectives  73.4 us (38%)
  Pallas kernels  51.5 us (27%)
  starting transfers between devices  27.9 us (15%)
  waiting for transfers between devices  16.1 us (8%)
  between operations  14.2 us (7%)
  local copies, waits for them, and re-layouts  6.53 us (3%)
    all_to_all x3, blocking collectives, to_each(): return lax.all_to_all(array, axis, split_axis=0, concat_axis=0, tiled=True)  73.4 us
    all_to_all x5, starting transfers between devices, to_each(): return lax.all_to_all(array, axis, split_axis=0, concat_axis=0, tiled=True)  26.8 us
    all_to_all x5, waiting for transfers between devices, to_each(): return lax.all_to_all(array, axis, split_axis=0, concat_axis=0, tiled=True)  12.7 us
    pallas_call x1, Pallas kernels, backward(): pl.pallas_call(lambda *refs: backward_kernel(block, count, *refs), in_spe...  11.4 us
    pallas_call x1, Pallas kernels, forward(): pl.pallas_call(lambda *refs: forward_kernel(patches, *refs), in_specs=[VM...  8.86 us
    pallas_call x1, Pallas kernels, flip(): pl.pallas_call(flip_kernel, in_specs=[VMEM] * 3, out_shape=(jax.ShapeDtyp...  7.85 us
    unnamed x20, local copies, waits for them, and re-layouts  6.53 us
    pallas_call x1, Pallas kernels, attend(): pl.pallas_call(lambda *refs: attend_kernel(patches, *refs), in_specs=[VME...  5.07 us
  transfers between devices with their start and end apart: 13, of which 5 were waited for; matrix products, arithmetic and copies ran while one was open for 1% of the time, Pallas kernels for 23%

profile of v2, /device:TPU:8, one launch (start us, length us, event | category | flops | bytes accessed | tf_op | source)
XLA Modules:
  0.0 191.2 jit_solution(14314100405237888692)
XLA Ops:
  8.3 21.2 %all_to_all.40 = bf16[8,4,8,1024]{3,2,1,0:T(8,128)(2,1)} all-to-all(bf16[8,4,8,1024]{3,2,1,0:T(8,128)(2,1)S(1)} %shard_map.84), channel_id=1, replica_groups=mesh['zh'=2,'x'=4,'y'=4,'zl'=4,'core'=2] {'zl','core'}, dimensions={0} | all-to-all | bytes 1048576 | tf_op jit(solution)/shard_map/all_to_all | solution.py:671
  29.5 8.9 %shard_map.85 = (bf16[256,1024]{1,0:T(8,128)(2,1)}, bf16[256,3072]{1,0:T(8,128)(2,1)}, f32[16,8,128]{2,1,0:T(8,128)}) custom-call(bf16[256,1024]{1,0:T(8,128)(2,1)} %bitcast.22, f32[1,1024]{1,0:T(1,128)} %bitcast.28, bf16[1024,3072]{1,0:T(8,128)(2,1)} %w_ref.2), custom_call_target="tpu_custom_call" | custom-call | flops 2684354560 | bytes 10485760 | tf_op jit(solution)/shard_map/pallas_call | solution.py:208
  38.4 14.9 %all_to_all.41.refs_0_ = f32[16,8,128]{2,1,0:T(8,128)S(1)} all-to-all(f32[16,8,128]{2,1,0:T(8,128)} %get-tuple-element.44), channel_id=1, replica_groups=mesh['zh'=2,'x'=4,'y'=4,'zl'=4,'core'=2] {'zh','zl','core'}, dimensions={0} | all-to-all | bytes 131072 | tf_op jit(solution)/shard_map/all_to_all | solution.py:671
  54.0 7.4 %all-to-all-start.2 = ((f32[16,2,8,128]{3,2,1,0:T(8,128)}), f32[16,2,8,128]{3,2,1,0:T(8,128)S(1)}, u32[]{:S(2)}, u32[]{:S(2)}) async-start(f32[16,2,8,128]{3,2,1,0:T(8,128)} %shard_map.86), calls=%async_computation.2 | async-start | bytes 262144 | tf_op jit(solution)/shard_map/all_to_all | solution.py:671
  62.2 7.8 %shard_map.87 = (bf16[1024,512]{1,0:T(8,128)(2,1)}, bf16[3072,1024]{1,0:T(8,128)(2,1)}) custom-call(bf16[256,1024]{1,0:T(8,128)(2,1)} %get-tuple-element.45.normed_ref, bf16[256,1024]{1,0:T(8,128)(2,1)} %copy-done.8, bf16[1024,3072]{1,0:T(8,128)(2,1)} %w_ref.2), custom_call_target="tpu_custom_call" | custom-call | bytes 14680064 | tf_op jit(solution)/shard_map/pallas_call | solution.py:240
  70.1 1.4 shard_map.88
  72.1 3.3 %all-to-all-start.3 = ((f32[8,8,128]{2,1,0:T(8,128)}), f32[8,8,128]{2,1,0:T(8,128)S(1)}, u32[]{:S(2)}, u32[]{:S(2)}) async-start(f32[8,8,128]{2,1,0:T(8,128)} %get-tuple-element.49), calls=%async_computation.3 | async-start | bytes 65536 | tf_op jit(solution)/shard_map/all_to_all | solution.py:671
  75.5 5.1 %shard_map.89 = (bf16[16,256,256]{2,1,0:T(8,128)(2,1)}, f32[16,256]{1,0:T(8,128)}) custom-call(bf16[256,3072]{1,0:T(8,128)(2,1)} %get-tuple-element.42.refs_0_.refs_2_), custom_call_target="tpu_custom_call" | custom-call | flops 201326592 | bytes 6291456 | tf_op jit(solution)/shard_map/pallas_call | solution.py:273
  80.5 1.3 all-to-all-done.3.refs_1_
  81.8 1.5 shard_map.90
  84.4 4.2 %all-to-all-start.4 = ((f32[8,8,128]{2,1,0:T(8,128)}), f32[8,8,128]{2,1,0:T(8,128)S(1)}, u32[]{:S(2)}, u32[]{:S(2)}) async-start(f32[8,8,128]{2,1,0:T(8,128)} %get-tuple-element.58), calls=%async_computation.4 | async-start | bytes 65536 | tf_op jit(solution)/shard_map/all_to_all | solution.py:671
  89.5 4.9 %all-to-all-done.4.refs_2_.refs_4_ = f32[8,8,128]{2,1,0:T(8,128)S(1)} async-done(((f32[8,8,128]{2,1,0:T(8,128)}), f32[8,8,128]{2,1,0:T(8,128)S(1)}, u32[]{:S(2)}, u32[]{:S(2)}) %all-to-all-start.4) | async-done | bytes 32800 | tf_op jit(solution)/shard_map/all_to_all | solution.py:671
  95.0 4.9 %shard_map.93 = (bf16[256,1024]{1,0:T(8,128)(2,1)}, bf16[256,384]{1,0:T(8,128)(2,1)}, bf16[256,384]{1,0:T(8,128)(2,1)}) custom-call(s32[1]{0:T(128)} %bitcast.core_ref.refs_0_, bf16[256,1024]{1,0:T(8,128)(2,1)} %bitcast.17, f32[8,8,128]{2,1,0:T(8,128)} %copy-done.9, bf16[16,256,256]{2,1,0:T(8,128)(2,1)} %get-tuple-element.59.refs_3_.refs_5_), custom_call_target="tpu_custom_call" | custom-call | flops 268435456 | bytes 4194304 | tf_op jit(solution)/shard_map/pallas_call | solution.py:325
  100.0 1.6 collective-permute-done.3.refs_2_
  102.6 1.6 shard_map.97
  104.2 7.2 %all-to-all-start.5 = ((bf16[16,192,128]{2,1,0:T(8,128)(2,1)}), bf16[16,192,128]{2,1,0:T(8,128)(2,1)}, u32[]{:S(2)}, u32[]{:S(2)}) async-start(bf16[16,192,128]{2,1,0:T(8,128)(2,1)} %shard_map.97), calls=%async_computation.5 | async-start | bytes 1572864 | tf_op jit(solution)/shard_map/all_to_all | solution.py:671
  111.5 11.4 %shard_map.94 = (bf16[256,1152]{1,0:T(8,128)(2,1)}, bf16[256,1152]{1,0:T(8,128)(2,1)}, bf16[256,1024]{1,0:T(8,128)(2,1)}, f32[8,128]{1,0:T(8,128)}) custom-call(s32[1]{0:T(128)} %bitcast.core_ref.refs_0_, bf16[256,1024]{1,0:T(8,128)(2,1)} %bitcast.23, bf16[256,3072]{1,0:T(8,128)(2,1)} %get-tuple-element.42.refs_0_.refs_2_, bf16[256,1024]{1,0:T(8,128)(2,1)} %bitcast.18, ...), custom_call_target="tpu_custom_call" | custom-call | flops 939524096 | bytes 12582912 | tf_op jit(solution)/shard_map/pallas_call | solution.py:430
  123.5 1.7 collective-permute-done.5.refs_4_
  127.0 2.3 %shard_map.98 = bf16[16,592,128]{2,1,0:T(8,128)(2,1)S(1)} custom-call(bf16[1024,512]{1,0:T(8,128)(2,1)S(1)} %copy-done.2, bf16[256,1152]{1,0:T(8,128)(2,1)S(1)} %copy-done.3, bf16[256,1152]{1,0:T(8,128)(2,1)S(1)} %collective-permute-done.4.refs_2_, f32[8,128]{1,0:T(8,128)S(1)} %copy-done.6, f32[8,128]{1,0:T(8,128)S(1)} %collective-permute-done.5.refs_4_), custom_call_target="tpu_custom_call" | custom-call | flops 1207959552 | bytes 6291456 | tf_op jit(solution)/shard_map/pallas_call | solution.py:510
  129.3 37.4 %all_to_all.42.refs_0_ = bf16[16,592,128]{2,1,0:T(8,128)(2,1)S(1)} all-to-all(bf16[16,592,128]{2,1,0:T(8,128)(2,1)S(1)} %shard_map.98), channel_id=1, replica_groups=mesh['zh'=2,'x'=4,'y'=4,'zl'=4,'core'=2] {'x','y'}, dimensions={0} | all-to-all | bytes 4849664 | tf_op jit(solution)/shard_map/all_to_all | solution.py:671
  166.7 2.2 %shard_map.99 = bf16[2,4,112,128]{3,2,1,0:T(8,128)(2,1)} custom-call(bf16[16,592,128]{2,1,0:T(8,128)(2,1)S(1)} %all_to_all.42.refs_0_, bf16[16,192,128]{2,1,0:T(8,128)(2,1)} %all-to-all-done.5.refs_1_), custom_call_target="tpu_custom_call" | custom-call | flops 1212416 | bytes 4194304 | tf_op jit(solution)/shard_map/pallas_call | solution.py:543
  168.9 4.6 %all-to-all-start.7 = ((bf16[8,112,128]{2,1,0:T(8,128)(2,1)}), bf16[8,112,128]{2,1,0:T(8,128)(2,1)S(1)}, u32[]{:S(2)}, u32[]{:S(2)}) async-start(bf16[8,112,128]{2,1,0:T(8,128)(2,1)} %bitcast.14), calls=%async_computation.7 | async-start | bytes 458752 | tf_op jit(solution)/shard_map/all_to_all | solution.py:671
  174.7 1.6 fusion
  177.2 6.5 %all-to-all-done.7.terms_ref = bf16[8,112,128]{2,1,0:T(8,128)(2,1)S(1)} async-done(((bf16[8,112,128]{2,1,0:T(8,128)(2,1)}), bf16[8,112,128]{2,1,0:T(8,128)(2,1)S(1)}, u32[]{:S(2)}, u32[]{:S(2)}) %all-to-all-start.7) | async-done | bytes 229408 | tf_op jit(solution)/shard_map/all_to_all | solution.py:671
  (45 shorter events, 12.0 us)
Async XLA Ops:
  7.2 76.1 %all-gather.6.cloned.1.call-start = ((), (), s32[]{:S(2)}) async-start(), calls=%async_computation.9 | async-start | bytes 2621440 | tf_op jit(solution)/shard_map/all_gather | solution.py:692
  7.2 1.0 copy-start.4
  38.3 23.1 %collective-permute-start = (bf16[256,1024]{1,0:T(8,128)(2,1)}, bf16[256,1024]{1,0:T(8,128)(2,1)S(1)}, u32[]{:S(2)}, u32[]{:S(2)}) collective-permute-start(bf16[256,1024]{1,0:T(8,128)(2,1)} %get-tuple-element.45.normed_ref), channel_id=1, source_target_pairs={{0,1},{1,0},{2,3},{3,2},{4,5},{5,4},{6,7},{7,6},{8,9},{9,8},{10,11... | collective-permute-start | bytes 1572872 | tf_op jit(solution)/shard_map/ppermute | solution.py:696
  54.0 16.1 %all-to-all-start.2 = ((f32[16,2,8,128]{3,2,1,0:T(8,128)}), f32[16,2,8,128]{3,2,1,0:T(8,128)S(1)}, u32[]{:S(2)}, u32[]{:S(2)}) async-start(f32[16,2,8,128]{3,2,1,0:T(8,128)} %shard_map.86), calls=%async_computation.2 | async-start | bytes 262144 | tf_op jit(solution)/shard_map/all_to_all | solution.py:671
  61.4 8.7 %copy-start = (bf16[1024,1024]{1,0:T(8,128)(2,1)S(1)}, bf16[1024,1024]{1,0:T(8,128)(2,1)}, u32[]{:S(2)}) copy-start(bf16[1024,1024]{1,0:T(8,128)(2,1)} %refs_3_.1) | copy-start | bytes 6291460
  61.4 0.8 copy-start.8
  71.5 0.6 copy-start.7
  72.1 9.7 %all-to-all-start.3 = ((f32[8,8,128]{2,1,0:T(8,128)}), f32[8,8,128]{2,1,0:T(8,128)S(1)}, u32[]{:S(2)}, u32[]{:S(2)}) async-start(f32[8,8,128]{2,1,0:T(8,128)} %get-tuple-element.49), calls=%async_computation.3 | async-start | bytes 65536 | tf_op jit(solution)/shard_map/all_to_all | solution.py:671
  84.3 17.3 %copy-start.2 = (bf16[1024,512]{1,0:T(8,128)(2,1)S(1)}, bf16[1024,512]{1,0:T(8,128)(2,1)}, u32[]{:S(2)}) copy-start(bf16[1024,512]{1,0:T(8,128)(2,1)} %get-tuple-element.66.refs_0_) | copy-start | bytes 3145732
  84.3 4.3 %collective-permute-start.1 = (bf16[16,8,1024]{2,1,0:T(8,128)(2,1)S(1)}, bf16[16,8,1024]{2,1,0:T(8,128)(2,1)S(1)}, u32[]{:S(2)}, u32[]{:S(2)}) collective-permute-start(bf16[16,8,1024]{2,1,0:T(8,128)(2,1)S(1)} %get-tuple-element.57), channel_id=1, source_target_pairs={{0,1},{1,0},{2,3},{3,2},{4,5},{5,4},{6,7},{7,6},{8,9},{9,8},{10,11... | collective-permute-start | bytes 786440 | tf_op jit(solution)/shard_map/ppermute | solution.py:718
  84.4 10.0 %all-to-all-start.4 = ((f32[8,8,128]{2,1,0:T(8,128)}), f32[8,8,128]{2,1,0:T(8,128)S(1)}, u32[]{:S(2)}, u32[]{:S(2)}) async-start(f32[8,8,128]{2,1,0:T(8,128)} %get-tuple-element.58), calls=%async_computation.4 | async-start | bytes 65536 | tf_op jit(solution)/shard_map/all_to_all | solution.py:671
  88.7 0.8 copy-start.1
  94.4 0.6 copy-start.9
  99.9 1.7 collective-permute-start.3
  101.6 0.9 copy-start.5
  104.2 25.1 %all-to-all-start.5 = ((bf16[16,192,128]{2,1,0:T(8,128)(2,1)}), bf16[16,192,128]{2,1,0:T(8,128)(2,1)}, u32[]{:S(2)}, u32[]{:S(2)}) async-start(bf16[16,192,128]{2,1,0:T(8,128)(2,1)} %shard_map.97), calls=%async_computation.5 | async-start | bytes 1572864 | tf_op jit(solution)/shard_map/all_to_all | solution.py:671
  111.4 62.1 %all-gather.4.cloned.1.call-start = ((), (), s32[]{:S(2)}) async-start(), calls=%async_computation.8 | async-start | bytes 2621440 | tf_op jit(solution)/shard_map/all_gather | solution.py:745
  122.9 2.3 %collective-permute-start.4 = (bf16[256,1152]{1,0:T(8,128)(2,1)}, bf16[256,1152]{1,0:T(8,128)(2,1)S(1)}, u32[]{:S(2)}, u32[]{:S(2)}) collective-permute-start(bf16[256,1152]{1,0:T(8,128)(2,1)} %get-tuple-element.70), channel_id=1, source_target_pairs={{0,1},{1,0},{2,3},{3,2},{4,5},{5,4},{6,7},{7,6},{8,9},{9,8},{10,11... | collective-permute-start | bytes 1769480 | tf_op jit(solution)/shard_map/ppermute | solution.py:748
  123.0 2.2 %collective-permute-start.5 = (f32[8,128]{1,0:T(8,128)}, f32[8,128]{1,0:T(8,128)S(1)}, u32[]{:S(2)}, u32[]{:S(2)}) collective-permute-start(f32[8,128]{1,0:T(8,128)} %get-tuple-element.71.refs_3_), channel_id=1, source_target_pairs={{0,1},{1,0},{2,3},{3,2},{4,5},{5,4},{6,7},{7,6},{8,9},{9,8},{10,11... | collective-permute-start | bytes 12296 | tf_op jit(solution)/shard_map/ppermute | solution.py:748
  125.2 1.1 copy-start.3
  126.3 0.7 copy-start.6
  168.9 14.7 %all-to-all-start.7 = ((bf16[8,112,128]{2,1,0:T(8,128)(2,1)}), bf16[8,112,128]{2,1,0:T(8,128)(2,1)S(1)}, u32[]{:S(2)}, u32[]{:S(2)}) async-start(bf16[8,112,128]{2,1,0:T(8,128)(2,1)} %bitcast.14), calls=%async_computation.7 | async-start | bytes 458752 | tf_op jit(solution)/shard_map/all_to_all | solution.py:671
  174.6 1.7 collective-permute-start.2
Sparse Core Ops, SparseCore 0:
  29.6 52.2 all-gather.5
  123.0 49.1 all-gather.3

commit v3 on v2

v3 whole, which is shorter than its diff:
```python
import jax
import jax.numpy as jnp
from jax import lax
from jax.experimental import pallas as pl
from jax.experimental.pallas import tpu as pltpu
from jax.sharding import PartitionSpec as P

HEADS = 16
PARTS = 2
EPSILON = 1e-05
F32 = jnp.float32
BF16 = jnp.bfloat16
MIB = 1 << 20
NT = (((1,), (1,)), ((), ()))
TN = (((0,), (0,)), ((), ()))


def dot(a, b, dims=(((1,), (0,)), ((), ())), precision=None):
    return lax.dot_general(a, b, dims, precision=precision, preferred_element_type=F32)


def standardize(inputs):
    center = inputs - jnp.mean(inputs, axis=-1, keepdims=True)
    spread = lax.rsqrt(jnp.mean(center * center, axis=-1, keepdims=True) + EPSILON)
    return center * spread, spread


def far(array):
    return pltpu.with_memory_space_constraint(array, pltpu.HBM)


def far_shape(shape, dtype):
    return pltpu.HBM(shape, dtype)


def near(array):
    return pltpu.with_memory_space_constraint(array, pltpu.VMEM)


def near_shape(shape, dtype):
    return pltpu.VMEM(shape, dtype)


VMEM = pl.BlockSpec(memory_space=pltpu.VMEM)
SMEM = pl.BlockSpec(memory_space=pltpu.SMEM)
HBM = pl.BlockSpec(memory_space=pltpu.HBM)


def params(mib):
    return pltpu.CompilerParams(vmem_limit_bytes=mib * MIB)


def cost(flops, moved, exps=0):
    return pl.CostEstimate(flops=flops, bytes_accessed=moved, transcendentals=exps)


def pack_kernel(source, packed):
    groups, parts, rows, _ = packed.shape
    frames = source.shape[0]
    size = rows // frames
    for group in range(groups):
        for part in range(parts):
            at = (group * parts + part) * size
            pieces = [source[frame, at : at + size].astype(F32) for frame in range(frames)]
            packed[group, part] = jnp.concatenate(pieces, axis=0).astype(BF16)


def pack(array, groups):
    frames, patches, width = array.shape
    rows = frames * patches // (groups * PARTS)
    return pl.pallas_call(
        pack_kernel,
        out_shape=jax.ShapeDtypeStruct((groups, PARTS, rows, width), array.dtype),
        compiler_params=params(8),
        cost_estimate=cost(0, 4 * array.size),
    )(far(array))


def merge_kernel(index_ref, source, out, own, arrived):
    load = pltpu.make_async_copy(source.at[:, index_ref[0]], own, arrived.at[0])
    load.start()
    load.wait()
    parts, owners, rows, _ = out.shape
    frames = own.shape[0] // owners
    size = rows // frames
    for owner in range(owners):
        for part in range(parts):
            pieces = [
                own[owner * frames + frame, part * size : (part + 1) * size].astype(F32)
                for frame in range(frames)
            ]
            out[part, owner] = jnp.concatenate(pieces, axis=0).astype(BF16)


def merge(index, gathered, owners):
    frames, _, size, width = gathered.shape
    rows = frames * size // (owners * PARTS)
    return pl.pallas_call(
        merge_kernel,
        in_specs=[SMEM, HBM],
        out_specs=VMEM,
        out_shape=jax.ShapeDtypeStruct((PARTS, owners, rows, width), BF16),
        scratch_shapes=[pltpu.VMEM((frames, size, width), BF16), pltpu.SemaphoreType.DMA((1,))],
        compiler_params=params(8),
        cost_estimate=cost(0, 4 * frames * size * width),
    )(index, far(gathered))


def place_kernel(index_ref, source, target, own, arrived):
    load = pltpu.make_async_copy(source.at[:, index_ref[0]], own, arrived.at[0])
    load.start()
    load.wait()
    frames = target.shape[0]
    groups, parts, rows, _ = own.shape
    size = rows // frames
    for group in range(groups):
        for frame in range(frames):
            pieces = [
                own[group, part, frame * size : (frame + 1) * size].astype(F32)
                for part in range(parts)
            ]
            target[frame, group] = jnp.concatenate(pieces, axis=0).astype(BF16)


def place(index, gathered, frames):
    groups, _, parts, rows, width = gathered.shape
    size = parts * rows // frames
    placed = pl.pallas_call(
        place_kernel,
        in_specs=[SMEM, HBM],
        out_specs=VMEM,
        out_shape=jax.ShapeDtypeStruct((frames, groups, size, width), BF16),
        scratch_shapes=[
            pltpu.VMEM((groups, parts, rows, width), BF16),
            pltpu.SemaphoreType.DMA((1,)),
        ],
        compiler_params=params(8),
        cost_estimate=cost(0, 4 * groups * parts * rows * width),
    )(index, far(gathered))
    return placed.reshape(frames, groups * size, width)


def row_tiles(row):
    tile = row.shape[1] // 8
    return jnp.concatenate([row[:, i * tile : (i + 1) * tile] for i in range(8)], axis=0)


def tiles_row(tiles):
    return jnp.concatenate([tiles[i : i + 1] for i in range(tiles.shape[0])], axis=1)


def lane_halves(slab):
    lane = lax.broadcasted_iota(jnp.int32, slab.shape, 1)
    low = lane < slab.shape[1] // 2
    zero = jnp.zeros_like(slab)
    return jnp.where(low, slab, zero), jnp.where(low, zero, slab)


def same_patch(rows, columns, patches):
    first = lax.broadcasted_iota(jnp.int32, (rows, columns), 0)
    second = lax.broadcasted_iota(jnp.int32, (rows, columns), 1)
    return lax.rem(first, patches) == lax.rem(second, patches)


def stacked(slab):
    return jnp.concatenate(lane_halves(slab), axis=0)


def side_by_side(array):
    rows = array.shape[0] // 2
    return jnp.concatenate([array[:rows], array[rows:]], axis=1)


def fetch_kernel(source, target, arrived):
    load = pltpu.make_async_copy(source, target, arrived.at[0])
    load.start()
    load.wait()


def fetch(array):
    return pl.pallas_call(
        fetch_kernel,
        in_specs=[HBM],
        out_specs=VMEM,
        out_shape=near_shape(array.shape, array.dtype),
        scratch_shapes=[pltpu.SemaphoreType.DMA((1,))],
        compiler_params=params(4),
        cost_estimate=cost(0, 4 * array.size),
    )(far(array))


def forward_kernel(
    patches,
    x_ref,
    gain_ref,
    w_ref,
    inputs_hbm,
    normed_hbm,
    proj_hbm,
    pool_ref,
    inputs_ref,
    normed_ref,
    proj_ref,
    total,
    sent,
):
    rows, width = normed_ref.shape
    block_rows = rows // PARTS
    parts = sent.shape[0] - 2
    chunk = w_ref.shape[1] // parts
    chunks = [pl.ds(part * chunk, chunk) for part in range(parts)]
    for part in range(PARTS):
        block = x_ref[:, part]
        inputs_ref[part * block_rows : (part + 1) * block_rows] = block.reshape(block_rows, width)
    stores = [pltpu.make_async_copy(inputs_ref, inputs_hbm, sent.at[parts + 1])]
    stores[-1].start()
    inputs = inputs_ref[...].astype(F32)
    standard, _ = standardize(inputs)
    normed = (standard * gain_ref[...]).astype(BF16)
    normed_ref[...] = normed
    stores.append(pltpu.make_async_copy(normed_ref, normed_hbm, sent.at[parts]))
    stores[-1].start()
    total[...] = jnp.sum(inputs, axis=0, keepdims=True)
    for part, cols in enumerate(chunks):
        proj_ref[:, cols] = dot(normed, w_ref[:, cols]).astype(BF16)
        stores.append(
            pltpu.make_async_copy(proj_ref.at[:, cols], proj_hbm.at[:, cols], sent.at[part])
        )
        stores[-1].start()
    mask = same_patch(2 * block_rows, block_rows, patches // PARTS)
    slab = 2 * width // HEADS
    scale = (width // HEADS) ** -0.5
    for pair in range(HEADS // 2):
        at = pair * slab
        for part in range(PARTS):
            own = pl.ds(part * block_rows, block_rows)
            query = proj_ref[own, at : at + slab]
            keys = proj_ref[own, width + at : width + at + slab]
            values = proj_ref[own, 2 * width + at : 2 * width + at + slab]
            scores = jnp.where(mask, dot(stacked(query), keys, NT) * scale, -jnp.inf)
            weights = jnp.exp(scores - jnp.max(scores, axis=1, keepdims=True))
            probs = (weights / jnp.sum(weights, axis=1, keepdims=True)).astype(BF16)
            attended = dot(side_by_side(probs), stacked(values)).astype(BF16).astype(F32)
            total[:, at : at + slab] += jnp.sum(attended, axis=0, keepdims=True)
    tiles = row_tiles(total[...])
    for copy in range(pool_ref.shape[0]):
        pool_ref[copy] = tiles
    for store in stores:
        store.wait()


def forward(tokens, gain, w_project, patches, copies):
    width = tokens.shape[-1]
    rows = tokens.size // width
    parts = 6
    return pl.pallas_call(
        lambda *refs: forward_kernel(patches, *refs),
        in_specs=[VMEM] * 3,
        out_specs=[HBM, HBM, HBM, VMEM],
        out_shape=(
            far_shape((rows, width), BF16),
            far_shape((rows, width), BF16),
            far_shape((rows, 3 * width), BF16),
            jax.ShapeDtypeStruct((copies, 8, width // 8), F32),
        ),
        scratch_shapes=[
            pltpu.VMEM((rows, width), BF16),
            pltpu.VMEM((rows, width), BF16),
            pltpu.VMEM((rows, 3 * width), BF16),
            pltpu.VMEM((1, width), F32),
            pltpu.SemaphoreType.DMA((parts + 2,)),
        ],
        compiler_params=params(32),
        cost_estimate=cost(10 * rows * width * width, 10 * MIB, HEADS * rows * rows),
    )(tokens, gain, near(w_project))


def flip_kernel(*refs):
    *sources, target = refs
    at = 0
    for source in sources:
        rows, width = source.shape
        step = 256
        for start in range(0, width, step):
            target[start : start + step, at : at + rows] = source[:, start : start + step].T
        at += rows


def flip(*arrays):
    shape = (arrays[0].shape[1], sum(a.shape[0] for a in arrays))
    return pl.pallas_call(
        flip_kernel,
        in_specs=[VMEM] * len(arrays),
        out_shape=jax.ShapeDtypeStruct(shape, BF16),
        compiler_params=params(56),
        cost_estimate=cost(0, 4 * shape[0] * shape[1]),
    )(*arrays)


def attend_kernel(patches, proj_ref, rounded, norm):
    rows = rounded.shape[3]
    width = proj_ref.shape[1] // 3
    mask = same_patch(2 * rows, rows, patches // PARTS)
    slab = 2 * width // HEADS
    scale = (width // HEADS) ** -0.5
    for pair in range(HEADS // 2):
        at = pair * slab
        for part in range(PARTS):
            own = pl.ds(part * rows, rows)
            query = proj_ref[own, at : at + slab]
            keys = proj_ref[own, width + at : width + at + slab]
            scores = jnp.where(mask, dot(stacked(keys), query, NT) * scale, -jnp.inf)
            for head in range(2):
                score = scores[head * rows : (head + 1) * rows]
                weights = jnp.exp(score - jnp.max(score, axis=0, keepdims=True))
                probs = (weights / jnp.sum(weights, axis=0, keepdims=True)).astype(BF16)
                rounded[pair, part, head * rows : (head + 1) * rows] = probs
                number = (pair * PARTS + part) * 2 + head
                norm[number : number + 1] = 1.0 / jnp.sum(
                    probs.astype(F32), axis=0, keepdims=True
                )


def attend(projected, patches):
    rows = projected.shape[0] // PARTS
    pairs = HEADS // 2
    return pl.pallas_call(
        lambda *refs: attend_kernel(patches, *refs),
        in_specs=[VMEM],
        out_shape=(
            jax.ShapeDtypeStruct((pairs, PARTS, 2 * rows, rows), BF16),
            jax.ShapeDtypeStruct((HEADS * PARTS, rows), F32),
        ),
        compiler_params=params(56),
        cost_estimate=cost(rows * rows * projected.shape[1], 6 * MIB, HEADS * rows * rows),
    )(projected)


def total_share(parts_ref, count):
    return tiles_row(jnp.sum(parts_ref[...], axis=0)) / count


def backward_kernel(
    block,
    count,
    core_ref,
    x_ref,
    proj_ref,
    grad_ref,
    parts_ref,
    rounded,
    norm_ref,
    gain_ref,
    w_hbm,
    keep_hbm,
    send_hbm,
    token_ref,
    gain_out,
    proj_grad,
    sorted_grad,
    w_ref,
    arrived,
):
    rows, width = grad_ref.shape
    block_rows = rows // PARTS
    w_load = pltpu.make_async_copy(w_hbm, w_ref, arrived.at[0])
    w_load.start()
    share = tiles_row(jnp.sum(parts_ref[...], axis=0)) / count
    slab = 2 * width // HEADS
    scale = (width // HEADS) ** -0.5
    for pair in range(HEADS // 2):
        at = pair * slab
        for part in range(PARTS):
            own = pl.ds(part * block_rows, block_rows)
            query = proj_ref[own, at : at + slab]
            keys = proj_ref[own, width + at : width + at + slab]
            values = proj_ref[own, 2 * width + at : 2 * width + at + slab]
            grads = grad_ref[own, at : at + slab].astype(F32) + share[:, at : at + slab]
            grads = grads.astype(BF16)
            probs = rounded[pair, part]
            prob_grad = dot(stacked(values), grads, NT)
            score_grads = []
            for head in range(2):
                mine = slice(head * block_rows, (head + 1) * block_rows)
                number = (pair * PARTS + part) * 2 + head
                weights = probs[mine].astype(F32)
                moved = prob_grad[mine]
                mean = jnp.sum(weights * moved, axis=0, keepdims=True)
                mean = mean * norm_ref[number : number + 1]
                score_grads.append((weights * (moved - mean) * scale).astype(BF16))
            key_grad = dot(jnp.concatenate(score_grads, 1), stacked(query))
            query_grad = dot(jnp.concatenate(score_grads, 0), stacked(keys), TN)
            value_grad = dot(side_by_side(probs), stacked(grads))
            for first, grad in zip((0, width, 2 * width), (query_grad, key_grad, value_grad)):
                start = first + at
                grad = grad.astype(BF16)
                proj_grad[own, start : start + slab] = grad
                number, inside = divmod(start, block)
                owner, place = number % 2, number // 2 * block + inside
                sorted_grad[core_ref[0] ^ owner, own, place : place + slab] = grad

    stores = [
        pltpu.make_async_copy(sorted_grad.at[number], target, arrived.at[1 + number])
        for number, target in enumerate((keep_hbm, send_hbm))
    ]
    for store in stores:
        store.start()
    w_load.wait()
    normed_grad = dot(proj_grad[...], w_ref[...])
    standard, spread = standardize(x_ref[...].astype(F32))
    gain_out[...] = row_tiles(jnp.sum(normed_grad * standard, axis=0, keepdims=True))
    scaled = normed_grad * gain_ref[...]
    centered = (
        scaled
        - jnp.mean(scaled, axis=-1, keepdims=True)
        - standard * jnp.mean(scaled * standard, axis=-1, keepdims=True)
    )
    total_grad = grad_ref[...].astype(F32) + share
    token_grad = (total_grad + spread * centered).astype(BF16)
    owners, _, size, _ = token_ref.shape
    for part in range(PARTS):
        for owner in range(owners):
            start = part * block_rows + owner * size
            token_ref[owner, part] = token_grad[start : start + size]
    for store in stores:
        store.wait()


def backward(
    core, tokens, projected, grads, share_parts, rounded, norm, gain, w_flipped, block, count, owners
):
    rows, width = grads.shape
    half = jax.ShapeDtypeStruct((rows, 3 * width // 2), BF16)
    return pl.pallas_call(
        lambda *refs: backward_kernel(block, count, *refs),
        in_specs=[SMEM] + [VMEM] * 7 + [HBM],
        out_specs=[HBM, HBM, VMEM, VMEM],
        out_shape=(
            half,
            half,
            jax.ShapeDtypeStruct((owners, PARTS, rows // (owners * PARTS), width), BF16),
            jax.ShapeDtypeStruct((8, width // 8), F32),
        ),
        scratch_shapes=[
            pltpu.VMEM((rows, 3 * width), BF16),
            pltpu.VMEM((2, rows, 3 * width // 2), BF16),
            pltpu.VMEM(w_flipped.shape, BF16),
            pltpu.SemaphoreType.DMA((3,)),
        ],
        compiler_params=params(56),
        cost_estimate=cost(14 * rows * rows * width, 12 * MIB),
    )(
        core,
        tokens,
        projected,
        grads,
        share_parts,
        rounded,
        norm,
        gain,
        far(w_flipped),
    )


def split_sum(tiles):
    high = tiles.astype(BF16).astype(F32)
    return jnp.concatenate([high, tiles - high], axis=0).astype(BF16)


def weight_kernel(halves, flipped, grad_ref, other_grad_ref, *refs):
    *gain_refs, out_hbm, staged, sent = refs
    groups, _, lanes = out_hbm.shape
    steps = sent.shape[0] - 1
    cols = grad_ref.shape[1] // steps
    tiles = cols // lanes
    block = flipped.shape[0] // (groups * halves)
    span = tiles * halves * block
    copies = []
    for step in range(steps):
        at = pl.ds(step * cols, cols)
        both = jnp.concatenate([grad_ref[:, at], other_grad_ref[:, at]], axis=0)
        terms = dot(flipped[...], both).astype(BF16)
        for tile in range(tiles):
            for half in range(halves):
                for group in range(groups):
                    start = (half * groups + group) * block
                    place = step * span + (tile * halves + half) * block
                    staged[group, place : place + block] = terms[
                        start : start + block, tile * lanes : (tile + 1) * lanes
                    ]
        part = pl.ds(step * span, span)
        copies.append(
            pltpu.make_async_copy(staged.at[:, part], out_hbm.at[:, part], sent.at[step])
        )
        copies[-1].start()
    if gain_refs:
        gains = split_sum(gain_refs[0][...] + gain_refs[1][...])
        for group in range(groups):
            staged[group, steps * span :] = gains
        part = pl.ds(steps * span, 16)
        copies.append(
            pltpu.make_async_copy(staged.at[:, part], out_hbm.at[:, part], sent.at[steps])
        )
        copies[-1].start()
    for copy in copies:
        copy.wait()


def weight_terms(flipped, grads, other_grads, gains, groups, halves, steps):
    width, rows = flipped.shape
    lanes = 128
    extra = 16 if gains else 0
    shape = (groups, width // groups * grads.shape[1] // lanes + extra, lanes)
    return pl.pallas_call(
        lambda *refs: weight_kernel(halves, *refs),
        in_specs=[VMEM] * (3 + len(gains)),
        out_specs=HBM,
        out_shape=jax.ShapeDtypeStruct(shape, BF16),
        scratch_shapes=[pltpu.VMEM(shape, BF16), pltpu.SemaphoreType.DMA((steps + 1,))],
        compiler_params=params(24),
        cost_estimate=cost(2 * rows * width * grads.shape[1], 6 * MIB),
    )(flipped, grads, other_grads, *gains)


def regroup_kernel(block, terms_ref, out_ref):
    halves, steps, rows, _ = out_ref.shape
    tiles = (rows - 16) // block
    total = jnp.sum(terms_ref[...].astype(F32), axis=0)
    terms = total.astype(BF16)
    end = total.shape[0] - 16
    gains = split_sum(total[end : end + 8] + total[end + 8 :])
    for half in range(halves):
        for step in range(steps):
            for tile in range(tiles):
                start = ((step * tiles + tile) * halves + half) * block
                out_ref[half, step, tile * block : (tile + 1) * block] = terms[
                    start : start + block
                ]
            out_ref[half, step, tiles * block :] = gains


def regroup(terms, halves, steps, block):
    count, rows, lanes = terms.shape
    shape = (halves, steps, (rows - 16) // (halves * steps) + 16, lanes)
    return pl.pallas_call(
        lambda *refs: regroup_kernel(block, *refs),
        in_specs=[VMEM],
        out_shape=jax.ShapeDtypeStruct(shape, BF16),
        compiler_params=params(32),
        cost_estimate=cost(terms.size, 4 * MIB),
    )(terms)


def finish_kernel(terms_ref, out_ref, gain_ref):
    total = jnp.sum(terms_ref[...].astype(F32), axis=0)
    block = out_ref.shape[0]
    lanes = total.shape[1]
    for tile in range(out_ref.shape[1] // lanes):
        out_ref[:, tile * lanes : (tile + 1) * lanes] = total[tile * block : (tile + 1) * block]
    end = total.shape[0] - 16
    gain_ref[...] = tiles_row(total[end : end + 8] + total[end + 8 :])


def finish(terms, block):
    count, rows, lanes = terms.shape
    return pl.pallas_call(
        finish_kernel,
        in_specs=[VMEM],
        out_shape=(
            jax.ShapeDtypeStruct((block, (rows - 16) // block * lanes), F32),
            jax.ShapeDtypeStruct((1, 8 * lanes), F32),
        ),
        compiler_params=params(16),
        cost_estimate=cost(terms.size, MIB),
    )(terms)


def pool_kernel(halves, tokens, parts_ref, out_ref):
    per_clip = parts_ref.shape[0] // halves
    means = []
    for half in range(halves):
        pooled = jnp.sum(parts_ref[half * per_clip : (half + 1) * per_clip], axis=0) / tokens
        means.append(pooled)
    means = jnp.concatenate(means, axis=0).astype(BF16)
    for copy in range(out_ref.shape[0]):
        out_ref[copy] = means


def pool(parts, halves, tokens, copies):
    return pl.pallas_call(
        lambda *refs: pool_kernel(halves, tokens, *refs),
        in_specs=[VMEM],
        out_shape=jax.ShapeDtypeStruct((copies, halves * parts.shape[1], parts.shape[2]), BF16),
        compiler_params=params(8),
        cost_estimate=cost(parts.size, MIB),
    )(parts)


def embed_kernel(halves, pooled_ref, w_ref, pooled_out, centered_ref, gram_ref, rows_ref):
    groups, tiles, lanes = pooled_ref.shape
    tiles = tiles // halves
    means = pooled_ref[...].astype(F32)
    for half in range(halves):
        for tile in range(tiles):
            rows_ref[half * groups : (half + 1) * groups, tile * lanes : (tile + 1) * lanes] = (
                means[:, half * tiles + tile, :]
            )
    pooled = rows_ref[...].astype(BF16)
    pooled_out[...] = pooled
    embedding = dot(pooled, w_ref[...])
    centered = embedding - jnp.mean(embedding, axis=0, keepdims=True)
    centered_ref[...] = centered
    gram = dot(centered, centered, NT, lax.Precision.HIGHEST)
    size = gram_ref.shape[1]
    gram = [gram[i : i + size] for i in range(0, gram.shape[0], size)]
    gram = jnp.concatenate(gram, axis=1)
    for copy in range(gram_ref.shape[0]):
        gram_ref[copy] = gram


def embed(pooled, w_expand, copies, halves):
    clips = pooled.shape[0] * halves
    width, columns = w_expand.shape
    return pl.pallas_call(
        lambda *refs: embed_kernel(halves, *refs),
        in_specs=[VMEM, VMEM],
        out_shape=(
            jax.ShapeDtypeStruct((clips, width), BF16),
            jax.ShapeDtypeStruct((clips, columns), F32),
            jax.ShapeDtypeStruct((copies, min(clips, 8), clips * clips // min(clips, 8)), F32),
        ),
        scratch_shapes=[pltpu.VMEM((clips, width), F32)],
        compiler_params=params(16),
        cost_estimate=cost(2 * clips * w_expand.size, 2 * MIB),
    )(pooled, w_expand)


def embed_grad_kernel(coefficient, own_ref, gram_ref, centered_ref, w_ref, grad_ref, pool_ref):
    clips = centered_ref.shape[0]
    centered = centered_ref[...]
    gram = jnp.sum(gram_ref[...], axis=0)
    gram = [gram[:, i : i + clips] for i in range(0, gram.shape[1], clips)]
    gram = jnp.concatenate(gram, axis=0)
    variances = jnp.sum(centered * centered, axis=0, keepdims=True) / (clips - 1)
    mixed = dot(gram, centered, precision=lax.Precision.HIGHEST)
    grads = coefficient * (mixed / (clips - 1) - centered * variances)
    grad_ref[...] = grads.astype(BF16)
    row = lax.broadcasted_iota(jnp.int32, grads.shape, 0)
    own = jnp.sum(jnp.where(row == own_ref[0], grads, 0.0), axis=0, keepdims=True)
    own = jnp.broadcast_to(own, (16, own.shape[1])).astype(BF16)
    part = row_tiles(dot(own, w_ref[...], NT)[0:1])
    for copy in range(pool_ref.shape[0]):
        pool_ref[copy] = part


def embed_grads(own_index, gram_parts, centered, w_expand, coefficient):
    width = w_expand.shape[0]
    return pl.pallas_call(
        lambda *refs: embed_grad_kernel(coefficient, *refs),
        in_specs=[SMEM, VMEM, VMEM, VMEM],
        out_shape=(
            jax.ShapeDtypeStruct(centered.shape, BF16),
            jax.ShapeDtypeStruct((gram_parts.shape[0], 8, width // 8), F32),
        ),
        compiler_params=params(16),
        cost_estimate=cost(2 * 16 * w_expand.size, 2 * MIB),
    )(own_index, gram_parts, centered, w_expand)


DP = ("zh", "x", "y")
FRAME = ("zl", "core")
SIZES = {"zh": 2, "x": 4, "y": 4, "zl": 4, "core": 2}
SWAP = [(0, 1), (1, 0)]


def to_each(array, axis):
    return lax.all_to_all(array, axis, split_axis=0, concat_axis=0, tiled=True)


def per_device(clip_tokens, out_grad, ln_gain, w_project, w_expand):
    frame_count = lax.axis_size(FRAME)
    clip_count = lax.axis_size(DP)
    halves, steps = lax.axis_size("zh"), lax.axis_size("zl")
    plane = lax.axis_size(("x", "y"))
    core = lax.axis_index("core").reshape(1)
    own_frame = lax.axis_index(FRAME).reshape(1)
    own_clip = lax.axis_index(DP)
    frames_dev, patches, width = clip_tokens.shape[1:]
    patches_dev = patches // frame_count
    rows = frames_dev * patches
    tokens_clip = frames_dev * frame_count * patches
    column_block = 3 * width // frame_count
    block_rows = width // clip_count
    gain = ln_gain[None, :]

    w_near = fetch(w_project)
    tokens = to_each(pack(clip_tokens[0], frame_count), FRAME)
    out_grad, tokens, w_near = lax.optimization_barrier((out_grad, tokens, w_near))
    gathered = lax.all_gather(out_grad[0], FRAME, axis=0, tiled=True)
    tokens, normed, projected, pool_parts = forward(
        tokens, gain, w_near, patches_dev, halves * frame_count
    )
    other_normed = lax.ppermute(normed, "core", SWAP)

    pool_parts = to_each(pool_parts, ("zh",) + FRAME)
    pooled = to_each(pool(pool_parts, halves, tokens_clip, plane), ("x", "y"))
    rounded, norm = attend(projected, patches_dev)
    flipped = flip(normed, other_normed)
    pooled, rounded, norm, flipped = lax.optimization_barrier((pooled, rounded, norm, flipped))
    pooled_all, centered, gram_parts = embed(pooled, w_expand, frame_count, halves)
    gram_parts = to_each(gram_parts, FRAME)
    w_flipped = flip(w_project)
    gram_parts, w_flipped = lax.optimization_barrier((gram_parts, w_flipped))
    coefficient = 100.0 * tokens_clip / (w_expand.shape[1] * frame_count * (clip_count - 1))
    embed_grad, share_parts = embed_grads(
        own_clip.reshape(1), gram_parts, centered, w_expand, coefficient
    )
    share_parts = to_each(share_parts, FRAME)
    row_part = lax.dynamic_slice_in_dim(pooled_all, own_clip * block_rows, block_rows, 1)
    expand_grad = dot(row_part, embed_grad, TN)

    gathered, _ = lax.optimization_barrier((gathered, gram_parts))
    gathered = gathered.reshape(-1, frame_count, patches_dev, width)
    grads = merge(own_frame, gathered, frame_count).reshape(rows, width)

    kept, outgoing, token_part, gain_part = backward(
        core,
        tokens,
        projected,
        grads,
        share_parts,
        rounded,
        norm,
        gain,
        w_flipped,
        column_block,
        tokens_clip,
        frame_count,
    )
    token_parts = lax.all_gather(token_part, FRAME)
    incoming, other_gain = lax.ppermute((outgoing, gain_part), "core", SWAP)
    terms = weight_terms(
        flipped, kept, incoming, (gain_part, other_gain), plane, halves, steps
    )
    terms = to_each(terms, ("x", "y"))
    terms = regroup(terms, halves, steps, block_rows)
    terms = to_each(terms.reshape((-1,) + terms.shape[2:]), ("zh", "zl"))
    token_grad = place(own_frame, token_parts, frames_dev)[None]
    terms, token_grad = lax.optimization_barrier((terms, token_grad))
    project_grad, gain_grad = finish(terms, block_rows)
    return (token_grad, project_grad, expand_grad, gain_grad[0])


def solution(mesh):
    split = jax.sharding.Mesh(
        mesh.devices.reshape(tuple(SIZES.values())), tuple(SIZES)
    )
    return jax.shard_map(
        per_device,
        mesh=split,
        in_specs=(
            P(DP, FRAME, None, None),
            P(DP, FRAME, None, None),
            P(),
            P(),
            P(None, FRAME),
        ),
        out_specs=(P(DP, FRAME, None, None), P(DP, FRAME), P(DP, FRAME), P()),
        check_vma=False,
    )
```

time: 192 us -> 178 us (0.927)
  blocking collectives: 73.4 us -> 60.8 us
  Pallas kernels: 51.5 us -> 42.9 us
  waiting for transfers between devices: 16.1 us -> 22.7 us
  local copies, waits for them, and re-layouts: 6.53 us -> 9.48 us
    all_to_all x3 -> x2, blocking collectives: 73.4 us -> 60.8 us  [to_each(): return lax.all_to_all(array, axis, split_axis=0, concat_axis=0, tiled=True)]
    all_to_all x5, waiting for transfers between devices: 12.7 us -> 18.3 us  [to_each(): return lax.all_to_all(array, axis, split_axis=0, concat_axis=0, tiled=True)]
    pallas_call x1, Pallas kernels: 8.86 us -> 3.61 us  [forward(): pl.pallas_call(lambda *refs: forward_kernel(patches, *refs), in_specs=[VM...]
    unnamed x20, local copies, waits for them, and re-layouts: 6.53 us -> 9.48 us
    all_gather x2, waiting for transfers between devices: 0.01 us -> 2.39 us  [the longest x1 2.38 us: per_device(): gathered = lax.all_gather(out_grad[0], FRAME, axis=0, tiled=True)]
    pallas_call x8 -> x7, Pallas kernels: 17.1 us -> 19.2 us  [the longest x2 9.84 us: flip(): pl.pallas_call(flip_kernel, in_specs=[VMEM] * len(arrays), out_shape=jax....]
    pallas_call x2 -> x1, Pallas kernels: 3.94 us -> 3.15 us  [weight_terms(): pl.pallas_call(lambda *refs: weight_kernel(halves, *refs), in_specs=[VMEM...]
  transfers between devices with their start and end apart: 13 -> 10, of which waited for: 5 -> 5; matrix products, arithmetic and copies ran while one was open for 1% -> 1% of each run, Pallas kernels for 23% -> 17%
where the time goes in v3:
time: 178 us; the launch traced here: 177 us
  blocking collectives  60.8 us (34%)
  Pallas kernels  42.9 us (24%)
  starting transfers between devices  26.2 us (15%)
  waiting for transfers between devices  22.7 us (13%)
  between operations  14.2 us (8%)
  local copies, waits for them, and re-layouts  9.48 us (5%)
    all_to_all x2, blocking collectives, to_each(): return lax.all_to_all(array, axis, split_axis=0, concat_axis=0, tiled=True)  60.8 us
    all_to_all x5, starting transfers between devices, to_each(): return lax.all_to_all(array, axis, split_axis=0, concat_axis=0, tiled=True)  25.2 us
    all_to_all x5, waiting for transfers between devices, to_each(): return lax.all_to_all(array, axis, split_axis=0, concat_axis=0, tiled=True)  18.3 us
    pallas_call x2, Pallas kernels, flip(): pl.pallas_call(flip_kernel, in_specs=[VMEM] * len(arrays), out_shape=jax....  9.84 us
    pallas_call x1, Pallas kernels, backward(): pl.pallas_call(lambda *refs: backward_kernel(block, count, *refs), in_spe...  9.53 us
    unnamed x20, local copies, waits for them, and re-layouts  9.48 us
    pallas_call x1, Pallas kernels, forward(): pl.pallas_call(lambda *refs: forward_kernel(patches, *refs), in_specs=[VM...  3.61 us
  transfers between devices with their start and end apart: 10, of which 5 were waited for; matrix products, arithmetic and copies ran while one was open for 1% of the time, Pallas kernels for 17%

profile of v3, /device:TPU:8, one launch (start us, length us, event | category | flops | bytes accessed | tf_op | source)
XLA Modules:
  0.0 177.2 jit_solution(7231171469749586461)
XLA Ops:
  7.2 2.0 %shard_map.84 = bf16[8,2,16,1024]{3,2,1,0:T(8,128)(2,1)} custom-call(bf16[4,64,1024]{2,1,0:T(8,128)(2,1)} %bitcast.20), custom_call_target="tpu_custom_call" | custom-call | bytes 1048576 | tf_op jit(solution)/shard_map/pallas_call | solution.py:71
  9.2 5.9 %all-to-all-start = ((bf16[8,2,16,1024]{3,2,1,0:T(8,128)(2,1)}), bf16[8,2,16,1024]{3,2,1,0:T(8,128)(2,1)S(1)}, u32[]{:S(2)}, u32[]{:S(2)}) async-start(bf16[8,2,16,1024]{3,2,1,0:T(8,128)(2,1)} %shard_map.84), calls=%async_computation | async-start | bytes 1048576 | tf_op jit(solution)/shard_map/all_to_all | solution.py:677
  15.1 2.8 %shard_map.85.refs_2_ = bf16[1024,3072]{1,0:T(8,128)(2,1)S(1)} custom-call(bf16[1024,3072]{1,0:T(8,128)(2,1)} %refs_0_.1), custom_call_target="tpu_custom_call" | custom-call | bytes 12582912 | tf_op jit(solution)/shard_map/pallas_call | solution.py:181
  17.9 2.6 %copy-done.1 = bf16[1024,3072]{1,0:T(8,128)(2,1)} copy-done((bf16[1024,3072]{1,0:T(8,128)(2,1)}, bf16[1024,3072]{1,0:T(8,128)(2,1)S(1)}, u32[]{:S(2)}) %copy-start.1) | copy-done | bytes 6291480
  20.5 9.9 %all-to-all-done.refs_0_ = bf16[8,2,16,1024]{3,2,1,0:T(8,128)(2,1)S(1)} async-done(((bf16[8,2,16,1024]{3,2,1,0:T(8,128)(2,1)}), bf16[8,2,16,1024]{3,2,1,0:T(8,128)(2,1)S(1)}, u32[]{:S(2)}, u32[]{:S(2)}) %all-to-all-start) | async-done | bytes 524320 | tf_op jit(solution)/shard_map/all_to_all | solution.py:677
  30.5 2.8 %copy-done.2 = bf16[1024,3072]{1,0:T(8,128)(2,1)S(1)} copy-done((bf16[1024,3072]{1,0:T(8,128)(2,1)S(1)}, bf16[1024,3072]{1,0:T(8,128)(2,1)}, u32[]{:S(2)}) %copy-start.2) | copy-done | bytes 6291480
  33.2 3.6 %shard_map.86 = (bf16[256,1024]{1,0:T(8,128)(2,1)}, bf16[256,1024]{1,0:T(8,128)(2,1)}, bf16[256,3072]{1,0:T(8,128)(2,1)}, f32[16,8,128]{2,1,0:T(8,128)S(1)}) custom-call(bf16[8,2,16,1024]{3,2,1,0:T(8,128)(2,1)S(1)} %all-to-all-done.refs_0_, f32[1,1024]{1,0:T(1,128)S(1)} %bitcast.16, bf16[1024,3072]{1,0:T(8,128)(2,1)S(1)} %copy-done.2), custom_call_target="tpu_custom_call" | custom-call | flops 2684354560 | bytes 10485760 | tf_op jit(solution)/shard_map/pallas_call | solution.py:256
  37.0 14.6 %all_to_all.35.refs_0_ = f32[16,8,128]{2,1,0:T(8,128)S(1)} all-to-all(f32[16,8,128]{2,1,0:T(8,128)S(1)} %get-tuple-element.35), channel_id=1, replica_groups=mesh['zh'=2,'x'=4,'y'=4,'zl'=4,'core'=2] {'zh','zl','core'}, dimensions={0} | all-to-all | bytes 131072 | tf_op jit(solution)/shard_map/all_to_all | solution.py:677
  52.2 7.4 %all-to-all-start.2 = ((bf16[16,16,128]{2,1,0:T(8,128)(2,1)}), bf16[16,16,128]{2,1,0:T(8,128)(2,1)S(1)}, u32[]{:S(2)}, u32[]{:S(2)}) async-start(bf16[16,16,128]{2,1,0:T(8,128)(2,1)} %shard_map.87), calls=%async_computation.2 | async-start | bytes 131072 | tf_op jit(solution)/shard_map/all_to_all | solution.py:677
  59.6 3.5 %shard_map.88 = (bf16[8,2,256,128]{3,2,1,0:T(8,128)(2,1)}, f32[32,128]{1,0:T(8,128)}) custom-call(bf16[256,3072]{1,0:T(8,128)(2,1)} %get-tuple-element.36.refs_0_.refs_2_), custom_call_target="tpu_custom_call" | custom-call | flops 50331648 | bytes 6291456 | tf_op jit(solution)/shard_map/pallas_call | solution.py:327
  63.9 2.6 %shard_map.89.refs_0_ = bf16[1024,512]{1,0:T(8,128)(2,1)} custom-call(bf16[256,1024]{1,0:T(8,128)(2,1)} %get-tuple-element.39.refs_0_, bf16[256,1024]{1,0:T(8,128)(2,1)} %copy-done.8), custom_call_target="tpu_custom_call" | custom-call | bytes 2097152 | tf_op jit(solution)/shard_map/pallas_call | solution.py:291
  66.5 1.4 shard_map.90
  67.9 3.3 %all-to-all-start.3 = ((f32[8,8,128]{2,1,0:T(8,128)}), f32[8,8,128]{2,1,0:T(8,128)S(1)}, u32[]{:S(2)}, u32[]{:S(2)}) async-start(f32[8,8,128]{2,1,0:T(8,128)} %get-tuple-element.44), calls=%async_computation.3 | async-start | bytes 65536 | tf_op jit(solution)/shard_map/all_to_all | solution.py:677
  71.2 7.3 %shard_map.91.refs_8_ = bf16[3072,1024]{1,0:T(8,128)(2,1)} custom-call(bf16[1024,3072]{1,0:T(8,128)(2,1)} %refs_0_.1), custom_call_target="tpu_custom_call" | custom-call | bytes 12582912 | tf_op jit(solution)/shard_map/pallas_call | solution.py:291
  78.5 1.5 shard_map.93
  80.0 5.0 %all-to-all-start.4 = ((f32[8,8,128]{2,1,0:T(8,128)}), f32[8,8,128]{2,1,0:T(8,128)S(1)}, u32[]{:S(2)}, u32[]{:S(2)}) async-start(f32[8,8,128]{2,1,0:T(8,128)} %get-tuple-element.48), calls=%async_computation.4 | async-start | bytes 65536 | tf_op jit(solution)/shard_map/all_to_all | solution.py:677
  85.3 2.4 %all-gather.5.cloned.1.call-done = bf16[1,32,64,1024]{3,2,0,1:T(8,128)(2,1)} async-done(((bf16[1,4,64,1024]{3,2,0,1:T(8,128)(2,1)}), bf16[1,32,64,1024]{3,2,0,1:T(8,128)(2,1)}) %all-gather.5.cloned.1.call-update) | async-done | bytes 4194320 | tf_op jit(solution)/shard_map/all_gather | solution.py:699
  91.4 9.5 %shard_map.94 = (bf16[256,1536]{1,0:T(8,128)(2,1)}, bf16[256,1536]{1,0:T(8,128)(2,1)}, bf16[8,2,16,1024]{3,2,1,0:T(8,128)(2,1)}, f32[8,128]{1,0:T(8,128)}) custom-call(s32[1]{0:T(128)} %bitcast.2.refs_0_, bf16[256,1024]{1,0:T(8,128)(2,1)} %get-tuple-element.41.refs_1_, bf16[256,3072]{1,0:T(8,128)(2,1)} %get-tuple-element.36.refs_0_.refs_2_, ...), custom_call_target="tpu_custom_call" | custom-call | flops 939524096 | bytes 12582912 | tf_op jit(solution)/shard_map/pallas_call | solution.py:434
  101.5 2.0 %collective-permute-done.2.refs_4_ = f32[8,128]{1,0:T(8,128)S(1)} collective-permute-done((f32[8,128]{1,0:T(8,128)}, f32[8,128]{1,0:T(8,128)S(1)}, u32[]{:S(2)}, u32[]{:S(2)}) %collective-permute-start.2) | collective-permute-done | bytes 4128 | tf_op jit(solution)/shard_map/ppermute | solution.py:741
  105.4 3.1 %shard_map.95 = bf16[16,784,128]{2,1,0:T(8,128)(2,1)S(1)} custom-call(bf16[1024,512]{1,0:T(8,128)(2,1)S(1)} %copy-done.4, bf16[256,1536]{1,0:T(8,128)(2,1)S(1)} %copy-done.6, bf16[256,1536]{1,0:T(8,128)(2,1)S(1)} %collective-permute-done.1.refs_2_, f32[8,128]{1,0:T(8,128)S(1)} %copy-done.7, f32[8,128]{1,0:T(8,128)S(1)} %collective-permute-done.2.refs_4_), custom_call_target="tpu_custom_call" | custom-call | flops 1610612736 | bytes 6291456 | tf_op jit(solution)/shard_map/pallas_call | solution.py:514
  108.5 46.3 %all_to_all.36.refs_0_ = bf16[16,784,128]{2,1,0:T(8,128)(2,1)S(1)} all-to-all(bf16[16,784,128]{2,1,0:T(8,128)(2,1)S(1)} %shard_map.95), channel_id=1, replica_groups=mesh['zh'=2,'x'=4,'y'=4,'zl'=4,'core'=2] {'x','y'}, dimensions={0} | all-to-all | bytes 6422528 | tf_op jit(solution)/shard_map/all_to_all | solution.py:677
  155.9 3.5 %all-to-all-start.6 = ((bf16[8,112,128]{2,1,0:T(8,128)(2,1)}), bf16[8,112,128]{2,1,0:T(8,128)(2,1)S(1)}, u32[]{:S(2)}, u32[]{:S(2)}) async-start(bf16[8,112,128]{2,1,0:T(8,128)(2,1)} %bitcast.9), calls=%async_computation.6 | async-start | bytes 458752 | tf_op jit(solution)/shard_map/all_to_all | solution.py:677
  160.3 2.0 %shard_map.97 = bf16[4,8,8,1024]{3,2,1,0:T(8,128)(2,1)} custom-call(s32[1]{0:T(128)} %bitcast.3.index_ref, bf16[8,8,2,16,1024]{4,3,2,1,0:T(8,128)(2,1)} %bitcast.18), custom_call_target="tpu_custom_call" | custom-call | bytes 1048576 | tf_op jit(solution)/shard_map/pallas_call | solution.py:128
  162.3 7.4 %all-to-all-done.6.terms_ref = bf16[8,112,128]{2,1,0:T(8,128)(2,1)S(1)} async-done(((bf16[8,112,128]{2,1,0:T(8,128)(2,1)}), bf16[8,112,128]{2,1,0:T(8,128)(2,1)S(1)}, u32[]{:S(2)}, u32[]{:S(2)}) %all-to-all-start.6) | async-done | bytes 229408 | tf_op jit(solution)/shard_map/all_to_all | solution.py:677
  (36 shorter events, 10.7 us)
Async XLA Ops:
  9.2 21.3 %all-to-all-start = ((bf16[8,2,16,1024]{3,2,1,0:T(8,128)(2,1)}), bf16[8,2,16,1024]{3,2,1,0:T(8,128)(2,1)S(1)}, u32[]{:S(2)}, u32[]{:S(2)}) async-start(bf16[8,2,16,1024]{3,2,1,0:T(8,128)(2,1)} %shard_map.84), calls=%async_computation | async-start | bytes 1048576 | tf_op jit(solution)/shard_map/all_to_all | solution.py:677
  15.1 15.4 %copy-start.5 = (f32[1024]{0:T(1024)S(1)}, f32[1024]{0:T(1024)}, u32[]{:S(2)}) copy-start(f32[1024]{0:T(1024)} %param.7) | copy-start | bytes 12292
  15.1 72.6 %all-gather.5.cloned.1.call-start = ((), (), s32[]{:S(2)}) async-start(), calls=%async_computation.7 | async-start | bytes 4718592 | tf_op jit(solution)/shard_map/all_gather | solution.py:699
  17.9 2.6 %copy-start.1 = (bf16[1024,3072]{1,0:T(8,128)(2,1)}, bf16[1024,3072]{1,0:T(8,128)(2,1)S(1)}, u32[]{:S(2)}) copy-start(bf16[1024,3072]{1,0:T(8,128)(2,1)S(1)} %shard_map.85.refs_2_) | copy-start | bytes 18874372
  30.5 2.8 %copy-start.2 = (bf16[1024,3072]{1,0:T(8,128)(2,1)S(1)}, bf16[1024,3072]{1,0:T(8,128)(2,1)}, u32[]{:S(2)}) copy-start(bf16[1024,3072]{1,0:T(8,128)(2,1)} %copy-done.1) | copy-start | bytes 18874372
  36.9 29.6 %copy-start = (bf16[1024,1024]{1,0:T(8,128)(2,1)S(1)}, bf16[1024,1024]{1,0:T(8,128)(2,1)}, u32[]{:S(2)}) copy-start(bf16[1024,1024]{1,0:T(8,128)(2,1)} %refs_3_.1) | copy-start | bytes 6291460
  36.9 26.3 %collective-permute-start = (bf16[256,1024]{1,0:T(8,128)(2,1)}, bf16[256,1024]{1,0:T(8,128)(2,1)S(1)}, u32[]{:S(2)}, u32[]{:S(2)}) collective-permute-start(bf16[256,1024]{1,0:T(8,128)(2,1)} %get-tuple-element.39.refs_0_), channel_id=1, source_target_pairs={{0,1},{1,0},{2,3},{3,2},{4,5},{5,4},{6,7},{7,6},{8,9},{9,8},{10,11... | collective-permute-start | bytes 1572872 | tf_op jit(solution)/shard_map/ppermute | solution.py:703
  52.2 14.3 %all-to-all-start.2 = ((bf16[16,16,128]{2,1,0:T(8,128)(2,1)}), bf16[16,16,128]{2,1,0:T(8,128)(2,1)S(1)}, u32[]{:S(2)}, u32[]{:S(2)}) async-start(bf16[16,16,128]{2,1,0:T(8,128)(2,1)} %shard_map.87), calls=%async_computation.2 | async-start | bytes 131072 | tf_op jit(solution)/shard_map/all_to_all | solution.py:677
  63.1 0.8 copy-start.8
  67.9 10.6 %all-to-all-start.3 = ((f32[8,8,128]{2,1,0:T(8,128)}), f32[8,8,128]{2,1,0:T(8,128)S(1)}, u32[]{:S(2)}, u32[]{:S(2)}) async-start(f32[8,8,128]{2,1,0:T(8,128)} %get-tuple-element.44), calls=%async_computation.3 | async-start | bytes 65536 | tf_op jit(solution)/shard_map/all_to_all | solution.py:677
  80.0 10.7 %all-to-all-start.4 = ((f32[8,8,128]{2,1,0:T(8,128)}), f32[8,8,128]{2,1,0:T(8,128)S(1)}, u32[]{:S(2)}, u32[]{:S(2)}) async-start(f32[8,8,128]{2,1,0:T(8,128)} %get-tuple-element.48), calls=%async_computation.4 | async-start | bytes 65536 | tf_op jit(solution)/shard_map/all_to_all | solution.py:677
  85.0 75.3 %all-gather.7.cloned.1.call-start = ((), (), s32[]{:S(2)}) async-start(), calls=%async_computation.8 | async-start | bytes 4718592 | tf_op jit(solution)/shard_map/all_gather | solution.py:740
  88.8 0.8 copy-start.3
  90.8 0.6 copy-start.9
  91.4 12.2 %copy-start.4 = (bf16[1024,512]{1,0:T(8,128)(2,1)S(1)}, bf16[1024,512]{1,0:T(8,128)(2,1)}, u32[]{:S(2)}) copy-start(bf16[1024,512]{1,0:T(8,128)(2,1)} %shard_map.89.refs_0_) | copy-start | bytes 3145732
  100.9 2.6 %collective-permute-start.1 = (bf16[256,1536]{1,0:T(8,128)(2,1)}, bf16[256,1536]{1,0:T(8,128)(2,1)S(1)}, u32[]{:S(2)}, u32[]{:S(2)}) collective-permute-start(bf16[256,1536]{1,0:T(8,128)(2,1)} %get-tuple-element.53), channel_id=1, source_target_pairs={{0,1},{1,0},{2,3},{3,2},{4,5},{5,4},{6,7},{7,6},{8,9},{9,8},{10,11... | collective-permute-start | bytes 2359304 | tf_op jit(solution)/shard_map/ppermute | solution.py:741
  101.0 2.5 %collective-permute-start.2 = (f32[8,128]{1,0:T(8,128)}, f32[8,128]{1,0:T(8,128)S(1)}, u32[]{:S(2)}, u32[]{:S(2)}) collective-permute-start(f32[8,128]{1,0:T(8,128)} %get-tuple-element.54.refs_3_), channel_id=1, source_target_pairs={{0,1},{1,0},{2,3},{3,2},{4,5},{5,4},{6,7},{7,6},{8,9},{9,8},{10,11... | collective-permute-start | bytes 12296 | tf_op jit(solution)/shard_map/ppermute | solution.py:741
  103.5 1.1 copy-start.6
  104.7 0.7 copy-start.7
  155.9 13.8 %all-to-all-start.6 = ((bf16[8,112,128]{2,1,0:T(8,128)(2,1)}), bf16[8,112,128]{2,1,0:T(8,128)(2,1)S(1)}, u32[]{:S(2)}, u32[]{:S(2)}) async-start(bf16[8,112,128]{2,1,0:T(8,128)(2,1)} %bitcast.9), calls=%async_computation.6 | async-start | bytes 458752 | tf_op jit(solution)/shard_map/all_to_all | solution.py:677
Sparse Core Ops, SparseCore 0:
  30.6 57.0 all-gather.4
  101.1 52.4 all-gather.6

commit v4 on v3

--- a/solution.py
+++ b/solution.py
@@ -31,10 +31,6 @@
 
 def far_shape(shape, dtype):
     return pltpu.HBM(shape, dtype)
-
-
-def near(array):
-    return pltpu.with_memory_space_constraint(array, pltpu.VMEM)
 
 
 def near_shape(shape, dtype):
@@ -73,37 +69,7 @@
         out_shape=jax.ShapeDtypeStruct((groups, PARTS, rows, width), array.dtype),
         compiler_params=params(8),
         cost_estimate=cost(0, 4 * array.size),
-    )(far(array))
-
-
-def merge_kernel(index_ref, source, out, own, arrived):
-    load = pltpu.make_async_copy(source.at[:, index_ref[0]], own, arrived.at[0])
-    load.start()
-    load.wait()
-    parts, owners, rows, _ = out.shape
-    frames = own.shape[0] // owners
-    size = rows // frames
-    for owner in range(owners):
-        for part in range(parts):
-            pieces = [
-                own[owner * frames + frame, part * size : (part + 1) * size].astype(F32)
-                for frame in range(frames)
-            ]
-            out[part, owner] = jnp.concatenate(pieces, axis=0).astype(BF16)
-
-
-def merge(index, gathered, owners):
-    frames, _, size, width = gathered.shape
-    rows = frames * size // (owners * PARTS)
-    return pl.pallas_call(
-        merge_kernel,
-        in_specs=[SMEM, HBM],
-        out_specs=VMEM,
-        out_shape=jax.ShapeDtypeStruct((PARTS, owners, rows, width), BF16),
-        scratch_shapes=[pltpu.VMEM((frames, size, width), BF16), pltpu.SemaphoreType.DMA((1,))],
-        compiler_params=params(8),
-        cost_estimate=cost(0, 4 * frames * size * width),
-    )(index, far(gathered))
+    )(array)
 
 
 def place_kernel(index_ref, source, target, own, arrived):
@@ -171,29 +137,11 @@
     return jnp.concatenate([array[:rows], array[rows:]], axis=1)
 
 
-def fetch_kernel(source, target, arrived):
-    load = pltpu.make_async_copy(source, target, arrived.at[0])
-    load.start()
-    load.wait()
-
-
-def fetch(array):
-    return pl.pallas_call(
-        fetch_kernel,
-        in_specs=[HBM],
-        out_specs=VMEM,
-        out_shape=near_shape(array.shape, array.dtype),
-        scratch_shapes=[pltpu.SemaphoreType.DMA((1,))],
-        compiler_params=params(4),
-        cost_estimate=cost(0, 4 * array.size),
-    )(far(array))
-
-
 def forward_kernel(
     patches,
     x_ref,
     gain_ref,
-    w_ref,
+    w_hbm,
     inputs_hbm,
     normed_hbm,
     proj_hbm,
@@ -203,30 +151,43 @@
     proj_ref,
     total,
     sent,
+    w_ref,
+    arrived,
 ):
     rows, width = normed_ref.shape
     block_rows = rows // PARTS
-    parts = sent.shape[0] - 2
+    parts = sent.shape[0] - 1
     chunk = w_ref.shape[1] // parts
     chunks = [pl.ds(part * chunk, chunk) for part in range(parts)]
+    loads = [
+        pltpu.make_async_copy(w_hbm.at[:, cols], w_ref.at[:, cols], arrived.at[part])
+        for part, cols in enumerate(chunks)
+    ]
+    for load in loads:
+        load.start()
     for part in range(PARTS):
         block = x_ref[:, part]
         inputs_ref[part * block_rows : (part + 1) * block_rows] = block.reshape(block_rows, width)
-    stores = [pltpu.make_async_copy(inputs_ref, inputs_hbm, sent.at[parts + 1])]
+    stores = [pltpu.make_async_copy(inputs_ref, inputs_hbm, sent.at[parts, 1])]
     stores[-1].start()
     inputs = inputs_ref[...].astype(F32)
     standard, _ = standardize(inputs)
     normed = (standard * gain_ref[...]).astype(BF16)
     normed_ref[...] = normed
-    stores.append(pltpu.make_async_copy(normed_ref, normed_hbm, sent.at[parts]))
+    stores.append(pltpu.make_async_copy(normed_ref, normed_hbm, sent.at[parts, 0]))
     stores[-1].start()
     total[...] = jnp.sum(inputs, axis=0, keepdims=True)
     for part, cols in enumerate(chunks):
+        loads[part].wait()
         proj_ref[:, cols] = dot(normed, w_ref[:, cols]).astype(BF16)
-        stores.append(
-            pltpu.make_async_copy(proj_ref.at[:, cols], proj_hbm.at[:, cols], sent.at[part])
-        )
-        stores[-1].start()
+        for pair in range(proj_hbm.shape[0]):
+            lanes = pl.ds(part * chunk + pair * proj_hbm.shape[3], proj_hbm.shape[3])
+            stores.append(
+                pltpu.make_async_copy(
+                    proj_ref.at[:, lanes], proj_hbm.at[pair, part], sent.at[part, pair]
+                )
+            )
+            stores[-1].start()
     mask = same_patch(2 * block_rows, block_rows, patches // PARTS)
     slab = 2 * width // HEADS
     scale = (width // HEADS) ** -0.5
@@ -252,15 +213,15 @@
 def forward(tokens, gain, w_project, patches, copies):
     width = tokens.shape[-1]
     rows = tokens.size // width
-    parts = 6
+    parts = 3
     return pl.pallas_call(
         lambda *refs: forward_kernel(patches, *refs),
-        in_specs=[VMEM] * 3,
+        in_specs=[VMEM, VMEM, HBM],
         out_specs=[HBM, HBM, HBM, VMEM],
         out_shape=(
             far_shape((rows, width), BF16),
             far_shape((rows, width), BF16),
-            far_shape((rows, 3 * width), BF16),
+            far_shape((HEADS // 2, 3, rows, 2 * width // HEADS), BF16),
             jax.ShapeDtypeStruct((copies, 8, width // 8), F32),
         ),
         scratch_shapes=[
@@ -268,11 +229,13 @@
             pltpu.VMEM((rows, width), BF16),
             pltpu.VMEM((rows, 3 * width), BF16),
             pltpu.VMEM((1, width), F32),
-            pltpu.SemaphoreType.DMA((parts + 2,)),
+            pltpu.SemaphoreType.DMA((parts + 1, HEADS // 2)),
+            pltpu.VMEM(w_project.shape, BF16),
+            pltpu.SemaphoreType.DMA((parts,)),
         ],
         compiler_params=params(32),
         cost_estimate=cost(10 * rows * width * width, 10 * MIB, HEADS * rows * rows),
-    )(tokens, gain, near(w_project))
+    )(tokens, gain, far(w_project))
 
 
 def flip_kernel(*refs):
@@ -299,16 +262,13 @@
 
 def attend_kernel(patches, proj_ref, rounded, norm):
     rows = rounded.shape[3]
-    width = proj_ref.shape[1] // 3
     mask = same_patch(2 * rows, rows, patches // PARTS)
-    slab = 2 * width // HEADS
-    scale = (width // HEADS) ** -0.5
+    scale = (proj_ref.shape[3] // 2) ** -0.5
     for pair in range(HEADS // 2):
-        at = pair * slab
         for part in range(PARTS):
             own = pl.ds(part * rows, rows)
-            query = proj_ref[own, at : at + slab]
-            keys = proj_ref[own, width + at : width + at + slab]
+            query = proj_ref[pair, 0, own]
+            keys = proj_ref[pair, 1, own]
             scores = jnp.where(mask, dot(stacked(keys), query, NT) * scale, -jnp.inf)
             for head in range(2):
                 score = scores[head * rows : (head + 1) * rows]
@@ -322,7 +282,7 @@
 
 
 def attend(projected, patches):
-    rows = projected.shape[0] // PARTS
+    rows = projected.shape[2] // PARTS
     pairs = HEADS // 2
     return pl.pallas_call(
         lambda *refs: attend_kernel(patches, *refs),
@@ -332,7 +292,7 @@
             jax.ShapeDtypeStruct((HEADS * PARTS, rows), F32),
         ),
         compiler_params=params(56),
-        cost_estimate=cost(rows * rows * projected.shape[1], 6 * MIB, HEADS * rows * rows),
+        cost_estimate=cost(8 * rows * rows * projected.shape[3], 6 * MIB, HEADS * rows * rows),
     )(projected)
 
 
@@ -344,11 +304,12 @@
     block,
     count,
     core_ref,
-    x_ref,
-    proj_ref,
-    grad_ref,
+    frame_ref,
+    x_hbm,
+    proj_hbm,
+    gathered_hbm,
     parts_ref,
-    rounded,
+    rounded_hbm,
     norm_ref,
     gain_ref,
     w_hbm,
@@ -359,22 +320,57 @@
     proj_grad,
     sorted_grad,
     w_ref,
+    received,
+    grad_ref,
+    x_ref,
+    proj_ref,
+    rounded,
     arrived,
+    ready,
 ):
     rows, width = grad_ref.shape
     block_rows = rows // PARTS
+    load = pltpu.make_async_copy(gathered_hbm.at[:, frame_ref[0]], received, arrived.at[3])
+    load.start()
+    pairs = []
+    for pair in range(HEADS // 2):
+        pairs.append(
+            [
+                pltpu.make_async_copy(proj_hbm.at[pair], proj_ref.at[pair], ready.at[pair, 0]),
+                pltpu.make_async_copy(rounded_hbm.at[pair], rounded.at[pair], ready.at[pair, 1]),
+            ]
+        )
+        for pair_load in pairs[-1]:
+            pair_load.start()
+    x_load = pltpu.make_async_copy(x_hbm, x_ref, arrived.at[4])
+    x_load.start()
     w_load = pltpu.make_async_copy(w_hbm, w_ref, arrived.at[0])
     w_load.start()
+    load.wait()
+    frames, size, _ = received.shape
+    run = token_ref.shape[2] * PARTS // size
+    size = size // PARTS
+    for part in range(PARTS):
+        for first in range(0, frames, run):
+            pieces = [
+                received[frame, part * size : (part + 1) * size].astype(F32)
+                for frame in range(first, first + run)
+            ]
+            start = part * block_rows + first * size
+            grad_ref[start : start + run * size] = jnp.concatenate(pieces, axis=0).astype(BF16)
     share = tiles_row(jnp.sum(parts_ref[...], axis=0)) / count
     slab = 2 * width // HEADS
     scale = (width // HEADS) ** -0.5
     for pair in range(HEADS // 2):
         at = pair * slab
+        if pair % 2 == 0:
+            for pair_load in pairs[pair] + pairs[pair + 1]:
+                pair_load.wait()
         for part in range(PARTS):
             own = pl.ds(part * block_rows, block_rows)
-            query = proj_ref[own, at : at + slab]
-            keys = proj_ref[own, width + at : width + at + slab]
-            values = proj_ref[own, 2 * width + at : 2 * width + at + slab]
+            query = proj_ref[pair, 0, own]
+            keys = proj_ref[pair, 1, own]
+            values = proj_ref[pair, 2, own]
             grads = grad_ref[own, at : at + slab].astype(F32) + share[:, at : at + slab]
             grads = grads.astype(BF16)
             probs = rounded[pair, part]
@@ -405,6 +401,7 @@
     ]
     for store in stores:
         store.start()
+    x_load.wait()
     w_load.wait()
     normed_grad = dot(proj_grad[...], w_ref[...])
     standard, spread = standardize(x_ref[...].astype(F32))
@@ -427,35 +424,54 @@
 
 
 def backward(
-    core, tokens, projected, grads, share_parts, rounded, norm, gain, w_flipped, block, count, owners
+    core,
+    index,
+    tokens,
+    projected,
+    gathered,
+    share_parts,
+    rounded,
+    norm,
+    gain,
+    w_flipped,
+    block,
+    count,
+    owners,
 ):
-    rows, width = grads.shape
+    rows, width = tokens.shape
     half = jax.ShapeDtypeStruct((rows, 3 * width // 2), BF16)
     return pl.pallas_call(
         lambda *refs: backward_kernel(block, count, *refs),
-        in_specs=[SMEM] + [VMEM] * 7 + [HBM],
+        in_specs=[SMEM, SMEM, HBM, HBM, HBM, VMEM, HBM, VMEM, VMEM, HBM],
         out_specs=[HBM, HBM, VMEM, VMEM],
         out_shape=(
             half,
             half,
-            jax.ShapeDtypeStruct((owners, PARTS, rows // (owners * PARTS), width), BF16),
+            far_shape((owners, PARTS, rows // (owners * PARTS), width), BF16),
             jax.ShapeDtypeStruct((8, width // 8), F32),
         ),
         scratch_shapes=[
             pltpu.VMEM((rows, 3 * width), BF16),
             pltpu.VMEM((2, rows, 3 * width // 2), BF16),
             pltpu.VMEM(w_flipped.shape, BF16),
-            pltpu.SemaphoreType.DMA((3,)),
+            pltpu.VMEM(gathered.shape[:1] + gathered.shape[2:], BF16),
+            pltpu.VMEM((rows, width), BF16),
+            pltpu.VMEM(tokens.shape, BF16),
+            pltpu.VMEM(projected.shape, BF16),
+            pltpu.VMEM(rounded.shape, BF16),
+            pltpu.SemaphoreType.DMA((5,)),
+            pltpu.SemaphoreType.DMA((HEADS // 2, 2)),
         ],
-        compiler_params=params(56),
+        compiler_params=params(52),
         cost_estimate=cost(14 * rows * rows * width, 12 * MIB),
     )(
         core,
-        tokens,
-        projected,
-        grads,
+        index,
+        far(tokens),
+        far(projected),
+        far(gathered),
         share_parts,
-        rounded,
+        far(rounded),
         norm,
         gain,
         far(w_flipped),
@@ -467,59 +483,60 @@
     return jnp.concatenate([high, tiles - high], axis=0).astype(BF16)
 
 
-def weight_kernel(halves, flipped, grad_ref, other_grad_ref, *refs):
-    *gain_refs, out_hbm, staged, sent = refs
-    groups, _, lanes = out_hbm.shape
-    steps = sent.shape[0] - 1
-    cols = grad_ref.shape[1] // steps
+def weight_kernel(
+    halves, flipped, grad_hbm, other_ref, gain_hbm, other_gain, out_ref, grad_ref, gain_ref, arrived
+):
+    groups, total_rows, lanes = out_ref.shape
+    width = flipped.shape[0]
+    rows, cols = grad_ref.shape
+    block = width // (groups * halves)
+    steps = arrived.shape[0] - 1
+    cols = cols // steps
     tiles = cols // lanes
-    block = flipped.shape[0] // (groups * halves)
     span = tiles * halves * block
-    copies = []
-    for step in range(steps):
-        at = pl.ds(step * cols, cols)
-        both = jnp.concatenate([grad_ref[:, at], other_grad_ref[:, at]], axis=0)
+    spans = [pl.ds(step * cols, cols) for step in range(steps)]
+    loads = [
+        pltpu.make_async_copy(grad_hbm.at[:, at], grad_ref.at[:, at], arrived.at[step])
+        for step, at in enumerate(spans)
+    ]
+    loads.append(pltpu.make_async_copy(gain_hbm, gain_ref, arrived.at[steps]))
+    for load in loads:
+        load.start()
+    for step, at in enumerate(spans):
+        loads[step].wait()
+        both = jnp.concatenate([grad_ref[:, at], other_ref[:, at]], axis=0)
         terms = dot(flipped[...], both).astype(BF16)
         for tile in range(tiles):
             for half in range(halves):
                 for group in range(groups):
                     start = (half * groups + group) * block
                     place = step * span + (tile * halves + half) * block
-                    staged[group, place : place + block] = terms[
+                    out_ref[group, place : place + block] = terms[
                         start : start + block, tile * lanes : (tile + 1) * lanes
                     ]
-        part = pl.ds(step * span, span)
-        copies.append(
-            pltpu.make_async_copy(staged.at[:, part], out_hbm.at[:, part], sent.at[step])
-        )
-        copies[-1].start()
-    if gain_refs:
-        gains = split_sum(gain_refs[0][...] + gain_refs[1][...])
-        for group in range(groups):
-            staged[group, steps * span :] = gains
-        part = pl.ds(steps * span, 16)
-        copies.append(
-            pltpu.make_async_copy(staged.at[:, part], out_hbm.at[:, part], sent.at[steps])
-        )
-        copies[-1].start()
-    for copy in copies:
-        copy.wait()
-
-
-def weight_terms(flipped, grads, other_grads, gains, groups, halves, steps):
+    loads[steps].wait()
+    tail = split_sum(gain_ref[...] + other_gain[...])
+    for group in range(groups):
+        out_ref[group, steps * span :] = tail
+
+
+def weight_terms(flipped, grads, other_grads, gain, other_gain, groups, halves, steps):
     width, rows = flipped.shape
     lanes = 128
-    extra = 16 if gains else 0
-    shape = (groups, width // groups * grads.shape[1] // lanes + extra, lanes)
+    shape = (groups, width // groups * grads.shape[1] // lanes + 16, lanes)
     return pl.pallas_call(
         lambda *refs: weight_kernel(halves, *refs),
-        in_specs=[VMEM] * (3 + len(gains)),
-        out_specs=HBM,
-        out_shape=jax.ShapeDtypeStruct(shape, BF16),
-        scratch_shapes=[pltpu.VMEM(shape, BF16), pltpu.SemaphoreType.DMA((steps + 1,))],
+        in_specs=[VMEM, HBM, VMEM, HBM, VMEM],
+        out_specs=VMEM,
+        out_shape=near_shape(shape, BF16),
+        scratch_shapes=[
+            pltpu.VMEM(grads.shape, BF16),
+            pltpu.VMEM(gain.shape, F32),
+            pltpu.SemaphoreType.DMA((steps + 1,)),
+        ],
         compiler_params=params(24),
         cost_estimate=cost(2 * rows * width * grads.shape[1], 6 * MIB),
-    )(flipped, grads, other_grads, *gains)
+    )(flipped, far(grads), other_grads, far(gain), other_gain)
 
 
 def regroup_kernel(block, terms_ref, out_ref):
@@ -693,24 +710,23 @@
     block_rows = width // clip_count
     gain = ln_gain[None, :]
 
-    w_near = fetch(w_project)
+    w_flipped = flip(w_project)
     tokens = to_each(pack(clip_tokens[0], frame_count), FRAME)
-    out_grad, tokens, w_near = lax.optimization_barrier((out_grad, tokens, w_near))
+    out_grad, tokens, w_flipped = lax.optimization_barrier((out_grad, tokens, w_flipped))
     gathered = lax.all_gather(out_grad[0], FRAME, axis=0, tiled=True)
     tokens, normed, projected, pool_parts = forward(
-        tokens, gain, w_near, patches_dev, halves * frame_count
+        tokens, gain, w_project, patches_dev, halves * frame_count
     )
     other_normed = lax.ppermute(normed, "core", SWAP)
 
     pool_parts = to_each(pool_parts, ("zh",) + FRAME)
     pooled = to_each(pool(pool_parts, halves, tokens_clip, plane), ("x", "y"))
     rounded, norm = attend(projected, patches_dev)
-    flipped = flip(normed, other_normed)
-    pooled, rounded, norm, flipped = lax.optimization_barrier((pooled, rounded, norm, flipped))
+    pooled, rounded, norm = lax.optimization_barrier((pooled, rounded, norm))
     pooled_all, centered, gram_parts = embed(pooled, w_expand, frame_count, halves)
     gram_parts = to_each(gram_parts, FRAME)
-    w_flipped = flip(w_project)
-    gram_parts, w_flipped = lax.optimization_barrier((gram_parts, w_flipped))
+    flipped = flip(normed, other_normed)
+    gram_parts, flipped = lax.optimization_barrier((gram_parts, flipped))
     coefficient = 100.0 * tokens_clip / (w_expand.shape[1] * frame_count * (clip_count - 1))
     embed_grad, share_parts = embed_grads(
         own_clip.reshape(1), gram_parts, centered, w_expand, coefficient
@@ -721,13 +737,13 @@
 
     gathered, _ = lax.optimization_barrier((gathered, gram_parts))
     gathered = gathered.reshape(-1, frame_count, patches_dev, width)
-    grads = merge(own_frame, gathered, frame_count).reshape(rows, width)
 
     kept, outgoing, token_part, gain_part = backward(
         core,
+        own_frame,
         tokens,
         projected,
-        grads,
+        gathered,
         share_parts,
         rounded,
         norm,
@@ -740,7 +756,7 @@
     token_parts = lax.all_gather(token_part, FRAME)
     incoming, other_gain = lax.ppermute((outgoing, gain_part), "core", SWAP)
     terms = weight_terms(
-        flipped, kept, incoming, (gain_part, other_gain), plane, halves, steps
+        flipped, kept, incoming, gain_part, other_gain, plane, halves, steps
     )
     terms = to_each(terms, ("x", "y"))
     terms = regroup(terms, halves, steps, block_rows)

time: 178 us -> 176 us (0.989)
  waiting for transfers between devices: 22.7 us -> 29.6 us
  local copies, waits for them, and re-layouts: 9.48 us -> 2.78 us
    unnamed x20 -> x16, local copies, waits for them, and re-layouts: 9.48 us -> 2.78 us
    all_gather x1, waiting for transfers between devices: 2.38 us -> 6.91 us  [per_device(): gathered = lax.all_gather(out_grad[0], FRAME, axis=0, tiled=True)]
    pallas_call x2 -> x0, Pallas kernels: 4 us -> none  [the longest x1 2.8 us: fetch(): pl.pallas_call(fetch_kernel, in_specs=[HBM], out_specs=VMEM, out_shape=ne...]
    all_to_all x5, waiting for transfers between devices: 18.3 us -> 20.8 us  [to_each(): return lax.all_to_all(array, axis, split_axis=0, concat_axis=0, tiled=True)]
    pallas_call x1, Pallas kernels: 3.61 us -> 6.03 us  [forward(): pl.pallas_call(lambda *refs: forward_kernel(patches, *refs), in_specs=[VM...]
  transfers between devices with their start and end apart: 10 -> 10, of which waited for: 5 -> 6; matrix products, arithmetic and copies ran while one was open for 1% -> 1% of each run, Pallas kernels for 17% -> 17%
where the time goes in v4:
time: 176 us; the launch traced here: 175 us
  blocking collectives  60.6 us (34%)
  Pallas kernels  41.5 us (24%)
  waiting for transfers between devices  29.6 us (17%)
  starting transfers between devices  25.3 us (14%)
  between operations  14.2 us (8%)
  local copies, waits for them, and re-layouts  2.78 us (2%)
    all_to_all x2, blocking collectives, to_each(): return lax.all_to_all(array, axis, split_axis=0, concat_axis=0, tiled=True)  60.6 us
    all_to_all x5, starting transfers between devices, to_each(): return lax.all_to_all(array, axis, split_axis=0, concat_axis=0, tiled=True)  24.3 us
    all_to_all x5, waiting for transfers between devices, to_each(): return lax.all_to_all(array, axis, split_axis=0, concat_axis=0, tiled=True)  20.8 us
    pallas_call x1, Pallas kernels, backward(): pl.pallas_call(lambda *refs: backward_kernel(block, count, *refs), in_spe...  10.1 us
    pallas_call x2, Pallas kernels, flip(): pl.pallas_call(flip_kernel, in_specs=[VMEM] * len(arrays), out_shape=jax....  9.76 us
    all_gather x1, waiting for transfers between devices, per_device(): gathered = lax.all_gather(out_grad[0], FRAME, axis=0, tiled=True)  6.91 us
    pallas_call x1, Pallas kernels, forward(): pl.pallas_call(lambda *refs: forward_kernel(patches, *refs), in_specs=[VM...  6.03 us
    pallas_call x1, Pallas kernels, weight_terms(): pl.pallas_call(lambda *refs: weight_kernel(halves, *refs), in_specs=[VMEM...  3.82 us
  transfers between devices with their start and end apart: 10, of which 6 were waited for; matrix products, arithmetic and copies ran while one was open for 1% of the time, Pallas kernels for 17%

profile of v4, /device:TPU:8, one launch (start us, length us, event | category | flops | bytes accessed | tf_op | source)
XLA Modules:
  0.0 174.8 jit_solution(7702519828467147953)
XLA Ops:
  7.2 1.0 copy-done.2
  9.2 5.9 %all-to-all-start = ((bf16[8,2,16,1024]{3,2,1,0:T(8,128)(2,1)}), bf16[8,2,16,1024]{3,2,1,0:T(8,128)(2,1)S(1)}, u32[]{:S(2)}, u32[]{:S(2)}) async-start(bf16[8,2,16,1024]{3,2,1,0:T(8,128)(2,1)} %shard_map.84), calls=%async_computation | async-start | bytes 1048576 | tf_op jit(solution)/shard_map/all_to_all | solution.py:694
  15.1 7.2 %shard_map.85.refs_9_ = bf16[3072,1024]{1,0:T(8,128)(2,1)} custom-call(bf16[1024,3072]{1,0:T(8,128)(2,1)} %refs_2_.1), custom_call_target="tpu_custom_call" | custom-call | bytes 12582912 | tf_op jit(solution)/shard_map/pallas_call | solution.py:254
  22.3 8.1 %all-to-all-done.refs_0_ = bf16[8,2,16,1024]{3,2,1,0:T(8,128)(2,1)S(1)} async-done(((bf16[8,2,16,1024]{3,2,1,0:T(8,128)(2,1)}), bf16[8,2,16,1024]{3,2,1,0:T(8,128)(2,1)S(1)}, u32[]{:S(2)}, u32[]{:S(2)}) %all-to-all-start) | async-done | bytes 524320 | tf_op jit(solution)/shard_map/all_to_all | solution.py:694
  30.5 6.0 %shard_map.86 = (bf16[256,1024]{1,0:T(8,128)(2,1)}, bf16[256,1024]{1,0:T(8,128)(2,1)}, bf16[8,3,256,128]{3,2,1,0:T(8,128)(2,1)}, f32[16,8,128]{2,1,0:T(8,128)S(1)}) custom-call(bf16[8,2,16,1024]{3,2,1,0:T(8,128)(2,1)S(1)} %all-to-all-done.refs_0_, f32[1,1024]{1,0:T(1,128)S(1)} %bitcast.14, bf16[1024,3072]{1,0:T(8,128)(2,1)} %refs_2_.1), custom_call_target="tpu_custom_call" | custom-call | flops 2684354560 | bytes 10485760 | tf_op jit(solution)/shard_map/pallas_call | solution.py:217
  36.6 14.4 %all_to_all.35.refs_0_ = f32[16,8,128]{2,1,0:T(8,128)S(1)} all-to-all(f32[16,8,128]{2,1,0:T(8,128)S(1)} %get-tuple-element.33), channel_id=1, replica_groups=mesh['zh'=2,'x'=4,'y'=4,'zl'=4,'core'=2] {'zh','zl','core'}, dimensions={0} | all-to-all | bytes 131072 | tf_op jit(solution)/shard_map/all_to_all | solution.py:694
  51.6 7.5 %all-to-all-start.2 = ((bf16[16,16,128]{2,1,0:T(8,128)(2,1)}), bf16[16,16,128]{2,1,0:T(8,128)(2,1)S(1)}, u32[]{:S(2)}, u32[]{:S(2)}) async-start(bf16[16,16,128]{2,1,0:T(8,128)(2,1)} %shard_map.87), calls=%async_computation.2 | async-start | bytes 131072 | tf_op jit(solution)/shard_map/all_to_all | solution.py:694
  59.0 3.5 %shard_map.88 = (bf16[8,2,256,128]{3,2,1,0:T(8,128)(2,1)}, f32[32,128]{1,0:T(8,128)}) custom-call(bf16[8,3,256,128]{3,2,1,0:T(8,128)(2,1)} %get-tuple-element.34.refs_0_.refs_3_), custom_call_target="tpu_custom_call" | custom-call | flops 16777216 | bytes 6291456 | tf_op jit(solution)/shard_map/pallas_call | solution.py:287
  62.6 2.8 %all-to-all-done.2.refs_0_ = bf16[16,16,128]{2,1,0:T(8,128)(2,1)S(1)} async-done(((bf16[16,16,128]{2,1,0:T(8,128)(2,1)}), bf16[16,16,128]{2,1,0:T(8,128)(2,1)S(1)}, u32[]{:S(2)}, u32[]{:S(2)}) %all-to-all-start.2) | async-done | bytes 65568 | tf_op jit(solution)/shard_map/all_to_all | solution.py:694
  65.4 1.4 shard_map.89
  66.8 3.3 %all-to-all-start.3 = ((f32[8,8,128]{2,1,0:T(8,128)}), f32[8,8,128]{2,1,0:T(8,128)S(1)}, u32[]{:S(2)}, u32[]{:S(2)}) async-start(f32[8,8,128]{2,1,0:T(8,128)} %get-tuple-element.38), calls=%async_computation.3 | async-start | bytes 65536 | tf_op jit(solution)/shard_map/all_to_all | solution.py:694
  71.0 2.6 %shard_map.90.refs_0_ = bf16[1024,512]{1,0:T(8,128)(2,1)} custom-call(bf16[256,1024]{1,0:T(8,128)(2,1)} %get-tuple-element.39.refs_0_, bf16[256,1024]{1,0:T(8,128)(2,1)} %copy-done.7), custom_call_target="tpu_custom_call" | custom-call | bytes 2097152 | tf_op jit(solution)/shard_map/pallas_call | solution.py:254
  73.5 2.7 %all-to-all-done.3.refs_1_ = f32[8,8,128]{2,1,0:T(8,128)S(1)} async-done(((f32[8,8,128]{2,1,0:T(8,128)}), f32[8,8,128]{2,1,0:T(8,128)S(1)}, u32[]{:S(2)}, u32[]{:S(2)}) %all-to-all-start.3) | async-done | bytes 32800 | tf_op jit(solution)/shard_map/all_to_all | solution.py:694
  76.2 1.5 shard_map.91
  77.7 3.3 %all-to-all-start.4 = ((f32[8,8,128]{2,1,0:T(8,128)}), f32[8,8,128]{2,1,0:T(8,128)S(1)}, u32[]{:S(2)}, u32[]{:S(2)}) async-start(f32[8,8,128]{2,1,0:T(8,128)} %get-tuple-element.46), calls=%async_computation.4 | async-start | bytes 65536 | tf_op jit(solution)/shard_map/all_to_all | solution.py:694
  81.3 6.9 %all-gather.5.cloned.1.call-done = bf16[1,32,64,1024]{3,2,0,1:T(8,128)(2,1)} async-done(((bf16[1,4,64,1024]{3,2,0,1:T(8,128)(2,1)}), bf16[1,32,64,1024]{3,2,0,1:T(8,128)(2,1)}) %all-gather.5.cloned.1.call-update) | async-done | bytes 4194320 | tf_op jit(solution)/shard_map/all_gather | solution.py:716
  88.2 10.1 %shard_map.92 = (bf16[256,1536]{1,0:T(8,128)(2,1)S(1)}, bf16[256,1536]{1,0:T(8,128)(2,1)S(1)}, bf16[8,2,16,1024]{3,2,1,0:T(8,128)(2,1)}, f32[8,128]{1,0:T(8,128)S(1)}) custom-call(s32[1]{0:T(128)} %bitcast.2.refs_0_, s32[1]{0:T(128)} %bitcast.3.refs_1_.index_ref, bf16[256,1024]{1,0:T(8,128)(2,1)} %get-tuple-element.41.refs_2_, ...), custom_call_target="tpu_custom_call" | custom-call | flops 939524096 | bytes 12582912 | tf_op jit(solution)/shard_map/pallas_call | solution.py:443
  99.8 1.8 %collective-permute-done.2.refs_4_ = f32[8,128]{1,0:T(8,128)S(1)} collective-permute-done((f32[8,128]{1,0:T(8,128)S(1)}, f32[8,128]{1,0:T(8,128)S(1)}, u32[]{:S(2)}, u32[]{:S(2)}) %collective-permute-start.2) | collective-permute-done | bytes 4128 | tf_op jit(solution)/shard_map/ppermute | solution.py:757
  101.6 3.8 %shard_map.93 = bf16[16,784,128]{2,1,0:T(8,128)(2,1)S(1)} custom-call(bf16[1024,512]{1,0:T(8,128)(2,1)S(1)} %copy-done.1, bf16[256,1536]{1,0:T(8,128)(2,1)} %copy-done.5, bf16[256,1536]{1,0:T(8,128)(2,1)S(1)} %collective-permute-done.1.refs_2_, f32[8,128]{1,0:T(8,128)} %copy-done.6, f32[8,128]{1,0:T(8,128)S(1)} %collective-permute-done.2.refs_4_), custom_call_target="tpu_custom_call" | custom-call | flops 1610612736 | bytes 6291456 | tf_op jit(solution)/shard_map/pallas_call | solution.py:527
  105.4 46.3 %all_to_all.36.refs_0_ = bf16[16,784,128]{2,1,0:T(8,128)(2,1)S(1)} all-to-all(bf16[16,784,128]{2,1,0:T(8,128)(2,1)S(1)} %shard_map.93), channel_id=1, replica_groups=mesh['zh'=2,'x'=4,'y'=4,'zl'=4,'core'=2] {'x','y'}, dimensions={0} | all-to-all | bytes 6422528 | tf_op jit(solution)/shard_map/all_to_all | solution.py:694
  151.7 1.1 shard_map.94
  152.8 4.3 %all-to-all-start.6 = ((bf16[8,112,128]{2,1,0:T(8,128)(2,1)}), bf16[8,112,128]{2,1,0:T(8,128)(2,1)S(1)}, u32[]{:S(2)}, u32[]{:S(2)}) async-start(bf16[8,112,128]{2,1,0:T(8,128)(2,1)} %bitcast.8), calls=%async_computation.6 | async-start | bytes 458752 | tf_op jit(solution)/shard_map/all_to_all | solution.py:694
  158.1 2.0 %shard_map.95 = bf16[4,8,8,1024]{3,2,1,0:T(8,128)(2,1)} custom-call(s32[1]{0:T(128)} %bitcast.3.refs_1_.index_ref, bf16[8,8,2,16,1024]{4,3,2,1,0:T(8,128)(2,1)} %bitcast.17), custom_call_target="tpu_custom_call" | custom-call | bytes 1048576 | tf_op jit(solution)/shard_map/pallas_call | solution.py:94
  160.1 7.3 %all-to-all-done.6.terms_ref = bf16[8,112,128]{2,1,0:T(8,128)(2,1)S(1)} async-done(((bf16[8,112,128]{2,1,0:T(8,128)(2,1)}), bf16[8,112,128]{2,1,0:T(8,128)(2,1)S(1)}, u32[]{:S(2)}, u32[]{:S(2)}) %all-to-all-start.6) | async-done | bytes 229408 | tf_op jit(solution)/shard_map/all_to_all | solution.py:694
  (30 shorter events, 5.9 us)
Async XLA Ops:
  7.2 1.0 copy-start.2
  9.2 21.3 %all-to-all-start = ((bf16[8,2,16,1024]{3,2,1,0:T(8,128)(2,1)}), bf16[8,2,16,1024]{3,2,1,0:T(8,128)(2,1)S(1)}, u32[]{:S(2)}, u32[]{:S(2)}) async-start(bf16[8,2,16,1024]{3,2,1,0:T(8,128)(2,1)} %shard_map.84), calls=%async_computation | async-start | bytes 1048576 | tf_op jit(solution)/shard_map/all_to_all | solution.py:694
  15.1 15.4 %copy-start.4 = (f32[1024]{0:T(1024)S(1)}, f32[1024]{0:T(1024)}, u32[]{:S(2)}) copy-start(f32[1024]{0:T(1024)} %param.7) | copy-start | bytes 12292
  15.1 73.1 %all-gather.5.cloned.1.call-start = ((), (), s32[]{:S(2)}) async-start(), calls=%async_computation.7 | async-start | bytes 4718592 | tf_op jit(solution)/shard_map/all_gather | solution.py:716
  30.5 34.9 %copy-start = (bf16[1024,1024]{1,0:T(8,128)(2,1)S(1)}, bf16[1024,1024]{1,0:T(8,128)(2,1)}, u32[]{:S(2)}) copy-start(bf16[1024,1024]{1,0:T(8,128)(2,1)} %refs_3_.1) | copy-start | bytes 6291460
  36.5 33.6 %collective-permute-start = (bf16[256,1024]{1,0:T(8,128)(2,1)}, bf16[256,1024]{1,0:T(8,128)(2,1)S(1)}, u32[]{:S(2)}, u32[]{:S(2)}) collective-permute-start(bf16[256,1024]{1,0:T(8,128)(2,1)} %get-tuple-element.39.refs_0_), channel_id=1, source_target_pairs={{0,1},{1,0},{2,3},{3,2},{4,5},{5,4},{6,7},{7,6},{8,9},{9,8},{10,11... | collective-permute-start | bytes 1572872 | tf_op jit(solution)/shard_map/ppermute | solution.py:720
  51.6 13.8 %all-to-all-start.2 = ((bf16[16,16,128]{2,1,0:T(8,128)(2,1)}), bf16[16,16,128]{2,1,0:T(8,128)(2,1)S(1)}, u32[]{:S(2)}, u32[]{:S(2)}) async-start(bf16[16,16,128]{2,1,0:T(8,128)(2,1)} %shard_map.87), calls=%async_computation.2 | async-start | bytes 131072 | tf_op jit(solution)/shard_map/all_to_all | solution.py:694
  62.6 25.6 %copy-start.3 = (f32[32,128]{1,0:T(8,128)S(1)}, f32[32,128]{1,0:T(8,128)}, u32[]{:S(2)}) copy-start(f32[32,128]{1,0:T(8,128)} %get-tuple-element.48.refs_7_) | copy-start | bytes 49156
  66.8 9.4 %all-to-all-start.3 = ((f32[8,8,128]{2,1,0:T(8,128)}), f32[8,8,128]{2,1,0:T(8,128)S(1)}, u32[]{:S(2)}, u32[]{:S(2)}) async-start(f32[8,8,128]{2,1,0:T(8,128)} %get-tuple-element.38), calls=%async_computation.3 | async-start | bytes 65536 | tf_op jit(solution)/shard_map/all_to_all | solution.py:694
  70.1 0.8 copy-start.7
  77.7 10.5 %all-to-all-start.4 = ((f32[8,8,128]{2,1,0:T(8,128)}), f32[8,8,128]{2,1,0:T(8,128)S(1)}, u32[]{:S(2)}, u32[]{:S(2)}) async-start(f32[8,8,128]{2,1,0:T(8,128)} %get-tuple-element.46), calls=%async_computation.4 | async-start | bytes 65536 | tf_op jit(solution)/shard_map/all_to_all | solution.py:694
  81.0 77.0 %all-gather.7.cloned.1.call-start = ((), (), s32[]{:S(2)}) async-start(), calls=%async_computation.8 | async-start | bytes 4718592 | tf_op jit(solution)/shard_map/all_gather | solution.py:756
  88.2 13.4 %copy-start.1 = (bf16[1024,512]{1,0:T(8,128)(2,1)S(1)}, bf16[1024,512]{1,0:T(8,128)(2,1)}, u32[]{:S(2)}) copy-start(bf16[1024,512]{1,0:T(8,128)(2,1)} %shard_map.90.refs_0_) | copy-start | bytes 3145732
  98.3 0.9 copy-start.5
  99.2 2.4 %copy-start.6 = (f32[8,128]{1,0:T(8,128)}, f32[8,128]{1,0:T(8,128)S(1)}, u32[]{:S(2)}) copy-start(f32[8,128]{1,0:T(8,128)S(1)} %get-tuple-element.52.refs_3_) | copy-start | bytes 12292
  99.2 2.4 %collective-permute-start.1 = (bf16[256,1536]{1,0:T(8,128)(2,1)S(1)}, bf16[256,1536]{1,0:T(8,128)(2,1)S(1)}, u32[]{:S(2)}, u32[]{:S(2)}) collective-permute-start(bf16[256,1536]{1,0:T(8,128)(2,1)S(1)} %get-tuple-element.51), channel_id=1, source_target_pairs={{0,1},{1,0},{2,3},{3,2},{4,5},{5,4},{6,7},{7,6},{8,9},{9,8},{10,11... | collective-permute-start | bytes 2359304 | tf_op jit(solution)/shard_map/ppermute | solution.py:757
  99.3 2.3 %collective-permute-start.2 = (f32[8,128]{1,0:T(8,128)S(1)}, f32[8,128]{1,0:T(8,128)S(1)}, u32[]{:S(2)}, u32[]{:S(2)}) collective-permute-start(f32[8,128]{1,0:T(8,128)S(1)} %get-tuple-element.52.refs_3_), channel_id=1, source_target_pairs={{0,1},{1,0},{2,3},{3,2},{4,5},{5,4},{6,7},{7,6},{8,9},{9,8},{10,11... | collective-permute-start | bytes 12296 | tf_op jit(solution)/shard_map/ppermute | solution.py:757
  152.8 14.5 %all-to-all-start.6 = ((bf16[8,112,128]{2,1,0:T(8,128)(2,1)}), bf16[8,112,128]{2,1,0:T(8,128)(2,1)S(1)}, u32[]{:S(2)}, u32[]{:S(2)}) async-start(bf16[8,112,128]{2,1,0:T(8,128)(2,1)} %bitcast.8), calls=%async_computation.6 | async-start | bytes 458752 | tf_op jit(solution)/shard_map/all_to_all | solution.py:694
Sparse Core Ops, SparseCore 0:
  30.6 57.5 all-gather.4
  99.3 53.2 all-gather.6

commit v5 on v4

--- a/solution.py
+++ b/solution.py
@@ -484,26 +484,17 @@
 
 
 def weight_kernel(
-    halves, flipped, grad_hbm, other_ref, gain_hbm, other_gain, out_ref, grad_ref, gain_ref, arrived
+    halves, steps, flipped, grad_ref, other_ref, gain_ref, other_gain, out_ref
 ):
     groups, total_rows, lanes = out_ref.shape
     width = flipped.shape[0]
     rows, cols = grad_ref.shape
     block = width // (groups * halves)
-    steps = arrived.shape[0] - 1
     cols = cols // steps
     tiles = cols // lanes
     span = tiles * halves * block
     spans = [pl.ds(step * cols, cols) for step in range(steps)]
-    loads = [
-        pltpu.make_async_copy(grad_hbm.at[:, at], grad_ref.at[:, at], arrived.at[step])
-        for step, at in enumerate(spans)
-    ]
-    loads.append(pltpu.make_async_copy(gain_hbm, gain_ref, arrived.at[steps]))
-    for load in loads:
-        load.start()
     for step, at in enumerate(spans):
-        loads[step].wait()
         both = jnp.concatenate([grad_ref[:, at], other_ref[:, at]], axis=0)
         terms = dot(flipped[...], both).astype(BF16)
         for tile in range(tiles):
@@ -514,7 +505,6 @@
                     out_ref[group, place : place + block] = terms[
                         start : start + block, tile * lanes : (tile + 1) * lanes
                     ]
-    loads[steps].wait()
     tail = split_sum(gain_ref[...] + other_gain[...])
     for group in range(groups):
         out_ref[group, steps * span :] = tail
@@ -525,18 +515,13 @@
     lanes = 128
     shape = (groups, width // groups * grads.shape[1] // lanes + 16, lanes)
     return pl.pallas_call(
-        lambda *refs: weight_kernel(halves, *refs),
-        in_specs=[VMEM, HBM, VMEM, HBM, VMEM],
+        lambda *refs: weight_kernel(halves, steps, *refs),
+        in_specs=[VMEM] * 5,
         out_specs=VMEM,
         out_shape=near_shape(shape, BF16),
-        scratch_shapes=[
-            pltpu.VMEM(grads.shape, BF16),
-            pltpu.VMEM(gain.shape, F32),
-            pltpu.SemaphoreType.DMA((steps + 1,)),
-        ],
         compiler_params=params(24),
         cost_estimate=cost(2 * rows * width * grads.shape[1], 6 * MIB),
-    )(flipped, far(grads), other_grads, far(gain), other_gain)
+    )(flipped, grads, other_grads, gain, other_gain)
 
 
 def regroup_kernel(block, terms_ref, out_ref):

time: 176 us -> 173 us (0.983)
  transfers between devices with their start and end apart: 10 -> 10, of which waited for: 6 -> 6; matrix products, arithmetic and copies ran while one was open for 1% -> 1% of each run, Pallas kernels for 17% -> 16%
where the time goes in v5:
time: 173 us; the launch traced here: 172 us
  blocking collectives  60.7 us (35%)
  Pallas kernels  40 us (23%)
  waiting for transfers between devices  29.5 us (17%)
  starting transfers between devices  25.3 us (15%)
  between operations  14.2 us (8%)
  local copies, waits for them, and re-layouts  1.86 us (1%)
    all_to_all x2, blocking collectives, to_each(): return lax.all_to_all(array, axis, split_axis=0, concat_axis=0, tiled=True)  60.7 us
    all_to_all x5, starting transfers between devices, to_each(): return lax.all_to_all(array, axis, split_axis=0, concat_axis=0, tiled=True)  24.3 us
    all_to_all x5, waiting for transfers between devices, to_each(): return lax.all_to_all(array, axis, split_axis=0, concat_axis=0, tiled=True)  20.8 us
    pallas_call x1, Pallas kernels, backward(): pl.pallas_call(lambda *refs: backward_kernel(block, count, *refs), in_spe...  10.1 us
    pallas_call x2, Pallas kernels, flip(): pl.pallas_call(flip_kernel, in_specs=[VMEM] * len(arrays), out_shape=jax....  9.7 us
    all_gather x1, waiting for transfers between devices, per_device(): gathered = lax.all_gather(out_grad[0], FRAME, axis=0, tiled=True)  6.91 us
    pallas_call x1, Pallas kernels, forward(): pl.pallas_call(lambda *refs: forward_kernel(patches, *refs), in_specs=[VM...  6.03 us
    pallas_call x1, Pallas kernels, attend(): pl.pallas_call(lambda *refs: attend_kernel(patches, *refs), in_specs=[VME...  3.61 us
  transfers between devices with their start and end apart: 10, of which 6 were waited for; matrix products, arithmetic and copies ran while one was open for 1% of the time, Pallas kernels for 16%

profile of v5, /device:TPU:8, one launch (start us, length us, event | category | flops | bytes accessed | tf_op | source)
XLA Modules:
  0.0 172.4 jit_solution(6363619037518085371)
XLA Ops:
  7.2 1.0 copy-done.2
  9.2 5.9 %all-to-all-start = ((bf16[8,2,16,1024]{3,2,1,0:T(8,128)(2,1)}), bf16[8,2,16,1024]{3,2,1,0:T(8,128)(2,1)S(1)}, u32[]{:S(2)}, u32[]{:S(2)}) async-start(bf16[8,2,16,1024]{3,2,1,0:T(8,128)(2,1)} %shard_map.84), calls=%async_computation | async-start | bytes 1048576 | tf_op jit(solution)/shard_map/all_to_all | solution.py:679
  15.1 7.2 %shard_map.85.refs_9_ = bf16[3072,1024]{1,0:T(8,128)(2,1)} custom-call(bf16[1024,3072]{1,0:T(8,128)(2,1)} %refs_2_.1), custom_call_target="tpu_custom_call" | custom-call | bytes 12582912 | tf_op jit(solution)/shard_map/pallas_call | solution.py:254
  22.3 8.1 %all-to-all-done.refs_0_ = bf16[8,2,16,1024]{3,2,1,0:T(8,128)(2,1)S(1)} async-done(((bf16[8,2,16,1024]{3,2,1,0:T(8,128)(2,1)}), bf16[8,2,16,1024]{3,2,1,0:T(8,128)(2,1)S(1)}, u32[]{:S(2)}, u32[]{:S(2)}) %all-to-all-start) | async-done | bytes 524320 | tf_op jit(solution)/shard_map/all_to_all | solution.py:679
  30.5 6.0 %shard_map.86 = (bf16[256,1024]{1,0:T(8,128)(2,1)}, bf16[256,1024]{1,0:T(8,128)(2,1)}, bf16[8,3,256,128]{3,2,1,0:T(8,128)(2,1)}, f32[16,8,128]{2,1,0:T(8,128)S(1)}) custom-call(bf16[8,2,16,1024]{3,2,1,0:T(8,128)(2,1)S(1)} %all-to-all-done.refs_0_, f32[1,1024]{1,0:T(1,128)S(1)} %bitcast.14, bf16[1024,3072]{1,0:T(8,128)(2,1)} %refs_2_.1), custom_call_target="tpu_custom_call" | custom-call | flops 2684354560 | bytes 10485760 | tf_op jit(solution)/shard_map/pallas_call | solution.py:217
  36.6 14.4 %all_to_all.35.refs_0_ = f32[16,8,128]{2,1,0:T(8,128)S(1)} all-to-all(f32[16,8,128]{2,1,0:T(8,128)S(1)} %get-tuple-element.33), channel_id=1, replica_groups=mesh['zh'=2,'x'=4,'y'=4,'zl'=4,'core'=2] {'zh','zl','core'}, dimensions={0} | all-to-all | bytes 131072 | tf_op jit(solution)/shard_map/all_to_all | solution.py:679
  51.6 7.5 %all-to-all-start.2 = ((bf16[16,16,128]{2,1,0:T(8,128)(2,1)}), bf16[16,16,128]{2,1,0:T(8,128)(2,1)S(1)}, u32[]{:S(2)}, u32[]{:S(2)}) async-start(bf16[16,16,128]{2,1,0:T(8,128)(2,1)} %shard_map.87), calls=%async_computation.2 | async-start | bytes 131072 | tf_op jit(solution)/shard_map/all_to_all | solution.py:679
  59.0 3.6 %shard_map.88 = (bf16[8,2,256,128]{3,2,1,0:T(8,128)(2,1)}, f32[32,128]{1,0:T(8,128)}) custom-call(bf16[8,3,256,128]{3,2,1,0:T(8,128)(2,1)} %get-tuple-element.34.refs_0_.refs_3_), custom_call_target="tpu_custom_call" | custom-call | flops 16777216 | bytes 6291456 | tf_op jit(solution)/shard_map/pallas_call | solution.py:287
  62.7 2.7 %all-to-all-done.2.refs_0_ = bf16[16,16,128]{2,1,0:T(8,128)(2,1)S(1)} async-done(((bf16[16,16,128]{2,1,0:T(8,128)(2,1)}), bf16[16,16,128]{2,1,0:T(8,128)(2,1)S(1)}, u32[]{:S(2)}, u32[]{:S(2)}) %all-to-all-start.2) | async-done | bytes 65568 | tf_op jit(solution)/shard_map/all_to_all | solution.py:679
  65.4 1.4 shard_map.89
  66.8 3.3 %all-to-all-start.3 = ((f32[8,8,128]{2,1,0:T(8,128)}), f32[8,8,128]{2,1,0:T(8,128)S(1)}, u32[]{:S(2)}, u32[]{:S(2)}) async-start(f32[8,8,128]{2,1,0:T(8,128)} %get-tuple-element.38), calls=%async_computation.3 | async-start | bytes 65536 | tf_op jit(solution)/shard_map/all_to_all | solution.py:679
  70.9 2.5 %shard_map.90.refs_0_ = bf16[1024,512]{1,0:T(8,128)(2,1)} custom-call(bf16[256,1024]{1,0:T(8,128)(2,1)} %get-tuple-element.39.refs_0_, bf16[256,1024]{1,0:T(8,128)(2,1)} %copy-done.5), custom_call_target="tpu_custom_call" | custom-call | bytes 2097152 | tf_op jit(solution)/shard_map/pallas_call | solution.py:254
  73.4 2.7 %all-to-all-done.3.refs_1_ = f32[8,8,128]{2,1,0:T(8,128)S(1)} async-done(((f32[8,8,128]{2,1,0:T(8,128)}), f32[8,8,128]{2,1,0:T(8,128)S(1)}, u32[]{:S(2)}, u32[]{:S(2)}) %all-to-all-start.3) | async-done | bytes 32800 | tf_op jit(solution)/shard_map/all_to_all | solution.py:679
  76.2 1.5 shard_map.91
  77.7 3.3 %all-to-all-start.4 = ((f32[8,8,128]{2,1,0:T(8,128)}), f32[8,8,128]{2,1,0:T(8,128)S(1)}, u32[]{:S(2)}, u32[]{:S(2)}) async-start(f32[8,8,128]{2,1,0:T(8,128)} %get-tuple-element.46), calls=%async_computation.4 | async-start | bytes 65536 | tf_op jit(solution)/shard_map/all_to_all | solution.py:679
  81.3 6.9 %all-gather.5.cloned.1.call-done = bf16[1,32,64,1024]{3,2,0,1:T(8,128)(2,1)} async-done(((bf16[1,4,64,1024]{3,2,0,1:T(8,128)(2,1)}), bf16[1,32,64,1024]{3,2,0,1:T(8,128)(2,1)}) %all-gather.5.cloned.1.call-update) | async-done | bytes 4194320 | tf_op jit(solution)/shard_map/all_gather | solution.py:701
  88.2 10.1 %shard_map.92 = (bf16[256,1536]{1,0:T(8,128)(2,1)S(1)}, bf16[256,1536]{1,0:T(8,128)(2,1)S(1)}, bf16[8,2,16,1024]{3,2,1,0:T(8,128)(2,1)}, f32[8,128]{1,0:T(8,128)S(1)}) custom-call(s32[1]{0:T(128)} %bitcast.2.refs_0_, s32[1]{0:T(128)} %bitcast.3.refs_1_.index_ref, bf16[256,1024]{1,0:T(8,128)(2,1)} %get-tuple-element.41.refs_2_, ...), custom_call_target="tpu_custom_call" | custom-call | flops 939524096 | bytes 12582912 | tf_op jit(solution)/shard_map/pallas_call | solution.py:443
  98.9 1.8 %collective-permute-done.2.refs_4_ = f32[8,128]{1,0:T(8,128)S(1)} collective-permute-done((f32[8,128]{1,0:T(8,128)S(1)}, f32[8,128]{1,0:T(8,128)S(1)}, u32[]{:S(2)}, u32[]{:S(2)}) %collective-permute-start.2) | collective-permute-done | bytes 4128 | tf_op jit(solution)/shard_map/ppermute | solution.py:742
  100.7 2.3 %shard_map.93 = bf16[16,784,128]{2,1,0:T(8,128)(2,1)S(1)} custom-call(bf16[1024,512]{1,0:T(8,128)(2,1)S(1)} %copy-done.1, bf16[256,1536]{1,0:T(8,128)(2,1)S(1)} %get-tuple-element.50.refs_1_, bf16[256,1536]{1,0:T(8,128)(2,1)S(1)} %collective-permute-done.1.refs_2_, f32[8,128]{1,0:T(8,128)S(1)} %get-tuple-element.52.refs_3_, ...), custom_call_target="tpu_custom_call" | custom-call | flops 1610612736 | bytes 6291456 | tf_op jit(solution)/shard_map/pallas_call | solution.py:517
  103.0 46.3 %all_to_all.36.refs_0_ = bf16[16,784,128]{2,1,0:T(8,128)(2,1)S(1)} all-to-all(bf16[16,784,128]{2,1,0:T(8,128)(2,1)S(1)} %shard_map.93), channel_id=1, replica_groups=mesh['zh'=2,'x'=4,'y'=4,'zl'=4,'core'=2] {'x','y'}, dimensions={0} | all-to-all | bytes 6422528 | tf_op jit(solution)/shard_map/all_to_all | solution.py:679
  149.3 1.1 shard_map.94
  150.4 4.3 %all-to-all-start.6 = ((bf16[8,112,128]{2,1,0:T(8,128)(2,1)}), bf16[8,112,128]{2,1,0:T(8,128)(2,1)S(1)}, u32[]{:S(2)}, u32[]{:S(2)}) async-start(bf16[8,112,128]{2,1,0:T(8,128)(2,1)} %bitcast.8), calls=%async_computation.6 | async-start | bytes 458752 | tf_op jit(solution)/shard_map/all_to_all | solution.py:679
  155.7 2.0 %shard_map.95 = bf16[4,8,8,1024]{3,2,1,0:T(8,128)(2,1)} custom-call(s32[1]{0:T(128)} %bitcast.3.refs_1_.index_ref, bf16[8,8,2,16,1024]{4,3,2,1,0:T(8,128)(2,1)} %bitcast.17), custom_call_target="tpu_custom_call" | custom-call | bytes 1048576 | tf_op jit(solution)/shard_map/pallas_call | solution.py:94
  157.7 7.3 %all-to-all-done.6.terms_ref = bf16[8,112,128]{2,1,0:T(8,128)(2,1)S(1)} async-done(((bf16[8,112,128]{2,1,0:T(8,128)(2,1)}), bf16[8,112,128]{2,1,0:T(8,128)(2,1)S(1)}, u32[]{:S(2)}, u32[]{:S(2)}) %all-to-all-start.6) | async-done | bytes 229408 | tf_op jit(solution)/shard_map/all_to_all | solution.py:679
  (26 shorter events, 5.0 us)
Async XLA Ops:
  7.2 1.0 copy-start.2
  9.2 21.3 %all-to-all-start = ((bf16[8,2,16,1024]{3,2,1,0:T(8,128)(2,1)}), bf16[8,2,16,1024]{3,2,1,0:T(8,128)(2,1)S(1)}, u32[]{:S(2)}, u32[]{:S(2)}) async-start(bf16[8,2,16,1024]{3,2,1,0:T(8,128)(2,1)} %shard_map.84), calls=%async_computation | async-start | bytes 1048576 | tf_op jit(solution)/shard_map/all_to_all | solution.py:679
  15.1 15.4 %copy-start.4 = (f32[1024]{0:T(1024)S(1)}, f32[1024]{0:T(1024)}, u32[]{:S(2)}) copy-start(f32[1024]{0:T(1024)} %param.7) | copy-start | bytes 12292
  15.1 73.1 %all-gather.5.cloned.1.call-start = ((), (), s32[]{:S(2)}) async-start(), calls=%async_computation.7 | async-start | bytes 4718592 | tf_op jit(solution)/shard_map/all_gather | solution.py:701
  30.5 34.9 %copy-start = (bf16[1024,1024]{1,0:T(8,128)(2,1)S(1)}, bf16[1024,1024]{1,0:T(8,128)(2,1)}, u32[]{:S(2)}) copy-start(bf16[1024,1024]{1,0:T(8,128)(2,1)} %refs_3_.1) | copy-start | bytes 6291460
  36.5 33.6 %collective-permute-start = (bf16[256,1024]{1,0:T(8,128)(2,1)}, bf16[256,1024]{1,0:T(8,128)(2,1)S(1)}, u32[]{:S(2)}, u32[]{:S(2)}) collective-permute-start(bf16[256,1024]{1,0:T(8,128)(2,1)} %get-tuple-element.39.refs_0_), channel_id=1, source_target_pairs={{0,1},{1,0},{2,3},{3,2},{4,5},{5,4},{6,7},{7,6},{8,9},{9,8},{10,11... | collective-permute-start | bytes 1572872 | tf_op jit(solution)/shard_map/ppermute | solution.py:705
  51.6 13.8 %all-to-all-start.2 = ((bf16[16,16,128]{2,1,0:T(8,128)(2,1)}), bf16[16,16,128]{2,1,0:T(8,128)(2,1)S(1)}, u32[]{:S(2)}, u32[]{:S(2)}) async-start(bf16[16,16,128]{2,1,0:T(8,128)(2,1)} %shard_map.87), calls=%async_computation.2 | async-start | bytes 131072 | tf_op jit(solution)/shard_map/all_to_all | solution.py:679
  62.7 25.5 %copy-start.3 = (f32[32,128]{1,0:T(8,128)S(1)}, f32[32,128]{1,0:T(8,128)}, u32[]{:S(2)}) copy-start(f32[32,128]{1,0:T(8,128)} %get-tuple-element.48.refs_7_) | copy-start | bytes 49156
  66.8 9.4 %all-to-all-start.3 = ((f32[8,8,128]{2,1,0:T(8,128)}), f32[8,8,128]{2,1,0:T(8,128)S(1)}, u32[]{:S(2)}, u32[]{:S(2)}) async-start(f32[8,8,128]{2,1,0:T(8,128)} %get-tuple-element.38), calls=%async_computation.3 | async-start | bytes 65536 | tf_op jit(solution)/shard_map/all_to_all | solution.py:679
  70.1 0.8 copy-start.5
  77.7 10.5 %all-to-all-start.4 = ((f32[8,8,128]{2,1,0:T(8,128)}), f32[8,8,128]{2,1,0:T(8,128)S(1)}, u32[]{:S(2)}, u32[]{:S(2)}) async-start(f32[8,8,128]{2,1,0:T(8,128)} %get-tuple-element.46), calls=%async_computation.4 | async-start | bytes 65536 | tf_op jit(solution)/shard_map/all_to_all | solution.py:679
  81.0 74.6 %all-gather.7.cloned.1.call-start = ((), (), s32[]{:S(2)}) async-start(), calls=%async_computation.8 | async-start | bytes 4718592 | tf_op jit(solution)/shard_map/all_gather | solution.py:741
  88.2 12.5 %copy-start.1 = (bf16[1024,512]{1,0:T(8,128)(2,1)S(1)}, bf16[1024,512]{1,0:T(8,128)(2,1)}, u32[]{:S(2)}) copy-start(bf16[1024,512]{1,0:T(8,128)(2,1)} %shard_map.90.refs_0_) | copy-start | bytes 3145732
  98.3 2.4 %collective-permute-start.1 = (bf16[256,1536]{1,0:T(8,128)(2,1)S(1)}, bf16[256,1536]{1,0:T(8,128)(2,1)S(1)}, u32[]{:S(2)}, u32[]{:S(2)}) collective-permute-start(bf16[256,1536]{1,0:T(8,128)(2,1)S(1)} %get-tuple-element.51), channel_id=1, source_target_pairs={{0,1},{1,0},{2,3},{3,2},{4,5},{5,4},{6,7},{7,6},{8,9},{9,8},{10,11... | collective-permute-start | bytes 2359304 | tf_op jit(solution)/shard_map/ppermute | solution.py:742
  98.4 2.3 %collective-permute-start.2 = (f32[8,128]{1,0:T(8,128)S(1)}, f32[8,128]{1,0:T(8,128)S(1)}, u32[]{:S(2)}, u32[]{:S(2)}) collective-permute-start(f32[8,128]{1,0:T(8,128)S(1)} %get-tuple-element.52.refs_3_), channel_id=1, source_target_pairs={{0,1},{1,0},{2,3},{3,2},{4,5},{5,4},{6,7},{7,6},{8,9},{9,8},{10,11... | collective-permute-start | bytes 12296 | tf_op jit(solution)/shard_map/ppermute | solution.py:742
  150.4 14.5 %all-to-all-start.6 = ((bf16[8,112,128]{2,1,0:T(8,128)(2,1)}), bf16[8,112,128]{2,1,0:T(8,128)(2,1)S(1)}, u32[]{:S(2)}, u32[]{:S(2)}) async-start(bf16[8,112,128]{2,1,0:T(8,128)(2,1)} %bitcast.8), calls=%async_computation.6 | async-start | bytes 458752 | tf_op jit(solution)/shard_map/all_to_all | solution.py:679
Sparse Core Ops, SparseCore 0:
  30.6 57.5 all-gather.4
  98.4 53.2 all-gather.6

commit v6 on v5

--- a/solution.py
+++ b/solution.py
@@ -255,7 +255,7 @@
         flip_kernel,
         in_specs=[VMEM] * len(arrays),
         out_shape=jax.ShapeDtypeStruct(shape, BF16),
-        compiler_params=params(56),
+        compiler_params=params(50),
         cost_estimate=cost(0, 4 * shape[0] * shape[1]),
     )(*arrays)
 
@@ -291,7 +291,7 @@
             jax.ShapeDtypeStruct((pairs, PARTS, 2 * rows, rows), BF16),
             jax.ShapeDtypeStruct((HEADS * PARTS, rows), F32),
         ),
-        compiler_params=params(56),
+        compiler_params=params(50),
         cost_estimate=cost(8 * rows * rows * projected.shape[3], 6 * MIB, HEADS * rows * rows),
     )(projected)
 

time: 173 us -> 173 us (level)
  Pallas kernels: 40 us -> 35.2 us
  local copies, waits for them, and re-layouts: 1.86 us -> 6.37 us
    unnamed x12 -> x16, local copies, waits for them, and re-layouts: 1.86 us -> 6.37 us
    pallas_call x1, Pallas kernels: 3.61 us -> 1.13 us  [attend(): pl.pallas_call(lambda *refs: attend_kernel(patches, *refs), in_specs=[VME...]
    pallas_call x2, Pallas kernels: 9.7 us -> 7.52 us  [flip(): pl.pallas_call(flip_kernel, in_specs=[VMEM] * len(arrays), out_shape=jax....]
  transfers between devices with their start and end apart: 10 -> 10, of which waited for: 6 -> 6; matrix products, arithmetic and copies ran while one was open for 1% -> 1% of each run, Pallas kernels for 16% -> 14%
where the time goes in v6:
time: 173 us; the launch traced here: 172 us
  blocking collectives  60.7 us (35%)
  Pallas kernels  35.2 us (20%)
  waiting for transfers between devices  29.6 us (17%)
  starting transfers between devices  25.3 us (15%)
  between operations  14.2 us (8%)
  local copies, waits for them, and re-layouts  6.37 us (4%)
    all_to_all x2, blocking collectives, to_each(): return lax.all_to_all(array, axis, split_axis=0, concat_axis=0, tiled=True)  60.7 us
    all_to_all x5, starting transfers between devices, to_each(): return lax.all_to_all(array, axis, split_axis=0, concat_axis=0, tiled=True)  24.4 us
    all_to_all x5, waiting for transfers between devices, to_each(): return lax.all_to_all(array, axis, split_axis=0, concat_axis=0, tiled=True)  20.9 us
    pallas_call x1, Pallas kernels, backward(): pl.pallas_call(lambda *refs: backward_kernel(block, count, *refs), in_spe...  9.97 us
    pallas_call x2, Pallas kernels, flip(): pl.pallas_call(flip_kernel, in_specs=[VMEM] * len(arrays), out_shape=jax....  7.52 us
    all_gather x1, waiting for transfers between devices, per_device(): gathered = lax.all_gather(out_grad[0], FRAME, axis=0, tiled=True)  6.91 us
    unnamed x16, local copies, waits for them, and re-layouts  6.37 us
    pallas_call x1, Pallas kernels, forward(): pl.pallas_call(lambda *refs: forward_kernel(patches, *refs), in_specs=[VM...  6.03 us
  transfers between devices with their start and end apart: 10, of which 6 were waited for; matrix products, arithmetic and copies ran while one was open for 1% of the time, Pallas kernels for 14%

profile of v6, /device:TPU:8, one launch (start us, length us, event | category | flops | bytes accessed | tf_op | source)
XLA Modules:
  0.0 172.3 jit_solution(11535417071405167423)
XLA Ops:
  9.2 5.9 %all-to-all-start = ((bf16[8,2,16,1024]{3,2,1,0:T(8,128)(2,1)}), bf16[8,2,16,1024]{3,2,1,0:T(8,128)(2,1)S(1)}, u32[]{:S(2)}, u32[]{:S(2)}) async-start(bf16[8,2,16,1024]{3,2,1,0:T(8,128)(2,1)} %shard_map.84), calls=%async_computation | async-start | bytes 1048576 | tf_op jit(solution)/shard_map/all_to_all | solution.py:679
  15.1 7.2 %shard_map.85.refs_9_ = bf16[3072,1024]{1,0:T(8,128)(2,1)} custom-call(bf16[1024,3072]{1,0:T(8,128)(2,1)} %refs_2_.1), custom_call_target="tpu_custom_call" | custom-call | bytes 12582912 | tf_op jit(solution)/shard_map/pallas_call | solution.py:254
  22.3 8.1 %all-to-all-done.refs_0_ = bf16[8,2,16,1024]{3,2,1,0:T(8,128)(2,1)S(1)} async-done(((bf16[8,2,16,1024]{3,2,1,0:T(8,128)(2,1)}), bf16[8,2,16,1024]{3,2,1,0:T(8,128)(2,1)S(1)}, u32[]{:S(2)}, u32[]{:S(2)}) %all-to-all-start) | async-done | bytes 524320 | tf_op jit(solution)/shard_map/all_to_all | solution.py:679
  30.5 6.0 %shard_map.86 = (bf16[256,1024]{1,0:T(8,128)(2,1)}, bf16[256,1024]{1,0:T(8,128)(2,1)}, bf16[8,3,256,128]{3,2,1,0:T(8,128)(2,1)}, f32[16,8,128]{2,1,0:T(8,128)S(1)}) custom-call(bf16[8,2,16,1024]{3,2,1,0:T(8,128)(2,1)S(1)} %all-to-all-done.refs_0_, f32[1,1024]{1,0:T(1,128)S(1)} %bitcast.14, bf16[1024,3072]{1,0:T(8,128)(2,1)} %refs_2_.1), custom_call_target="tpu_custom_call" | custom-call | flops 2684354560 | bytes 10485760 | tf_op jit(solution)/shard_map/pallas_call | solution.py:217
  36.6 14.4 %all_to_all.35.refs_0_ = f32[16,8,128]{2,1,0:T(8,128)S(1)} all-to-all(f32[16,8,128]{2,1,0:T(8,128)S(1)} %get-tuple-element.33), channel_id=1, replica_groups=mesh['zh'=2,'x'=4,'y'=4,'zl'=4,'core'=2] {'zh','zl','core'}, dimensions={0} | all-to-all | bytes 131072 | tf_op jit(solution)/shard_map/all_to_all | solution.py:679
  51.6 7.5 %all-to-all-start.2 = ((bf16[16,16,128]{2,1,0:T(8,128)(2,1)}), bf16[16,16,128]{2,1,0:T(8,128)(2,1)S(1)}, u32[]{:S(2)}, u32[]{:S(2)}) async-start(bf16[16,16,128]{2,1,0:T(8,128)(2,1)} %shard_map.87), calls=%async_computation.2 | async-start | bytes 131072 | tf_op jit(solution)/shard_map/all_to_all | solution.py:679
  59.1 1.4 copy-done.1
  60.5 1.1 shard_map.88
  62.6 2.7 %all-to-all-done.2.refs_0_ = bf16[16,16,128]{2,1,0:T(8,128)(2,1)S(1)} async-done(((bf16[16,16,128]{2,1,0:T(8,128)(2,1)}), bf16[16,16,128]{2,1,0:T(8,128)(2,1)S(1)}, u32[]{:S(2)}, u32[]{:S(2)}) %all-to-all-start.2) | async-done | bytes 65568 | tf_op jit(solution)/shard_map/all_to_all | solution.py:679
  65.4 1.4 shard_map.89
  66.8 3.3 %all-to-all-start.3 = ((f32[8,8,128]{2,1,0:T(8,128)}), f32[8,8,128]{2,1,0:T(8,128)S(1)}, u32[]{:S(2)}, u32[]{:S(2)}) async-start(f32[8,8,128]{2,1,0:T(8,128)} %get-tuple-element.38), calls=%async_computation.3 | async-start | bytes 65536 | tf_op jit(solution)/shard_map/all_to_all | solution.py:679
  72.0 1.0 copy-done.6
  73.3 2.8 %all-to-all-done.3.refs_1_ = f32[8,8,128]{2,1,0:T(8,128)S(1)} async-done(((f32[8,8,128]{2,1,0:T(8,128)}), f32[8,8,128]{2,1,0:T(8,128)S(1)}, u32[]{:S(2)}, u32[]{:S(2)}) %all-to-all-start.3) | async-done | bytes 32800 | tf_op jit(solution)/shard_map/all_to_all | solution.py:679
  76.2 1.5 shard_map.91
  77.7 3.3 %all-to-all-start.4 = ((f32[8,8,128]{2,1,0:T(8,128)}), f32[8,8,128]{2,1,0:T(8,128)S(1)}, u32[]{:S(2)}, u32[]{:S(2)}) async-start(f32[8,8,128]{2,1,0:T(8,128)} %get-tuple-element.46), calls=%async_computation.4 | async-start | bytes 65536 | tf_op jit(solution)/shard_map/all_to_all | solution.py:679
  81.3 6.9 %all-gather.5.cloned.1.call-done = bf16[1,32,64,1024]{3,2,0,1:T(8,128)(2,1)} async-done(((bf16[1,4,64,1024]{3,2,0,1:T(8,128)(2,1)}), bf16[1,32,64,1024]{3,2,0,1:T(8,128)(2,1)}) %all-gather.5.cloned.1.call-update) | async-done | bytes 4194320 | tf_op jit(solution)/shard_map/all_gather | solution.py:701
  88.2 10.0 %shard_map.92 = (bf16[256,1536]{1,0:T(8,128)(2,1)S(1)}, bf16[256,1536]{1,0:T(8,128)(2,1)S(1)}, bf16[8,2,16,1024]{3,2,1,0:T(8,128)(2,1)}, f32[8,128]{1,0:T(8,128)S(1)}) custom-call(s32[1]{0:T(128)} %bitcast.2.refs_0_, s32[1]{0:T(128)} %bitcast.3.refs_1_.index_ref, bf16[256,1024]{1,0:T(8,128)(2,1)} %get-tuple-element.41.refs_2_, ...), custom_call_target="tpu_custom_call" | custom-call | flops 939524096 | bytes 12582912 | tf_op jit(solution)/shard_map/pallas_call | solution.py:443
  98.8 1.8 %collective-permute-done.2.refs_4_ = f32[8,128]{1,0:T(8,128)S(1)} collective-permute-done((f32[8,128]{1,0:T(8,128)S(1)}, f32[8,128]{1,0:T(8,128)S(1)}, u32[]{:S(2)}, u32[]{:S(2)}) %collective-permute-start.2) | collective-permute-done | bytes 4128 | tf_op jit(solution)/shard_map/ppermute | solution.py:742
  100.6 2.3 %shard_map.93 = bf16[16,784,128]{2,1,0:T(8,128)(2,1)S(1)} custom-call(bf16[1024,512]{1,0:T(8,128)(2,1)S(1)} %shard_map.90.refs_0_, bf16[256,1536]{1,0:T(8,128)(2,1)S(1)} %get-tuple-element.50.refs_1_, bf16[256,1536]{1,0:T(8,128)(2,1)S(1)} %collective-permute-done.1.refs_2_, f32[8,128]{1,0:T(8,128)S(1)} %get-tuple-element.52.refs_3_, ...), custom_call_target="tpu_custom_call" | custom-call | flops 1610612736 | bytes 6291456 | tf_op jit(solution)/shard_map/pallas_call | solution.py:517
  102.9 46.3 %all_to_all.36.refs_0_ = bf16[16,784,128]{2,1,0:T(8,128)(2,1)S(1)} all-to-all(bf16[16,784,128]{2,1,0:T(8,128)(2,1)S(1)} %shard_map.93), channel_id=1, replica_groups=mesh['zh'=2,'x'=4,'y'=4,'zl'=4,'core'=2] {'x','y'}, dimensions={0} | all-to-all | bytes 6422528 | tf_op jit(solution)/shard_map/all_to_all | solution.py:679
  149.2 1.1 shard_map.94
  150.3 4.3 %all-to-all-start.6 = ((bf16[8,112,128]{2,1,0:T(8,128)(2,1)}), bf16[8,112,128]{2,1,0:T(8,128)(2,1)S(1)}, u32[]{:S(2)}, u32[]{:S(2)}) async-start(bf16[8,112,128]{2,1,0:T(8,128)(2,1)} %bitcast.8), calls=%async_computation.6 | async-start | bytes 458752 | tf_op jit(solution)/shard_map/all_to_all | solution.py:679
  155.6 2.0 %shard_map.95 = bf16[4,8,8,1024]{3,2,1,0:T(8,128)(2,1)} custom-call(s32[1]{0:T(128)} %bitcast.3.refs_1_.index_ref, bf16[8,8,2,16,1024]{4,3,2,1,0:T(8,128)(2,1)} %bitcast.17), custom_call_target="tpu_custom_call" | custom-call | bytes 1048576 | tf_op jit(solution)/shard_map/pallas_call | solution.py:94
  157.6 7.3 %all-to-all-done.6.terms_ref = bf16[8,112,128]{2,1,0:T(8,128)(2,1)S(1)} async-done(((bf16[8,112,128]{2,1,0:T(8,128)(2,1)}), bf16[8,112,128]{2,1,0:T(8,128)(2,1)S(1)}, u32[]{:S(2)}, u32[]{:S(2)}) %all-to-all-start.6) | async-done | bytes 229408 | tf_op jit(solution)/shard_map/all_to_all | solution.py:679
  (30 shorter events, 8.4 us)
Async XLA Ops:
  7.2 1.0 copy-start.3
  9.2 21.3 %all-to-all-start = ((bf16[8,2,16,1024]{3,2,1,0:T(8,128)(2,1)}), bf16[8,2,16,1024]{3,2,1,0:T(8,128)(2,1)S(1)}, u32[]{:S(2)}, u32[]{:S(2)}) async-start(bf16[8,2,16,1024]{3,2,1,0:T(8,128)(2,1)} %shard_map.84), calls=%async_computation | async-start | bytes 1048576 | tf_op jit(solution)/shard_map/all_to_all | solution.py:679
  15.1 15.4 %copy-start.7 = (f32[1024]{0:T(1024)S(1)}, f32[1024]{0:T(1024)}, u32[]{:S(2)}) copy-start(f32[1024]{0:T(1024)} %param.7) | copy-start | bytes 12292
  15.1 73.1 %all-gather.5.cloned.1.call-start = ((), (), s32[]{:S(2)}) async-start(), calls=%async_computation.7 | async-start | bytes 4718592 | tf_op jit(solution)/shard_map/all_gather | solution.py:701
  30.5 34.9 %copy-start = (bf16[1024,1024]{1,0:T(8,128)(2,1)S(1)}, bf16[1024,1024]{1,0:T(8,128)(2,1)}, u32[]{:S(2)}) copy-start(bf16[1024,1024]{1,0:T(8,128)(2,1)} %refs_3_.1) | copy-start | bytes 6291460
  36.5 33.6 %collective-permute-start = (bf16[256,1024]{1,0:T(8,128)(2,1)}, bf16[256,1024]{1,0:T(8,128)(2,1)S(1)}, u32[]{:S(2)}, u32[]{:S(2)}) collective-permute-start(bf16[256,1024]{1,0:T(8,128)(2,1)} %get-tuple-element.39.refs_0_), channel_id=1, source_target_pairs={{0,1},{1,0},{2,3},{3,2},{4,5},{5,4},{6,7},{7,6},{8,9},{9,8},{10,11... | collective-permute-start | bytes 1572872 | tf_op jit(solution)/shard_map/ppermute | solution.py:705
  51.6 13.8 %all-to-all-start.2 = ((bf16[16,16,128]{2,1,0:T(8,128)(2,1)}), bf16[16,16,128]{2,1,0:T(8,128)(2,1)S(1)}, u32[]{:S(2)}, u32[]{:S(2)}) async-start(bf16[16,16,128]{2,1,0:T(8,128)(2,1)} %shard_map.87), calls=%async_computation.2 | async-start | bytes 131072 | tf_op jit(solution)/shard_map/all_to_all | solution.py:679
  59.0 1.4 copy-start.1
  61.6 1.0 copy-start.2
  66.8 9.4 %all-to-all-start.3 = ((f32[8,8,128]{2,1,0:T(8,128)}), f32[8,8,128]{2,1,0:T(8,128)S(1)}, u32[]{:S(2)}, u32[]{:S(2)}) async-start(f32[8,8,128]{2,1,0:T(8,128)} %get-tuple-element.38), calls=%async_computation.3 | async-start | bytes 65536 | tf_op jit(solution)/shard_map/all_to_all | solution.py:679
  70.1 0.8 copy-start.5
  70.9 1.0 copy-start.4
  72.0 1.0 copy-start.6
  77.7 10.5 %all-to-all-start.4 = ((f32[8,8,128]{2,1,0:T(8,128)}), f32[8,8,128]{2,1,0:T(8,128)S(1)}, u32[]{:S(2)}, u32[]{:S(2)}) async-start(f32[8,8,128]{2,1,0:T(8,128)} %get-tuple-element.46), calls=%async_computation.4 | async-start | bytes 65536 | tf_op jit(solution)/shard_map/all_to_all | solution.py:679
  81.0 74.5 %all-gather.7.cloned.1.call-start = ((), (), s32[]{:S(2)}) async-start(), calls=%async_computation.8 | async-start | bytes 4718592 | tf_op jit(solution)/shard_map/all_gather | solution.py:741
  98.2 2.4 %collective-permute-start.1 = (bf16[256,1536]{1,0:T(8,128)(2,1)S(1)}, bf16[256,1536]{1,0:T(8,128)(2,1)S(1)}, u32[]{:S(2)}, u32[]{:S(2)}) collective-permute-start(bf16[256,1536]{1,0:T(8,128)(2,1)S(1)} %get-tuple-element.51), channel_id=1, source_target_pairs={{0,1},{1,0},{2,3},{3,2},{4,5},{5,4},{6,7},{7,6},{8,9},{9,8},{10,11... | collective-permute-start | bytes 2359304 | tf_op jit(solution)/shard_map/ppermute | solution.py:742
  98.3 2.3 %collective-permute-start.2 = (f32[8,128]{1,0:T(8,128)S(1)}, f32[8,128]{1,0:T(8,128)S(1)}, u32[]{:S(2)}, u32[]{:S(2)}) collective-permute-start(f32[8,128]{1,0:T(8,128)S(1)} %get-tuple-element.52.refs_3_), channel_id=1, source_target_pairs={{0,1},{1,0},{2,3},{3,2},{4,5},{5,4},{6,7},{7,6},{8,9},{9,8},{10,11... | collective-permute-start | bytes 12296 | tf_op jit(solution)/shard_map/ppermute | solution.py:742
  150.3 14.5 %all-to-all-start.6 = ((bf16[8,112,128]{2,1,0:T(8,128)(2,1)}), bf16[8,112,128]{2,1,0:T(8,128)(2,1)S(1)}, u32[]{:S(2)}, u32[]{:S(2)}) async-start(bf16[8,112,128]{2,1,0:T(8,128)(2,1)} %bitcast.8), calls=%async_computation.6 | async-start | bytes 458752 | tf_op jit(solution)/shard_map/all_to_all | solution.py:679
Sparse Core Ops, SparseCore 0:
  30.6 57.5 all-gather.4
  98.3 53.2 all-gather.6

commit v7 on v5

--- a/solution.py
+++ b/solution.py
@@ -363,9 +363,10 @@
     scale = (width // HEADS) ** -0.5
     for pair in range(HEADS // 2):
         at = pair * slab
-        if pair % 2 == 0:
-            for pair_load in pairs[pair] + pairs[pair + 1]:
-                pair_load.wait()
+        if pair % 4 == 0:
+            for group in pairs[pair : pair + 4]:
+                for pair_load in group:
+                    pair_load.wait()
         for part in range(PARTS):
             own = pl.ds(part * block_rows, block_rows)
             query = proj_ref[pair, 0, own]

time: 173 us -> 173 us (level)
  no operation moved by 1% of the time
where the time goes in v7:
time: 173 us; the launch traced here: 172 us
  blocking collectives  60.6 us (35%)
  Pallas kernels  39.7 us (23%)
  waiting for transfers between devices  29.5 us (17%)
  starting transfers between devices  25.3 us (15%)
  between operations  14.2 us (8%)
  local copies, waits for them, and re-layouts  1.86 us (1%)
    all_to_all x2, blocking collectives, to_each(): return lax.all_to_all(array, axis, split_axis=0, concat_axis=0, tiled=True)  60.6 us
    all_to_all x5, starting transfers between devices, to_each(): return lax.all_to_all(array, axis, split_axis=0, concat_axis=0, tiled=True)  24.4 us
    all_to_all x5, waiting for transfers between devices, to_each(): return lax.all_to_all(array, axis, split_axis=0, concat_axis=0, tiled=True)  20.8 us
    pallas_call x1, Pallas kernels, backward(): pl.pallas_call(lambda *refs: backward_kernel(block, count, *refs), in_spe...  9.76 us
    pallas_call x2, Pallas kernels, flip(): pl.pallas_call(flip_kernel, in_specs=[VMEM] * len(arrays), out_shape=jax....  9.7 us
    all_gather x1, waiting for transfers between devices, per_device(): gathered = lax.all_gather(out_grad[0], FRAME, axis=0, tiled=True)  6.91 us
    pallas_call x1, Pallas kernels, forward(): pl.pallas_call(lambda *refs: forward_kernel(patches, *refs), in_specs=[VM...  6.03 us
    pallas_call x1, Pallas kernels, attend(): pl.pallas_call(lambda *refs: attend_kernel(patches, *refs), in_specs=[VME...  3.61 us
  transfers between devices with their start and end apart: 10, of which 6 were waited for; matrix products, arithmetic and copies ran while one was open for 1% of the time, Pallas kernels for 16%

profile of v7, /device:TPU:8, one launch (start us, length us, event | category | flops | bytes accessed | tf_op | source)
XLA Modules:
  0.0 172.1 jit_solution(4172418037803988105)
XLA Ops:
  7.2 1.0 copy-done.2
  9.2 5.9 %all-to-all-start = ((bf16[8,2,16,1024]{3,2,1,0:T(8,128)(2,1)}), bf16[8,2,16,1024]{3,2,1,0:T(8,128)(2,1)S(1)}, u32[]{:S(2)}, u32[]{:S(2)}) async-start(bf16[8,2,16,1024]{3,2,1,0:T(8,128)(2,1)} %shard_map.84), calls=%async_computation | async-start | bytes 1048576 | tf_op jit(solution)/shard_map/all_to_all | solution.py:680
  15.1 7.2 %shard_map.85.refs_9_ = bf16[3072,1024]{1,0:T(8,128)(2,1)} custom-call(bf16[1024,3072]{1,0:T(8,128)(2,1)} %refs_2_.1), custom_call_target="tpu_custom_call" | custom-call | bytes 12582912 | tf_op jit(solution)/shard_map/pallas_call | solution.py:254
  22.3 8.1 %all-to-all-done.refs_0_ = bf16[8,2,16,1024]{3,2,1,0:T(8,128)(2,1)S(1)} async-done(((bf16[8,2,16,1024]{3,2,1,0:T(8,128)(2,1)}), bf16[8,2,16,1024]{3,2,1,0:T(8,128)(2,1)S(1)}, u32[]{:S(2)}, u32[]{:S(2)}) %all-to-all-start) | async-done | bytes 524320 | tf_op jit(solution)/shard_map/all_to_all | solution.py:680
  30.5 6.0 %shard_map.86 = (bf16[256,1024]{1,0:T(8,128)(2,1)}, bf16[256,1024]{1,0:T(8,128)(2,1)}, bf16[8,3,256,128]{3,2,1,0:T(8,128)(2,1)}, f32[16,8,128]{2,1,0:T(8,128)S(1)}) custom-call(bf16[8,2,16,1024]{3,2,1,0:T(8,128)(2,1)S(1)} %all-to-all-done.refs_0_, f32[1,1024]{1,0:T(1,128)S(1)} %bitcast.14, bf16[1024,3072]{1,0:T(8,128)(2,1)} %refs_2_.1), custom_call_target="tpu_custom_call" | custom-call | flops 2684354560 | bytes 10485760 | tf_op jit(solution)/shard_map/pallas_call | solution.py:217
  36.6 14.4 %all_to_all.35.refs_0_ = f32[16,8,128]{2,1,0:T(8,128)S(1)} all-to-all(f32[16,8,128]{2,1,0:T(8,128)S(1)} %get-tuple-element.33), channel_id=1, replica_groups=mesh['zh'=2,'x'=4,'y'=4,'zl'=4,'core'=2] {'zh','zl','core'}, dimensions={0} | all-to-all | bytes 131072 | tf_op jit(solution)/shard_map/all_to_all | solution.py:680
  51.6 7.5 %all-to-all-start.2 = ((bf16[16,16,128]{2,1,0:T(8,128)(2,1)}), bf16[16,16,128]{2,1,0:T(8,128)(2,1)S(1)}, u32[]{:S(2)}, u32[]{:S(2)}) async-start(bf16[16,16,128]{2,1,0:T(8,128)(2,1)} %shard_map.87), calls=%async_computation.2 | async-start | bytes 131072 | tf_op jit(solution)/shard_map/all_to_all | solution.py:680
  59.0 3.6 %shard_map.88 = (bf16[8,2,256,128]{3,2,1,0:T(8,128)(2,1)}, f32[32,128]{1,0:T(8,128)}) custom-call(bf16[8,3,256,128]{3,2,1,0:T(8,128)(2,1)} %get-tuple-element.34.refs_0_.refs_3_), custom_call_target="tpu_custom_call" | custom-call | flops 16777216 | bytes 6291456 | tf_op jit(solution)/shard_map/pallas_call | solution.py:287
  62.7 2.7 %all-to-all-done.2.refs_0_ = bf16[16,16,128]{2,1,0:T(8,128)(2,1)S(1)} async-done(((bf16[16,16,128]{2,1,0:T(8,128)(2,1)}), bf16[16,16,128]{2,1,0:T(8,128)(2,1)S(1)}, u32[]{:S(2)}, u32[]{:S(2)}) %all-to-all-start.2) | async-done | bytes 65568 | tf_op jit(solution)/shard_map/all_to_all | solution.py:680
  65.4 1.4 shard_map.89
  66.8 3.3 %all-to-all-start.3 = ((f32[8,8,128]{2,1,0:T(8,128)}), f32[8,8,128]{2,1,0:T(8,128)S(1)}, u32[]{:S(2)}, u32[]{:S(2)}) async-start(f32[8,8,128]{2,1,0:T(8,128)} %get-tuple-element.38), calls=%async_computation.3 | async-start | bytes 65536 | tf_op jit(solution)/shard_map/all_to_all | solution.py:680
  70.9 2.5 %shard_map.90.refs_0_ = bf16[1024,512]{1,0:T(8,128)(2,1)} custom-call(bf16[256,1024]{1,0:T(8,128)(2,1)} %get-tuple-element.39.refs_0_, bf16[256,1024]{1,0:T(8,128)(2,1)} %copy-done.5), custom_call_target="tpu_custom_call" | custom-call | bytes 2097152 | tf_op jit(solution)/shard_map/pallas_call | solution.py:254
  73.4 2.7 %all-to-all-done.3.refs_1_ = f32[8,8,128]{2,1,0:T(8,128)S(1)} async-done(((f32[8,8,128]{2,1,0:T(8,128)}), f32[8,8,128]{2,1,0:T(8,128)S(1)}, u32[]{:S(2)}, u32[]{:S(2)}) %all-to-all-start.3) | async-done | bytes 32800 | tf_op jit(solution)/shard_map/all_to_all | solution.py:680
  76.2 1.5 shard_map.91
  77.7 3.3 %all-to-all-start.4 = ((f32[8,8,128]{2,1,0:T(8,128)}), f32[8,8,128]{2,1,0:T(8,128)S(1)}, u32[]{:S(2)}, u32[]{:S(2)}) async-start(f32[8,8,128]{2,1,0:T(8,128)} %get-tuple-element.46), calls=%async_computation.4 | async-start | bytes 65536 | tf_op jit(solution)/shard_map/all_to_all | solution.py:680
  81.3 6.9 %all-gather.5.cloned.1.call-done = bf16[1,32,64,1024]{3,2,0,1:T(8,128)(2,1)} async-done(((bf16[1,4,64,1024]{3,2,0,1:T(8,128)(2,1)}), bf16[1,32,64,1024]{3,2,0,1:T(8,128)(2,1)}) %all-gather.5.cloned.1.call-update) | async-done | bytes 4194320 | tf_op jit(solution)/shard_map/all_gather | solution.py:702
  88.2 9.8 %shard_map.92 = (bf16[256,1536]{1,0:T(8,128)(2,1)S(1)}, bf16[256,1536]{1,0:T(8,128)(2,1)S(1)}, bf16[8,2,16,1024]{3,2,1,0:T(8,128)(2,1)}, f32[8,128]{1,0:T(8,128)S(1)}) custom-call(s32[1]{0:T(128)} %bitcast.2.refs_0_, s32[1]{0:T(128)} %bitcast.3.refs_1_.index_ref, bf16[256,1024]{1,0:T(8,128)(2,1)} %get-tuple-element.41.refs_2_, ...), custom_call_target="tpu_custom_call" | custom-call | flops 939524096 | bytes 12582912 | tf_op jit(solution)/shard_map/pallas_call | solution.py:444
  98.6 1.8 %collective-permute-done.2.refs_4_ = f32[8,128]{1,0:T(8,128)S(1)} collective-permute-done((f32[8,128]{1,0:T(8,128)S(1)}, f32[8,128]{1,0:T(8,128)S(1)}, u32[]{:S(2)}, u32[]{:S(2)}) %collective-permute-start.2) | collective-permute-done | bytes 4128 | tf_op jit(solution)/shard_map/ppermute | solution.py:743
  100.4 2.3 %shard_map.93 = bf16[16,784,128]{2,1,0:T(8,128)(2,1)S(1)} custom-call(bf16[1024,512]{1,0:T(8,128)(2,1)S(1)} %copy-done.1, bf16[256,1536]{1,0:T(8,128)(2,1)S(1)} %get-tuple-element.50.refs_1_, bf16[256,1536]{1,0:T(8,128)(2,1)S(1)} %collective-permute-done.1.refs_2_, f32[8,128]{1,0:T(8,128)S(1)} %get-tuple-element.52.refs_3_, ...), custom_call_target="tpu_custom_call" | custom-call | flops 1610612736 | bytes 6291456 | tf_op jit(solution)/shard_map/pallas_call | solution.py:518
  102.7 46.3 %all_to_all.36.refs_0_ = bf16[16,784,128]{2,1,0:T(8,128)(2,1)S(1)} all-to-all(bf16[16,784,128]{2,1,0:T(8,128)(2,1)S(1)} %shard_map.93), channel_id=1, replica_groups=mesh['zh'=2,'x'=4,'y'=4,'zl'=4,'core'=2] {'x','y'}, dimensions={0} | all-to-all | bytes 6422528 | tf_op jit(solution)/shard_map/all_to_all | solution.py:680
  149.0 1.1 shard_map.94
  150.1 4.3 %all-to-all-start.6 = ((bf16[8,112,128]{2,1,0:T(8,128)(2,1)}), bf16[8,112,128]{2,1,0:T(8,128)(2,1)S(1)}, u32[]{:S(2)}, u32[]{:S(2)}) async-start(bf16[8,112,128]{2,1,0:T(8,128)(2,1)} %bitcast.8), calls=%async_computation.6 | async-start | bytes 458752 | tf_op jit(solution)/shard_map/all_to_all | solution.py:680
  155.3 2.0 %shard_map.95 = bf16[4,8,8,1024]{3,2,1,0:T(8,128)(2,1)} custom-call(s32[1]{0:T(128)} %bitcast.3.refs_1_.index_ref, bf16[8,8,2,16,1024]{4,3,2,1,0:T(8,128)(2,1)} %bitcast.17), custom_call_target="tpu_custom_call" | custom-call | bytes 1048576 | tf_op jit(solution)/shard_map/pallas_call | solution.py:94
  157.4 7.3 %all-to-all-done.6.terms_ref = bf16[8,112,128]{2,1,0:T(8,128)(2,1)S(1)} async-done(((bf16[8,112,128]{2,1,0:T(8,128)(2,1)}), bf16[8,112,128]{2,1,0:T(8,128)(2,1)S(1)}, u32[]{:S(2)}, u32[]{:S(2)}) %all-to-all-start.6) | async-done | bytes 229408 | tf_op jit(solution)/shard_map/all_to_all | solution.py:680
  (26 shorter events, 5.0 us)
Async XLA Ops:
  7.2 1.0 copy-start.2
  9.2 21.3 %all-to-all-start = ((bf16[8,2,16,1024]{3,2,1,0:T(8,128)(2,1)}), bf16[8,2,16,1024]{3,2,1,0:T(8,128)(2,1)S(1)}, u32[]{:S(2)}, u32[]{:S(2)}) async-start(bf16[8,2,16,1024]{3,2,1,0:T(8,128)(2,1)} %shard_map.84), calls=%async_computation | async-start | bytes 1048576 | tf_op jit(solution)/shard_map/all_to_all | solution.py:680
  15.1 15.4 %copy-start.4 = (f32[1024]{0:T(1024)S(1)}, f32[1024]{0:T(1024)}, u32[]{:S(2)}) copy-start(f32[1024]{0:T(1024)} %param.7) | copy-start | bytes 12292
  15.1 73.1 %all-gather.5.cloned.1.call-start = ((), (), s32[]{:S(2)}) async-start(), calls=%async_computation.7 | async-start | bytes 4718592 | tf_op jit(solution)/shard_map/all_gather | solution.py:702
  30.5 34.9 %copy-start = (bf16[1024,1024]{1,0:T(8,128)(2,1)S(1)}, bf16[1024,1024]{1,0:T(8,128)(2,1)}, u32[]{:S(2)}) copy-start(bf16[1024,1024]{1,0:T(8,128)(2,1)} %refs_3_.1) | copy-start | bytes 6291460
  36.5 33.6 %collective-permute-start = (bf16[256,1024]{1,0:T(8,128)(2,1)}, bf16[256,1024]{1,0:T(8,128)(2,1)S(1)}, u32[]{:S(2)}, u32[]{:S(2)}) collective-permute-start(bf16[256,1024]{1,0:T(8,128)(2,1)} %get-tuple-element.39.refs_0_), channel_id=1, source_target_pairs={{0,1},{1,0},{2,3},{3,2},{4,5},{5,4},{6,7},{7,6},{8,9},{9,8},{10,11... | collective-permute-start | bytes 1572872 | tf_op jit(solution)/shard_map/ppermute | solution.py:706
  51.6 13.8 %all-to-all-start.2 = ((bf16[16,16,128]{2,1,0:T(8,128)(2,1)}), bf16[16,16,128]{2,1,0:T(8,128)(2,1)S(1)}, u32[]{:S(2)}, u32[]{:S(2)}) async-start(bf16[16,16,128]{2,1,0:T(8,128)(2,1)} %shard_map.87), calls=%async_computation.2 | async-start | bytes 131072 | tf_op jit(solution)/shard_map/all_to_all | solution.py:680
  62.7 25.5 %copy-start.3 = (f32[32,128]{1,0:T(8,128)S(1)}, f32[32,128]{1,0:T(8,128)}, u32[]{:S(2)}) copy-start(f32[32,128]{1,0:T(8,128)} %get-tuple-element.48.refs_7_) | copy-start | bytes 49156
  66.8 9.4 %all-to-all-start.3 = ((f32[8,8,128]{2,1,0:T(8,128)}), f32[8,8,128]{2,1,0:T(8,128)S(1)}, u32[]{:S(2)}, u32[]{:S(2)}) async-start(f32[8,8,128]{2,1,0:T(8,128)} %get-tuple-element.38), calls=%async_computation.3 | async-start | bytes 65536 | tf_op jit(solution)/shard_map/all_to_all | solution.py:680
  70.1 0.8 copy-start.5
  77.7 10.5 %all-to-all-start.4 = ((f32[8,8,128]{2,1,0:T(8,128)}), f32[8,8,128]{2,1,0:T(8,128)S(1)}, u32[]{:S(2)}, u32[]{:S(2)}) async-start(f32[8,8,128]{2,1,0:T(8,128)} %get-tuple-element.46), calls=%async_computation.4 | async-start | bytes 65536 | tf_op jit(solution)/shard_map/all_to_all | solution.py:680
  81.0 74.3 %all-gather.7.cloned.1.call-start = ((), (), s32[]{:S(2)}) async-start(), calls=%async_computation.8 | async-start | bytes 4718592 | tf_op jit(solution)/shard_map/all_gather | solution.py:742
  88.2 12.2 %copy-start.1 = (bf16[1024,512]{1,0:T(8,128)(2,1)S(1)}, bf16[1024,512]{1,0:T(8,128)(2,1)}, u32[]{:S(2)}) copy-start(bf16[1024,512]{1,0:T(8,128)(2,1)} %shard_map.90.refs_0_) | copy-start | bytes 3145732
  98.0 2.4 %collective-permute-start.1 = (bf16[256,1536]{1,0:T(8,128)(2,1)S(1)}, bf16[256,1536]{1,0:T(8,128)(2,1)S(1)}, u32[]{:S(2)}, u32[]{:S(2)}) collective-permute-start(bf16[256,1536]{1,0:T(8,128)(2,1)S(1)} %get-tuple-element.51), channel_id=1, source_target_pairs={{0,1},{1,0},{2,3},{3,2},{4,5},{5,4},{6,7},{7,6},{8,9},{9,8},{10,11... | collective-permute-start | bytes 2359304 | tf_op jit(solution)/shard_map/ppermute | solution.py:743
  98.1 2.3 %collective-permute-start.2 = (f32[8,128]{1,0:T(8,128)S(1)}, f32[8,128]{1,0:T(8,128)S(1)}, u32[]{:S(2)}, u32[]{:S(2)}) collective-permute-start(f32[8,128]{1,0:T(8,128)S(1)} %get-tuple-element.52.refs_3_), channel_id=1, source_target_pairs={{0,1},{1,0},{2,3},{3,2},{4,5},{5,4},{6,7},{7,6},{8,9},{9,8},{10,11... | collective-permute-start | bytes 12296 | tf_op jit(solution)/shard_map/ppermute | solution.py:743
  150.1 14.5 %all-to-all-start.6 = ((bf16[8,112,128]{2,1,0:T(8,128)(2,1)}), bf16[8,112,128]{2,1,0:T(8,128)(2,1)S(1)}, u32[]{:S(2)}, u32[]{:S(2)}) async-start(bf16[8,112,128]{2,1,0:T(8,128)(2,1)} %bitcast.8), calls=%async_computation.6 | async-start | bytes 458752 | tf_op jit(solution)/shard_map/all_to_all | solution.py:680
Sparse Core Ops, SparseCore 0:
  30.6 57.5 all-gather.4
  98.1 53.2 all-gather.6
